TPU v7x, 256 devices: a whole 4x4x8 slice. The times are simulated.
256 devices in a mesh: blk: 64 (over y, x_hi, z), dp: 4 (over x_lo, core).
Axes of the slice: x: 4 (x_hi: 2, x_lo: 2; x = x_hi * 2 + x_lo), y: 4, z: 8, core: 2. Of those that a mesh axis runs over, the one named last changes fastest.
Arguments:
- documents: bfloat16 [393216, 1024], P(('blk', 'dp')), may hold values from -30 to 30
- centroids: bfloat16 [1024, 1024], P('blk'), may hold values from -6 to 6
Outputs:
- new_centroids: float32 [1024, 1024], P('blk')
- normalizer: float32 [393216], P(('blk', 'dp'))
All inputs are finite; a program needn't handle non-finite values.
Results may differ from a plain program's by a relative error of at most 0.008.
Values may be sent and summed in bfloat16 or wider, within the bound.
No kernel may reach another device: no remote copies, remote signals or barrier semaphores. Data moves between devices by JAX's collectives and lax.ppermute only.
A program may use at most 64 MiB of HBM per device.

v0:
```python
import math

import jax
import jax.numpy as jnp
from jax import lax
from jax.sharding import PartitionSpec as P


def scores(piece, documents, beta):
    product = lax.dot_general(
        piece, documents, (((1,), (1,)), ((), ())), preferred_element_type=jnp.float32
    )
    widened = piece.astype(jnp.float32)
    norms = jnp.sum(widened * widened, axis=1, keepdims=True)
    return beta * product - 0.5 * beta * norms


def body(documents, centroids):
    beta = 3.0 / math.sqrt(documents.shape[1])
    count_docs = documents.shape[0]
    total_rows = centroids.shape[0] * lax.axis_size("blk")
    start_top = jnp.full((count_docs,), -1e30, jnp.float32)
    start_total = jnp.zeros((count_docs,), jnp.float32)
    initial = (start_top, start_total, jnp.zeros((total_rows, count_docs), jnp.float32))
    logits = scores(lax.all_gather(centroids, "blk", axis=0, tiled=True), documents, beta)
    new_top = jnp.maximum(initial[0], jnp.max(logits, axis=0))
    total = jnp.sum(jnp.exp(logits - new_top[None, :]), axis=0)
    normalizer = new_top + jnp.log(total)
    weights = jnp.exp(logits - normalizer[None, :])
    counts = jnp.sum(weights, axis=1)
    sums = jnp.dot(weights.astype(jnp.bfloat16), documents, preferred_element_type=jnp.float32)
    part_sums, part_counts = (
        lax.psum_scatter(sums, "blk", scatter_dimension=0, tiled=True),
        lax.psum_scatter(counts, "blk", scatter_dimension=0, tiled=True),
    )
    own_sums, own_counts = lax.psum((part_sums, part_counts), "dp")
    new_centroids = (own_sums + centroids.astype(jnp.float32)) / (own_counts[:, None] + 1.0)
    return (new_centroids, normalizer)


def solution(mesh):
    in_specs = (P(("blk", "dp"), None), P("blk", None))
    out_specs = (P("blk", None), P(("blk", "dp")))
    return jax.shard_map(body, mesh=mesh, in_specs=in_specs, out_specs=out_specs, check_vma=False)
```

profile of v0, /device:TPU:1, one launch (start us, length us, event | category | flops | bytes accessed | tf_op | source)
XLA Modules:
  0.0 560.7 jit_solution(10656709972670906758)
XLA Ops:
  7.2 0.0 copy-start
  7.2 0.0 all-gather.2.cloned.1.call-start
  7.2 0.7 all-gather.2.cloned.1.call-update
  7.9 0.0 reduce-scatter.2.cloned.1.call-start
  8.0 122.8 %all-gather.2.cloned.1.call-done = bf16[1024,1024]{1,0:T(8,128)(2,1)} async-done(((bf16[16,1024]{1,0:T(8,128)(2,1)}), bf16[1024,1024]{1,0:T(8,128)(2,1)}) %all-gather.2.cloned.1.call-update) | async-done | bytes 2097168 | tf_op jit(solution)/shard_map/all_gather | solution.py:25
  130.8 2.1 multiply_reduce_fusion
  132.9 0.0 copy-done
  132.9 5.1 fusion.5
  137.9 0.0 copy-start.1
  138.0 0.9 exponential_reduce_fusion
  138.9 1.7 copy-done.1
  140.6 0.0 copy-start.3
  140.6 0.0 copy-start.4
  140.6 5.0 fusion.2
  145.6 0.0 copy-start.2
  145.6 0.0 reduce-scatter.2.cloned.1.call-update
  145.6 0.0 all-reduce.3.cloned.1.call-start
  145.7 0.0 copy-done.4
  145.7 0.6 dynamic-slice
  146.9 0.0 copy-done.3
  146.9 3.7 fusion
  150.6 155.2 %all-reduce = f32[1024]{0:T(1024)S(1)} all-reduce(f32[1024]{0:T(1024)S(1)} %fusion), channel_id=3, replica_groups=mesh['blk'=64,'dp'=4] {'blk'}, use_global_device_ids=true, to_apply=%region_6.0.clone | all-reduce | flops 1024 | bytes 8192
  305.9 0.1 dynamic-slice.1
  305.9 34.2 %psum.15 = f32[16]{0:T(128)S(1)} all-reduce(f32[16]{0:T(128)S(1)} %dynamic-slice.1), channel_id=1, replica_groups=mesh['blk'=64,'dp'=4] {'dp'}, use_global_device_ids=true, to_apply=%region_7.0 | all-reduce | flops 16 | bytes 128 | tf_op jit(solution)/shard_map/psum | solution.py:36
  340.1 126.7 %reduce-scatter.2.cloned.1.call-done = f32[16,1024]{1,0:T(8,128)} async-done(((f32[1024,1024]{1,0:T(8,128)}), f32[16,1024]{1,0:T(8,128)}) %reduce-scatter.2.cloned.1.call-update) | async-done | bytes 65552 | tf_op jit(solution)/shard_map/reduce_scatter | solution.py:33
  466.8 0.0 all-reduce.3.cloned.1.call-update
  466.8 85.8 %all-reduce.3.cloned.1.call-done = f32[16,1024]{1,0:T(8,128)} async-done(((f32[16,1024]{1,0:T(8,128)}), f32[16,1024]{1,0:T(8,128)}) %all-reduce.3.cloned.1.call-update) | async-done | bytes 65552 | tf_op jit(solution)/shard_map/psum | solution.py:36
  552.6 0.0 copy-done.2
  552.6 1.5 add_divide_fusion
  (4 shorter events, 0.0 us)
Async XLA Ops:
  7.2 125.7 %copy-start = (bf16[1536,1024]{1,0:T(8,128)(2,1)S(1)}, bf16[1536,1024]{1,0:T(8,128)(2,1)}, u32[]{:S(2)}) copy-start(bf16[1536,1024]{1,0:T(8,128)(2,1)} %param.2) | copy-start | bytes 9437188
  7.2 123.6 %all-gather.2.cloned.1.call-start = ((), (), s32[]{:S(2)}) async-start(), calls=%async_computation.1 | async-start | bytes 2129920 | tf_op jit(solution)/shard_map/all_gather | solution.py:25
  7.9 458.9 %reduce-scatter.2.cloned.1.call-start = ((), (), s32[]{:S(2)}) async-start(), calls=%async_computation.2 | async-start | bytes 4259840 | tf_op jit(solution)/shard_map/reduce_scatter | solution.py:33
  137.9 2.7 copy-start.1
  140.6 6.3 %copy-start.3 = (f32[1536]{0:T(1024)}, f32[1536]{0:T(1024)S(1)}, u32[]{:S(2)}) copy-start(f32[1536]{0:T(1024)S(1)} %log_add_fusion) | copy-start | bytes 18436
  140.6 5.1 copy-start.4
  145.6 407.0 %copy-start.2 = (bf16[16,1024]{1,0:T(8,128)(2,1)S(1)}, bf16[16,1024]{1,0:T(8,128)(2,1)}, u32[]{:S(2)}) copy-start(bf16[16,1024]{1,0:T(8,128)(2,1)} %param.3) | copy-start | bytes 98308
  145.6 407.0 %all-reduce.3.cloned.1.call-start = ((), (), s32[]{:S(2)}) async-start(), calls=%async_computation.3 | async-start | bytes 131072 | tf_op jit(solution)/shard_map/psum | solution.py:36
Sparse Core Ops, SparseCore 0:
  11.6 119.1 all-gather.1
  145.7 320.9 reduce-scatter.1
  469.6 82.9 all-reduce.2
where the time goes:
time: 561 us
  waiting for transfers between devices  336 us (60%)
  blocking collectives  189 us (34%)
  between operations  14.5 us (3%)
  matrix products  10 us (2%)
  other arithmetic  8.22 us (1%)
    unnamed x1, blocking collectives  155 us
    reduce_scatter x1, waiting for transfers between devices, body(): lax.psum_scatter(sums, 'blk', scatter_dimension=0, tiled=True)  127 us
    all_gather x1, waiting for transfers between devices, body(): lax.all_gather(centroids, 'blk', axis=0, tiled=True)  123 us
    psum x1, waiting for transfers between devices, body(): own_sums, own_counts = lax.psum((part_sums, part_counts), 'dp')  85.8 us
    psum x1, blocking collectives, body(): own_sums, own_counts = lax.psum((part_sums, part_counts), 'dp')  34.2 us
  transfers between devices with their start and end apart: 3, of which 3 were waited for; matrix products, arithmetic and copies ran while one was open for 1% of the time, Pallas kernels for 0%

commit v1 on v0

v1 whole, which is shorter than its diff:
```python
import math

import jax
import jax.numpy as jnp
from jax import lax
from jax.sharding import Mesh, PartitionSpec as P

AXES = ("y", "xh", "z", "xl", "core")
SWAP = [(0, 1), (1, 0)]
OFFSETS = ((0, 1, -1, 2), (-2, 3, -3, 4))


def toward(j, sign):
    pairs = []
    for z in range(8):
        for core in range(2):
            far = ((z + OFFSETS[core][j]) % 8) * 2 + core
            near = z * 2 + core
            pairs.append((far, near) if sign > 0 else (near, far))
    return pairs


def scores(piece, norms, documents, beta):
    product = lax.dot_general(
        piece, documents, (((1,), (1,)), ((), ())), preferred_element_type=jnp.float32
    )
    return beta * product - 0.5 * beta * norms


def body(documents, centroids):
    beta = 3.0 / math.sqrt(documents.shape[1])
    width = documents.shape[1]
    others = lax.ppermute(documents, "core", SWAP)

    near = jnp.stack([lax.ppermute(centroids, ("z", "core"), toward(j, 1)) for j in range(4)])
    near = near.reshape(4, 2, 8, width).swapaxes(0, 1).reshape(1, 64, width)
    held = lax.all_to_all(
        jnp.broadcast_to(near, (8, 64, width)), ("y", "xh"), 0, 0, tiled=True
    ).reshape(512, width)

    widened = held.astype(jnp.float32)
    norms = jnp.sum(widened * widened, axis=1, keepdims=True)
    logits = (scores(held, norms, documents, beta), scores(held, norms, others, beta))
    tops = [jnp.max(part, axis=0) for part in logits]
    totals = [jnp.sum(jnp.exp(part - top[None, :]), axis=0) for part, top in zip(logits, tops)]
    mine = jnp.stack(tops + totals)
    theirs = lax.ppermute(mine, "core", SWAP)
    weights, normalizers = [], []
    for i in range(2):
        top = jnp.maximum(mine[i], theirs[1 - i])
        total = mine[2 + i] * jnp.exp(mine[i] - top) + theirs[3 - i] * jnp.exp(theirs[1 - i] - top)
        normalizers.append(top + jnp.log(total))
        weights.append(jnp.exp(logits[i] - normalizers[i][None, :]))
    counts = jnp.sum(weights[0], axis=1) + jnp.sum(weights[1], axis=1)
    sums = jnp.dot(weights[0].astype(jnp.bfloat16), documents, preferred_element_type=jnp.float32)
    sums += jnp.dot(weights[1].astype(jnp.bfloat16), others, preferred_element_type=jnp.float32)

    high = counts.astype(jnp.bfloat16)
    low = (counts - high.astype(jnp.float32)).astype(jnp.bfloat16)
    tail = jnp.pad(jnp.stack([high, low], axis=1), ((0, 0), (0, 126)))
    packed = jnp.concatenate([sums.astype(jnp.bfloat16), tail], axis=1).reshape(16, 32, -1)
    packed = lax.all_to_all(packed, ("y", "xh", "xl"), 0, 0, tiled=True)
    part = jnp.sum(packed.astype(jnp.float32), axis=0).reshape(4, 8, -1)
    part = sum(lax.ppermute(part[j], ("z", "core"), toward(j, -1)) for j in range(4))
    part = part + lax.ppermute(part, "core", SWAP)
    side = lax.axis_index("xl")
    own = lax.dynamic_slice_in_dim(centroids, side * 8, 8, 0).astype(jnp.float32)
    new = (part[:, :width] + own) / (part[:, width : width + 1] + part[:, width + 1 : width + 2] + 1.0)
    other = lax.ppermute(new, "xl", SWAP)
    first = side == 0
    new_centroids = jnp.concatenate([jnp.where(first, new, other), jnp.where(first, other, new)])
    return (new_centroids, normalizers[0])


def solution(mesh):
    fine = Mesh(mesh.devices.reshape(4, 2, 8, 2, 2), AXES)
    in_specs = (P(AXES, None), P(("y", "xh", "z"), None))
    out_specs = (P(("y", "xh", "z"), None), P(AXES))
    return jax.shard_map(body, mesh=fine, in_specs=in_specs, out_specs=out_specs, check_vma=False)
```

time: 561 us -> 101 us (0.18)
  waiting for transfers between devices: 336 us -> 13.2 us
  blocking collectives: 189 us -> 41.8 us
  starting transfers between devices: 0.12 us -> 27 us
  between operations: 14.5 us -> 0.85 us
    unnamed x1 -> x0, blocking collectives: 155 us -> none
    reduce_scatter x1 -> x0, waiting for transfers between devices: 127 us -> none  [body(): lax.psum_scatter(sums, 'blk', scatter_dimension=0, tiled=True)]
    all_gather x1 -> x0, waiting for transfers between devices: 123 us -> none  [body(): lax.all_gather(centroids, 'blk', axis=0, tiled=True)]
    psum x1 -> x0, waiting for transfers between devices: 85.8 us -> none  [body(): own_sums, own_counts = lax.psum((part_sums, part_counts), 'dp')]
    all_to_all x0 -> x2, blocking collectives: none -> 41.8 us  [the longest x1 21.1 us: body(): packed = lax.all_to_all(packed, ('y', 'xh', 'xl'), 0, 0, tiled=True)]
    psum x1 -> x0, blocking collectives: 34.2 us -> none  [body(): own_sums, own_counts = lax.psum((part_sums, part_counts), 'dp')]
    ppermute x0 -> x12, starting transfers between devices: none -> 27 us  [the longest x4 11.6 us: body(): lax.ppermute(centroids, ('z', 'core'), toward(j, 1))]
    ppermute x0 -> x12, waiting for transfers between devices: none -> 13.2 us  [the longest x4 5.72 us: body(): lax.ppermute(part[j], ('z', 'core'), toward(j, -1))]
  transfers between devices with their start and end apart: 3 -> 12, of which waited for: 3 -> 7; matrix products, arithmetic and copies ran while one was open for 1% -> 5% of each run, Pallas kernels for 0% -> 0%
where the time goes in v1:
time: 101 us; the launch traced here: 100 us
  blocking collectives  41.8 us (41%)
  starting transfers between devices  27 us (27%)
  waiting for transfers between devices  13.2 us (13%)
  matrix products  13.1 us (13%)
  other arithmetic  4.12 us (4%)
    all_to_all x1, blocking collectives, body(): packed = lax.all_to_all(packed, ('y', 'xh', 'xl'), 0, 0, tiled=True)  21.1 us
    all_to_all x1, blocking collectives, body(): lax.all_to_all(jnp.broadcast_to(near, (8, 64, width)), ('y', 'xh'), 0, 0,...  20.7 us
    ppermute x4, starting transfers between devices, body(): lax.ppermute(centroids, ('z', 'core'), toward(j, 1))  11.6 us
    ppermute x4, starting transfers between devices, body(): lax.ppermute(part[j], ('z', 'core'), toward(j, -1))  11.3 us
    dot_general x2, matrix products, scores(): lax.dot_general(piece, documents, (((1,), (1,)), ((), ())), preferred_ele...  7.46 us
    ppermute x4, waiting for transfers between devices, body(): lax.ppermute(part[j], ('z', 'core'), toward(j, -1))  5.72 us
    dot_general x1, matrix products, body(): jnp.dot(weights[1].astype(jnp.bfloat16), others, preferred_element_type=j...  3.83 us
    ppermute x1, starting transfers between devices, body(): others = lax.ppermute(documents, 'core', SWAP)  3.33 us
  transfers between devices with their start and end apart: 12, of which 7 were waited for; matrix products, arithmetic and copies ran while one was open for 5% of the time, Pallas kernels for 0%

profile of v1, /device:TPU:1, one launch (start us, length us, event | category | flops | bytes accessed | tf_op | source)
XLA Modules:
  0.0 100.4 jit_solution(2773247231569146982)
XLA Ops:
  0.6 3.3 %collective-permute-start.4 = (bf16[1536,1024]{1,0:T(8,128)(2,1)}, bf16[1536,1024]{1,0:T(8,128)(2,1)}, u32[]{:S(2)}, u32[]{:S(2)}) collective-permute-start(bf16[1536,1024]{1,0:T(8,128)(2,1)} %param.2), channel_id=1, source_target_pairs={{0,1},{1,0},{2,3},{3,2},{4,5},{5,4},{6,7},{7,6},{8,9},{9,8},{10,11... | collective-permute-start | bytes 9437192 | tf_op jit(solution)/shard_map/ppermute | solution.py:33
  4.0 3.2 %collective-permute-start = (bf16[16,1024]{1,0:T(8,128)(2,1)}, bf16[16,1024]{1,0:T(8,128)(2,1)S(1)}, u32[]{:S(2)}, u32[]{:S(2)}) collective-permute-start(bf16[16,1024]{1,0:T(8,128)(2,1)} %param.3), channel_id=1, source_target_pairs={{0,0},{25,1},{4,4},{29,5},{8,8},{1,9},{12,12},{5,13},{16,16},{9,17... | collective-permute-start | bytes 98312 | tf_op jit(solution)/shard_map/ppermute | solution.py:35
  7.1 4.7 %collective-permute-start.1 = (bf16[16,1024]{1,0:T(8,128)(2,1)}, bf16[16,1024]{1,0:T(8,128)(2,1)S(1)}, u32[]{:S(2)}, u32[]{:S(2)}) collective-permute-start(bf16[16,1024]{1,0:T(8,128)(2,1)} %param.3), channel_id=1, source_target_pairs={{4,0},{13,1},{8,4},{17,5},{12,8},{21,9},{16,12},{25,13},{20,16},{2... | collective-permute-start | bytes 98312 | tf_op jit(solution)/shard_map/ppermute | solution.py:35
  11.9 3.6 %collective-permute-start.3 = (bf16[16,1024]{1,0:T(8,128)(2,1)}, bf16[16,1024]{1,0:T(8,128)(2,1)S(1)}, u32[]{:S(2)}, u32[]{:S(2)}) collective-permute-start(bf16[16,1024]{1,0:T(8,128)(2,1)} %param.3), channel_id=1, source_target_pairs={{8,0},{17,1},{12,4},{21,5},{16,8},{25,9},{20,12},{29,13},{24,16},{... | collective-permute-start | bytes 98312 | tf_op jit(solution)/shard_map/ppermute | solution.py:35
  15.6 2.3 %collective-permute-done.2 = bf16[16,1024]{1,0:T(8,128)(2,1)S(1)} collective-permute-done((bf16[16,1024]{1,0:T(8,128)(2,1)}, bf16[16,1024]{1,0:T(8,128)(2,1)S(1)}, u32[]{:S(2)}, u32[]{:S(2)}) %collective-permute-start.2) | collective-permute-done | bytes 32800 | tf_op jit(solution)/shard_map/ppermute | solution.py:35
  17.8 1.0 collective-permute-done.3
  18.9 0.1 broadcast_in_dim.5
  19.0 20.7 %all_to_all.10 = bf16[8,64,1024]{2,1,0:T(8,128)(2,1)S(1)} all-to-all(bf16[8,64,1024]{2,1,0:T(8,128)(2,1)S(1)} %broadcast_in_dim.5), channel_id=1, replica_groups=mesh['y'=4,'xh'=2,'z'=8,'xl'=2,'core'=2] {'y','xh'}, dimensions={0} | all-to-all | bytes 2097152 | tf_op jit(solution)/shard_map/all_to_all | solution.py:37
  39.7 0.3 multiply_reduce_fusion
  40.0 3.7 %fusion.28 = (f32[1536]{0:T(1024)S(1)}, f32[512,1536]{1,0:T(8,128)S(1)}) fusion(f32[512]{0:T(512)S(1)} %mul.48, bf16[512,1024]{1,0:T(8,128)(2,1)S(1)} %bitcast.17, bf16[1536,1024]{1,0:T(8,128)(2,1)} %param.2), kind=kOutput, calls=%fused_computation.54 | convolution fusion | flops 1612970496 | bytes 7348224 | tf_op jit(solution)/shard_map/dot_general | solution.py:24
  43.8 0.5 exponential_reduce_fusion.1
  44.3 3.7 %fusion.27 = (f32[1536]{0:T(1024)S(1)}, f32[512,1536]{1,0:T(8,128)S(1)}) fusion(f32[512]{0:T(512)S(1)} %mul.48, bf16[512,1024]{1,0:T(8,128)(2,1)S(1)} %bitcast.18, bf16[1536,1024]{1,0:T(8,128)(2,1)} %collective-permute-done.4), kind=kOutput, calls=%fused_computation.53 | convolution fusion | flops 1612970496 | bytes 7348224 | tf_op jit(solution)/shard_map/dot_general | solution.py:24
  48.0 0.5 exponential_reduce_fusion
  48.5 0.3 collective-permute-start.5
  48.8 1.2 %collective-permute-done.5 = f32[4,1536]{1,0:T(4,128)S(1)} collective-permute-done((f32[4,1536]{1,0:T(4,128)S(1)}, f32[4,1536]{1,0:T(4,128)S(1)}, u32[]{:S(2)}, u32[]{:S(2)}) %collective-permute-start.5) | collective-permute-done | bytes 24608 | tf_op jit(solution)/shard_map/ppermute | solution.py:47
  50.1 0.9 fusion.2
  51.0 3.8 %fusion.7 = f32[512,1024]{1,0:T(8,128)S(1)} fusion(bf16[1536,1024]{1,0:T(8,128)(2,1)} %collective-permute-done.4, f32[512,1536]{1,0:T(8,128)S(1)} %get-tuple-element.13, f32[1536]{0:T(1024)S(1)} %get-tuple-element.4), kind=kOutput, calls=%fused_computation.17 | convolution fusion | flops 1612185600 | bytes 8394752 | tf_op jit(solution)/shard_map/dot_general | solution.py:56
  54.9 1.8 %add_convert_fusion = bf16[512,1024]{1,0:T(8,128)(2,1)S(1)} fusion(f32[512,1024]{1,0:T(8,128)S(1)} %fusion.7, bf16[1536,1024]{1,0:T(8,128)(2,1)S(1)} %copy-done.1, f32[512,1536]{1,0:T(8,128)S(1)} %get-tuple-element.15, f32[1536]{0:T(1024)S(1)} %get-tuple-element.5), kind=kOutput, calls=%fused_computation.15 | convolution fusion | flops 1613234176 | bytes 9443328 | tf_op jit(solution)/shard_map/dot_general | solution.py:55
  56.7 0.2 copy.7
  57.0 21.1 %all_to_all.11 = bf16[16,32,1152]{2,1,0:T(8,128)(2,1)S(1)} all-to-all(bf16[16,32,1152]{2,1,0:T(8,128)(2,1)S(1)} %bitcast.16), channel_id=1, replica_groups=mesh['y'=4,'xh'=2,'z'=8,'xl'=2,'core'=2] {'y','xh','xl'}, dimensions={0} | all-to-all | bytes 2359296 | tf_op jit(solution)/shard_map/all_to_all | solution.py:62
  78.1 0.2 convert_reduce_fusion
  78.3 5.4 %collective-permute-start.6 = (f32[8,1152]{1,0:T(8,128)S(1)}, f32[8,1152]{1,0:T(8,128)S(1)}, u32[]{:S(2)}, u32[]{:S(2)}) collective-permute-start(f32[8,1152]{1,0:T(8,128)S(1)} %get-tuple-element.9), channel_id=1, source_target_pairs={{0,0},{1,25},{4,4},{5,29},{8,8},{9,1},{12,12},{13,5},{16,16},{17,9... | collective-permute-start | bytes 110600 | tf_op jit(solution)/shard_map/ppermute | solution.py:64
  83.8 4.5 %collective-permute-start.8 = (f32[8,1152]{1,0:T(8,128)S(1)}, f32[8,1152]{1,0:T(8,128)S(1)}, u32[]{:S(2)}, u32[]{:S(2)}) collective-permute-start(f32[8,1152]{1,0:T(8,128)S(1)} %get-tuple-element.8), channel_id=1, source_target_pairs={{0,28},{1,21},{4,0},{5,25},{8,4},{9,29},{12,8},{13,1},{16,12},{17,... | collective-permute-start | bytes 110600 | tf_op jit(solution)/shard_map/ppermute | solution.py:64
  88.3 1.4 %collective-permute-start.9 = (f32[8,1152]{1,0:T(8,128)S(1)}, f32[8,1152]{1,0:T(8,128)S(1)}, u32[]{:S(2)}, u32[]{:S(2)}) collective-permute-start(f32[8,1152]{1,0:T(8,128)S(1)} %get-tuple-element.7), channel_id=1, source_target_pairs={{0,8},{1,17},{4,12},{5,21},{8,16},{9,25},{12,20},{13,29},{16,24},{... | collective-permute-start | bytes 110600 | tf_op jit(solution)/shard_map/ppermute | solution.py:64
  89.7 1.0 %collective-permute-done.7 = f32[8,1152]{1,0:T(8,128)S(1)} collective-permute-done((f32[8,1152]{1,0:T(8,128)S(1)}, f32[8,1152]{1,0:T(8,128)S(1)}, u32[]{:S(2)}, u32[]{:S(2)}) %collective-permute-start.7) | collective-permute-done | bytes 36896 | tf_op jit(solution)/shard_map/ppermute | solution.py:64
  90.7 4.7 %collective-permute-done.9 = f32[8,1152]{1,0:T(8,128)S(1)} collective-permute-done((f32[8,1152]{1,0:T(8,128)S(1)}, f32[8,1152]{1,0:T(8,128)S(1)}, u32[]{:S(2)}, u32[]{:S(2)}) %collective-permute-start.9) | collective-permute-done | bytes 36896 | tf_op jit(solution)/shard_map/ppermute | solution.py:64
  95.5 1.2 %collective-permute-done.10 = f32[8,1152]{1,0:T(8,128)S(1)} collective-permute-done((f32[8,1152]{1,0:T(8,128)S(1)}, f32[8,1152]{1,0:T(8,128)S(1)}, u32[]{:S(2)}, u32[]{:S(2)}) %collective-permute-start.10) | collective-permute-done | bytes 36896 | tf_op jit(solution)/shard_map/ppermute | solution.py:65
  96.7 0.2 fusion.25
  97.0 0.3 collective-permute-start.11
  97.3 0.6 log_add_fusion
  97.9 1.8 %collective-permute-done.11 = f32[8,1024]{1,0:T(8,128)S(1)} collective-permute-done((f32[8,1024]{1,0:T(8,128)S(1)}, f32[8,1024]{1,0:T(8,128)S(1)}, u32[]{:S(2)}, u32[]{:S(2)}) %collective-permute-start.11) | collective-permute-done | bytes 32800 | tf_op jit(solution)/shard_map/ppermute | solution.py:69
  99.8 0.6 pad_maximum_fusion.1
  (31 shorter events, 0.8 us)
Async XLA Ops:
  0.6 43.6 %collective-permute-start.4 = (bf16[1536,1024]{1,0:T(8,128)(2,1)}, bf16[1536,1024]{1,0:T(8,128)(2,1)}, u32[]{:S(2)}, u32[]{:S(2)}) collective-permute-start(bf16[1536,1024]{1,0:T(8,128)(2,1)} %param.2), channel_id=1, source_target_pairs={{0,1},{1,0},{2,3},{3,2},{4,5},{5,4},{6,7},{7,6},{8,9},{9,8},{10,11... | collective-permute-start | bytes 9437192 | tf_op jit(solution)/shard_map/ppermute | solution.py:33
  4.0 11.6 %collective-permute-start = (bf16[16,1024]{1,0:T(8,128)(2,1)}, bf16[16,1024]{1,0:T(8,128)(2,1)S(1)}, u32[]{:S(2)}, u32[]{:S(2)}) collective-permute-start(bf16[16,1024]{1,0:T(8,128)(2,1)} %param.3), channel_id=1, source_target_pairs={{0,0},{25,1},{4,4},{29,5},{8,8},{1,9},{12,12},{5,13},{16,16},{9,17... | collective-permute-start | bytes 98312 | tf_op jit(solution)/shard_map/ppermute | solution.py:35
  7.1 8.5 %collective-permute-start.1 = (bf16[16,1024]{1,0:T(8,128)(2,1)}, bf16[16,1024]{1,0:T(8,128)(2,1)S(1)}, u32[]{:S(2)}, u32[]{:S(2)}) collective-permute-start(bf16[16,1024]{1,0:T(8,128)(2,1)} %param.3), channel_id=1, source_target_pairs={{4,0},{13,1},{8,4},{17,5},{12,8},{21,9},{16,12},{25,13},{20,16},{2... | collective-permute-start | bytes 98312 | tf_op jit(solution)/shard_map/ppermute | solution.py:35
  11.9 6.0 %collective-permute-start.2 = (bf16[16,1024]{1,0:T(8,128)(2,1)}, bf16[16,1024]{1,0:T(8,128)(2,1)S(1)}, u32[]{:S(2)}, u32[]{:S(2)}) collective-permute-start(bf16[16,1024]{1,0:T(8,128)(2,1)} %param.3), channel_id=1, source_target_pairs={{28,0},{21,1},{0,4},{25,5},{4,8},{29,9},{8,12},{1,13},{12,16},{5,1... | collective-permute-start | bytes 98312 | tf_op jit(solution)/shard_map/ppermute | solution.py:35
  11.9 6.9 %collective-permute-start.3 = (bf16[16,1024]{1,0:T(8,128)(2,1)}, bf16[16,1024]{1,0:T(8,128)(2,1)S(1)}, u32[]{:S(2)}, u32[]{:S(2)}) collective-permute-start(bf16[16,1024]{1,0:T(8,128)(2,1)} %param.3), channel_id=1, source_target_pairs={{8,0},{17,1},{12,4},{21,5},{16,8},{25,9},{20,12},{29,13},{24,16},{... | collective-permute-start | bytes 98312 | tf_op jit(solution)/shard_map/ppermute | solution.py:35
  48.5 1.5 %collective-permute-start.5 = (f32[4,1536]{1,0:T(4,128)S(1)}, f32[4,1536]{1,0:T(4,128)S(1)}, u32[]{:S(2)}, u32[]{:S(2)}) collective-permute-start(f32[4,1536]{1,0:T(4,128)S(1)} %pad_maximum_fusion.2), channel_id=1, source_target_pairs={{0,1},{1,0},{2,3},{3,2},{4,5},{5,4},{6,7},{7,6},{8,9},{9,8},{10,11... | collective-permute-start | bytes 73736 | tf_op jit(solution)/shard_map/ppermute | solution.py:47
  51.0 3.9 %copy-start.1 = (bf16[1536,1024]{1,0:T(8,128)(2,1)S(1)}, bf16[1536,1024]{1,0:T(8,128)(2,1)}, u32[]{:S(2)}) copy-start(bf16[1536,1024]{1,0:T(8,128)(2,1)} %param.2) | copy-start | bytes 9437188
  56.9 40.0 %copy-start = (bf16[16,1024]{1,0:T(8,128)(2,1)S(1)}, bf16[16,1024]{1,0:T(8,128)(2,1)}, u32[]{:S(2)}) copy-start(bf16[16,1024]{1,0:T(8,128)(2,1)} %param.3) | copy-start | bytes 98308
  78.3 11.3 %collective-permute-start.6 = (f32[8,1152]{1,0:T(8,128)S(1)}, f32[8,1152]{1,0:T(8,128)S(1)}, u32[]{:S(2)}, u32[]{:S(2)}) collective-permute-start(f32[8,1152]{1,0:T(8,128)S(1)} %get-tuple-element.9), channel_id=1, source_target_pairs={{0,0},{1,25},{4,4},{5,29},{8,8},{9,1},{12,12},{13,5},{16,16},{17,9... | collective-permute-start | bytes 110600 | tf_op jit(solution)/shard_map/ppermute | solution.py:64
  83.7 7.0 %collective-permute-start.7 = (f32[8,1152]{1,0:T(8,128)S(1)}, f32[8,1152]{1,0:T(8,128)S(1)}, u32[]{:S(2)}, u32[]{:S(2)}) collective-permute-start(f32[8,1152]{1,0:T(8,128)S(1)} %get-tuple-element.6), channel_id=1, source_target_pairs={{0,4},{1,13},{4,8},{5,17},{8,12},{9,21},{12,16},{13,25},{16,20},{1... | collective-permute-start | bytes 110600 | tf_op jit(solution)/shard_map/ppermute | solution.py:64
  83.8 6.9 %collective-permute-start.8 = (f32[8,1152]{1,0:T(8,128)S(1)}, f32[8,1152]{1,0:T(8,128)S(1)}, u32[]{:S(2)}, u32[]{:S(2)}) collective-permute-start(f32[8,1152]{1,0:T(8,128)S(1)} %get-tuple-element.8), channel_id=1, source_target_pairs={{0,28},{1,21},{4,0},{5,25},{8,4},{9,29},{12,8},{13,1},{16,12},{17,... | collective-permute-start | bytes 110600 | tf_op jit(solution)/shard_map/ppermute | solution.py:64
  88.3 7.1 %collective-permute-start.9 = (f32[8,1152]{1,0:T(8,128)S(1)}, f32[8,1152]{1,0:T(8,128)S(1)}, u32[]{:S(2)}, u32[]{:S(2)}) collective-permute-start(f32[8,1152]{1,0:T(8,128)S(1)} %get-tuple-element.7), channel_id=1, source_target_pairs={{0,8},{1,17},{4,12},{5,21},{8,16},{9,25},{12,20},{13,29},{16,24},{... | collective-permute-start | bytes 110600 | tf_op jit(solution)/shard_map/ppermute | solution.py:64
  95.4 1.3 %collective-permute-start.10 = (f32[8,1152]{1,0:T(8,128)S(1)}, f32[8,1152]{1,0:T(8,128)S(1)}, u32[]{:S(2)}, u32[]{:S(2)}) collective-permute-start(f32[8,1152]{1,0:T(8,128)S(1)} %add_add_fusion), channel_id=1, source_target_pairs={{0,1},{1,0},{2,3},{3,2},{4,5},{5,4},{6,7},{7,6},{8,9},{9,8},{10,11... | collective-permute-start | bytes 110600 | tf_op jit(solution)/shard_map/ppermute | solution.py:65
  97.0 2.8 %collective-permute-start.11 = (f32[8,1024]{1,0:T(8,128)S(1)}, f32[8,1024]{1,0:T(8,128)S(1)}, u32[]{:S(2)}, u32[]{:S(2)}) collective-permute-start(f32[8,1024]{1,0:T(8,128)S(1)} %fusion.16), channel_id=1, source_target_pairs={{0,2},{2,0},{1,3},{3,1},{4,6},{6,4},{5,7},{7,5},{8,10},{10,8},{9,1... | collective-permute-start | bytes 98312 | tf_op jit(solution)/shard_map/ppermute | solution.py:69

commit v2 on v1

v2 whole, which is shorter than its diff:
```python
import functools
import math

import jax
import jax.numpy as jnp
from jax import lax
from jax.experimental import pallas as pl
from jax.experimental.pallas import tpu as pltpu
from jax.sharding import Mesh, PartitionSpec as P

AXES = ("y", "xh", "z", "xl", "core")
SIZES = (4, 2, 8, 2, 2)
SWAP = [(0, 1), (1, 0)]
OFFSETS = ((0, 1, -1, 2), (-2, 3, -3, 4))
PEERS = 16
TILE = 512
MIB = 2**20


def toward(j, sign):
    pairs = []
    for z in range(8):
        for core in range(2):
            far = ((z + OFFSETS[core][j]) % 8) * 2 + core
            near = z * 2 + core
            pairs.append((far, near) if sign > 0 else (near, far))
    return pairs


def logits_kernel(beta, held, docs, others, logits, stats):
    count = docs.shape[0]
    block = held[...]
    wide = block.astype(jnp.float32)
    shift = (0.5 * beta) * jnp.sum(wide * wide, axis=1, keepdims=True)
    for side, source in enumerate((docs, others)):
        for start in range(0, count, TILE):
            part = lax.dot_general(
                block,
                source[start : start + TILE, :],
                (((1,), (1,)), ((), ())),
                preferred_element_type=jnp.float32,
            )
            part = beta * part - shift
            logits[:, side * count + start : side * count + start + TILE] = part
            top = jnp.max(part, axis=0, keepdims=True)
            stats[side : side + 1, start : start + TILE] = top
            stats[2 + side : 3 + side, start : start + TILE] = jnp.sum(
                jnp.exp(part - top), axis=0, keepdims=True
            )


def sums_kernel(logits, mine, theirs, docs, others, normalizer, packed, low):
    count = docs.shape[0]
    rows = logits.shape[0]
    per = rows // PEERS
    counts = jnp.zeros((rows, 128), jnp.float32)
    for side in range(2):
        a, b = mine[side : side + 1, :], theirs[1 - side : 2 - side, :]
        top = jnp.maximum(a, b)
        total = mine[2 + side : 3 + side, :] * jnp.exp(a - top)
        total += theirs[3 - side : 4 - side, :] * jnp.exp(b - top)
        norm = top + jnp.log(total)
        if side == 0:
            normalizer[...] = norm
        for start in range(0, count, TILE):
            at = side * count + start
            weights = jnp.exp(logits[:, at : at + TILE] - norm[:, start : start + TILE])
            for k in range(0, TILE, 128):
                counts += weights[:, k : k + 128]
            low[:, at : at + TILE] = weights.astype(jnp.bfloat16)
    flat = jnp.sum(counts.T, axis=0, keepdims=True)
    high = flat.astype(jnp.bfloat16)
    rest = (flat - high.astype(jnp.float32)).astype(jnp.bfloat16)
    slab = [part[:, k : k + 128] for part in (high, rest) for k in range(0, rows, 128)]
    slab = jnp.concatenate(slab + [jnp.zeros((16 - len(slab), 128), jnp.bfloat16)], axis=0)
    for peer in range(PEERS):
        packed[peer, per * 8 : per * 8 + 16, :] = slab
    for start in range(0, docs.shape[1], 256):
        columns = slice(start, start + 256)
        sums = jnp.dot(low[:, :count], docs[:, columns], preferred_element_type=jnp.float32)
        sums += jnp.dot(low[:, count:], others[:, columns], preferred_element_type=jnp.float32)
        sums = sums.astype(jnp.bfloat16)
        for half in range(2):
            tile = start // 128 + half
            packed[:, tile * per : (tile + 1) * per, :] = sums[:, half * 128 : half * 128 + 128].reshape(
                PEERS, per, 128
            )


def split_kernel(place, packed, *outs):
    per = 32
    total = jnp.sum(packed[...].astype(jnp.float32), axis=0)
    counts = total[per * 8 : per * 8 + 4, :] + total[per * 8 + 4 : per * 8 + 8, :]
    row = place[0] // 4
    counts = jnp.sum(
        jnp.where(lax.broadcasted_iota(jnp.int32, (4, 128), 0) == row, counts, 0.0), axis=0, keepdims=True
    )
    lane = lax.broadcasted_iota(jnp.int32, (per, 128), 1)
    wanted = lax.broadcasted_iota(jnp.int32, (per, 128), 0) + (place[0] - row * 4) * per
    counts = jnp.sum(jnp.where(lane == wanted, counts, 0.0), axis=1, keepdims=True)
    for j, out in enumerate(outs):
        for tile in range(8):
            out[tile] = total[tile * per + j * 8 : tile * per + j * 8 + 8, :]
        out[8] = jnp.broadcast_to(counts[j * 8 : j * 8 + 8, :], (8, 128))


def final_kernel(side, mine, core, across, diagonal, centroids, out):
    same = mine[...] + core[...]
    far = across[...] + diagonal[...]
    first = side[0] == 0
    for half, part in enumerate((jnp.where(first, same, far), jnp.where(first, far, same))):
        scale = part[8] + 1.0
        for tile in range(8):
            lanes = slice(tile * 128, tile * 128 + 128)
            own = centroids[half * 8 : half * 8 + 8, lanes].astype(jnp.float32)
            out[half * 8 : half * 8 + 8, lanes] = (part[tile] + own) / scale


def call(kernel, outs, vmem, operands, scalars=0, scratch=(), flops=0):
    whole = pl.BlockSpec(memory_space=pltpu.VMEM)
    in_specs = [pl.BlockSpec(memory_space=pltpu.SMEM)] * scalars + [whole] * (len(operands) - scalars)
    return pl.pallas_call(
        kernel,
        out_shape=[jax.ShapeDtypeStruct(shape, dtype) for shape, dtype in outs],
        in_specs=in_specs,
        out_specs=[whole] * len(outs),
        scratch_shapes=scratch,
        compiler_params=pltpu.CompilerParams(vmem_limit_bytes=vmem * MIB),
        cost_estimate=pl.CostEstimate(flops=flops, bytes_accessed=MIB, transcendentals=0),
    )(*operands)


def body(documents, centroids):
    count, width = documents.shape
    beta = 3.0 / math.sqrt(width)
    others = lax.ppermute(documents, "core", SWAP)

    near = jnp.stack([lax.ppermute(centroids, ("z", "core"), toward(j, 1)) for j in range(4)])
    near = near.reshape(4, 2, 8, width).swapaxes(0, 1).reshape(1, 64, width)
    held = lax.all_to_all(
        jnp.broadcast_to(near, (8, 64, width)), ("y", "xh"), 0, 0, tiled=True
    ).reshape(512, width)

    flops = 2 * 512 * 2 * count * width
    logits, mine = call(
        functools.partial(logits_kernel, beta),
        [((512, 2 * count), jnp.float32), ((4, count), jnp.float32)],
        20,
        (held, documents, others),
        flops=flops,
    )
    theirs = lax.ppermute(mine, "core", SWAP)
    normalizer, packed = call(
        sums_kernel,
        [((1, count), jnp.float32), ((PEERS, 272, 128), jnp.bfloat16)],
        24,
        (logits, mine, theirs, documents, others),
        scratch=[pltpu.VMEM((512, 2 * count), jnp.bfloat16)],
        flops=flops,
    )

    packed = lax.all_to_all(packed, ("y", "xh", "xl"), 0, 0, tiled=True)
    side = lax.axis_index("xl")
    place = (lax.axis_index("y") * 2 + lax.axis_index("xh")) * 2 + side
    parts = call(
        split_kernel, [((9, 8, 128), jnp.float32)] * 4, 8, (place.reshape(1), packed), scalars=1
    )
    part = sum(lax.ppermute(parts[j], ("z", "core"), toward(j, -1)) for j in range(4))
    diagonal, across, core = (
        lax.ppermute(part, ("xl", "core"), [(i, i ^ bits) for i in range(4)]) for bits in (3, 2, 1)
    )
    (new_centroids,) = call(
        final_kernel,
        [((16, width), jnp.float32)],
        4,
        (side.reshape(1), part, core, across, diagonal, centroids),
        scalars=1,
    )
    return (new_centroids, normalizer.reshape(count))


def solution(mesh):
    fine = Mesh(mesh.devices.reshape(SIZES), AXES)
    in_specs = (P(AXES, None), P(("y", "xh", "z"), None))
    out_specs = (P(("y", "xh", "z"), None), P(AXES))
    return jax.shard_map(body, mesh=fine, in_specs=in_specs, out_specs=out_specs, check_vma=False)
```

time: 101 us -> 95.8 us (0.949)
  blocking collectives: 41.8 us -> 20.7 us
  waiting for transfers between devices: 13.2 us -> 30.7 us
  matrix products: 13.1 us -> 0 us
  Pallas kernels: 0 us -> 9.88 us
  starting transfers between devices: 27 us -> 32.7 us
  other arithmetic: 4.12 us -> 0.65 us
    all_to_all x1 -> x0, blocking collectives: 21.1 us -> none  [body(): packed = lax.all_to_all(packed, ('y', 'xh', 'xl'), 0, 0, tiled=True)]
    all_to_all x0 -> x1, waiting for transfers between devices: none -> 19.4 us  [body(): packed = lax.all_to_all(packed, ('y', 'xh', 'xl'), 0, 0, tiled=True)]
    dot_general x4 -> x0, matrix products: 13.1 us -> none  [the longest x2 7.46 us: scores(): lax.dot_general(piece, documents, (((1,), (1,)), ((), ())), preferred_ele...]
    pallas_call x0 -> x4, Pallas kernels: none -> 9.88 us  [call(): pl.pallas_call(kernel, out_shape=[jax.ShapeDtypeStruct(shape, dtype) for...]
    all_to_all x0 -> x1, starting transfers between devices: none -> 3.83 us  [body(): packed = lax.all_to_all(packed, ('y', 'xh', 'xl'), 0, 0, tiled=True)]
    reduce_sum x5 -> x0, other arithmetic: 2.29 us -> none  [the longest x2 0.93 us: body(): jnp.sum(jnp.exp(part - top[None, :]), axis=0)]
    ppermute x6 -> x7, starting transfers between devices: 11.8 us -> 13.7 us  [the longest x4 11.5 us: body(): lax.ppermute(parts[j], ('z', 'core'), toward(j, -1))]
    ppermute x6 -> x7, waiting for transfers between devices: 8.76 us -> 6.92 us  [the longest x4 5.51 us: body(): lax.ppermute(parts[j], ('z', 'core'), toward(j, -1))]
  transfers between devices with their start and end apart: 12 -> 14, of which waited for: 7 -> 8; matrix products, arithmetic and copies ran while one was open for 5% -> 1% of each run, Pallas kernels for 0% -> 0%
where the time goes in v2:
time: 95.8 us; the launch traced here: 95.5 us
  starting transfers between devices  32.7 us (34%)
  waiting for transfers between devices  30.7 us (32%)
  blocking collectives  20.7 us (22%)
  Pallas kernels  9.88 us (10%)
    all_to_all x1, blocking collectives, body(): lax.all_to_all(jnp.broadcast_to(near, (8, 64, width)), ('y', 'xh'), 0, 0,...  20.7 us
    all_to_all x1, waiting for transfers between devices, body(): packed = lax.all_to_all(packed, ('y', 'xh', 'xl'), 0, 0, tiled=True)  19.4 us
    ppermute x4, starting transfers between devices, body(): lax.ppermute(centroids, ('z', 'core'), toward(j, 1))  11.7 us
    ppermute x4, starting transfers between devices, body(): lax.ppermute(parts[j], ('z', 'core'), toward(j, -1))  11.5 us
    pallas_call x4, Pallas kernels, call(): pl.pallas_call(kernel, out_shape=[jax.ShapeDtypeStruct(shape, dtype) for...  9.88 us
    ppermute x4, waiting for transfers between devices, body(): lax.ppermute(parts[j], ('z', 'core'), toward(j, -1))  5.51 us
    all_to_all x1, starting transfers between devices, body(): packed = lax.all_to_all(packed, ('y', 'xh', 'xl'), 0, 0, tiled=True)  3.83 us
    ppermute x1, starting transfers between devices, body(): others = lax.ppermute(documents, 'core', SWAP)  3.33 us
  transfers between devices with their start and end apart: 14, of which 8 were waited for; matrix products, arithmetic and copies ran while one was open for 1% of the time, Pallas kernels for 0%

profile of v2, /device:TPU:1, one launch (start us, length us, event | category | flops | bytes accessed | tf_op | source)
XLA Modules:
  0.0 95.5 jit_solution(13144411578198623782)
XLA Ops:
  0.6 3.3 %collective-permute-start.4 = (bf16[1536,1024]{1,0:T(8,128)(2,1)}, bf16[1536,1024]{1,0:T(8,128)(2,1)S(1)}, u32[]{:S(2)}, u32[]{:S(2)}) collective-permute-start(bf16[1536,1024]{1,0:T(8,128)(2,1)} %docs.3), channel_id=1, source_target_pairs={{0,1},{1,0},{2,3},{3,2},{4,5},{5,4},{6,7},{7,6},{8,9},{9,8},{10,11... | collective-permute-start | bytes 9437192 | tf_op jit(solution)/shard_map/ppermute | solution.py:136
  4.0 3.3 %collective-permute-start = (bf16[16,1024]{1,0:T(8,128)(2,1)}, bf16[16,1024]{1,0:T(8,128)(2,1)S(1)}, u32[]{:S(2)}, u32[]{:S(2)}) collective-permute-start(bf16[16,1024]{1,0:T(8,128)(2,1)} %centroids.1), channel_id=1, source_target_pairs={{0,0},{25,1},{4,4},{29,5},{8,8},{1,9},{12,12},{5,13},{16,16},{9,17... | collective-permute-start | bytes 98312 | tf_op jit(solution)/shard_map/ppermute | solution.py:138
  7.3 4.7 %collective-permute-start.1 = (bf16[16,1024]{1,0:T(8,128)(2,1)}, bf16[16,1024]{1,0:T(8,128)(2,1)S(1)}, u32[]{:S(2)}, u32[]{:S(2)}) collective-permute-start(bf16[16,1024]{1,0:T(8,128)(2,1)} %centroids.1), channel_id=1, source_target_pairs={{4,0},{13,1},{8,4},{17,5},{12,8},{21,9},{16,12},{25,13},{20,16},{2... | collective-permute-start | bytes 98312 | tf_op jit(solution)/shard_map/ppermute | solution.py:138
  12.0 0.1 collective-permute-start.2
  12.1 3.6 %collective-permute-start.3 = (bf16[16,1024]{1,0:T(8,128)(2,1)}, bf16[16,1024]{1,0:T(8,128)(2,1)S(1)}, u32[]{:S(2)}, u32[]{:S(2)}) collective-permute-start(bf16[16,1024]{1,0:T(8,128)(2,1)} %centroids.1), channel_id=1, source_target_pairs={{8,0},{17,1},{12,4},{21,5},{16,8},{25,9},{20,12},{29,13},{24,16},{... | collective-permute-start | bytes 98312 | tf_op jit(solution)/shard_map/ppermute | solution.py:138
  15.7 0.0 collective-permute-done
  15.7 0.0 collective-permute-done.1
  15.7 2.3 %collective-permute-done.2 = bf16[16,1024]{1,0:T(8,128)(2,1)S(1)} collective-permute-done((bf16[16,1024]{1,0:T(8,128)(2,1)}, bf16[16,1024]{1,0:T(8,128)(2,1)S(1)}, u32[]{:S(2)}, u32[]{:S(2)}) %collective-permute-start.2) | collective-permute-done | bytes 32800 | tf_op jit(solution)/shard_map/ppermute | solution.py:138
  18.0 1.0 %collective-permute-done.3 = bf16[16,1024]{1,0:T(8,128)(2,1)S(1)} collective-permute-done((bf16[16,1024]{1,0:T(8,128)(2,1)}, bf16[16,1024]{1,0:T(8,128)(2,1)S(1)}, u32[]{:S(2)}, u32[]{:S(2)}) %collective-permute-start.3) | collective-permute-done | bytes 32800 | tf_op jit(solution)/shard_map/ppermute | solution.py:138
  19.0 0.1 broadcast_in_dim.8
  19.1 20.7 %all_to_all.10 = bf16[8,64,1024]{2,1,0:T(8,128)(2,1)S(1)} all-to-all(bf16[8,64,1024]{2,1,0:T(8,128)(2,1)S(1)} %broadcast_in_dim.8), channel_id=1, replica_groups=mesh['y'=4,'xh'=2,'z'=8,'xl'=2,'core'=2] {'y','xh'}, dimensions={0} | all-to-all | bytes 2097152 | tf_op jit(solution)/shard_map/all_to_all | solution.py:140
  39.8 0.0 collective-permute-done.4.others
  39.8 4.5 %shard_map.41 = (f32[512,3072]{1,0:T(8,128)S(1)}, f32[4,1536]{1,0:T(4,128)S(1)}) custom-call(bf16[512,1024]{1,0:T(8,128)(2,1)S(1)} %bitcast.10, bf16[1536,1024]{1,0:T(8,128)(2,1)S(1)} %copy-done, bf16[1536,1024]{1,0:T(8,128)(2,1)S(1)} %collective-permute-done.4.others), custom_call_target="tpu_custom_call" | custom-call | flops 3221225472 | bytes 1048576 | tf_op jit(solution)/shard_map/pallas_call | solution.py:122
  44.4 0.1 collective-permute-start.5
  44.5 1.2 %collective-permute-done.5.theirs = f32[4,1536]{1,0:T(4,128)S(1)} collective-permute-done((f32[4,1536]{1,0:T(4,128)S(1)}, f32[4,1536]{1,0:T(4,128)S(1)}, u32[]{:S(2)}, u32[]{:S(2)}) %collective-permute-start.5) | collective-permute-done | bytes 24608 | tf_op jit(solution)/shard_map/ppermute | solution.py:152
  45.6 4.5 %shard_map.42 = (f32[1,1536]{1,0:T(1,128)S(1)}, bf16[16,272,128]{2,1,0:T(8,128)(2,1)}) custom-call(f32[512,3072]{1,0:T(8,128)S(1)} %get-tuple-element.10.logits, f32[4,1536]{1,0:T(4,128)S(1)} %get-tuple-element.11.mine, f32[4,1536]{1,0:T(4,128)S(1)} %collective-permute-done.5.theirs, bf16[1536,1024]{1,0:T(8,128)(2,1)S(1)} %copy-done, ...), custom_call_target="tpu_custom_call" | custom-call | flops 3221225472 | bytes 1048576 | tf_op jit(solution)/shard_map/pallas_call | solution.py:122
  50.2 3.8 %all-to-all-start.1 = ((bf16[16,272,128]{2,1,0:T(8,128)(2,1)}), bf16[16,272,128]{2,1,0:T(8,128)(2,1)S(1)}, u32[]{:S(2)}, u32[]{:S(2)}) async-start(bf16[16,272,128]{2,1,0:T(8,128)(2,1)} %get-tuple-element.12), calls=%async_computation.1 | async-start | bytes 2228224 | tf_op jit(solution)/shard_map/all_to_all | solution.py:162
  54.0 19.4 %all-to-all-done.1.packed = bf16[16,272,128]{2,1,0:T(8,128)(2,1)S(1)} async-done(((bf16[16,272,128]{2,1,0:T(8,128)(2,1)}), bf16[16,272,128]{2,1,0:T(8,128)(2,1)S(1)}, u32[]{:S(2)}, u32[]{:S(2)}) %all-to-all-start.1) | async-done | bytes 1114144 | tf_op jit(solution)/shard_map/all_to_all | solution.py:162
  73.4 0.2 shard_map.43
  73.6 5.3 %collective-permute-start.6 = (f32[9,8,128]{2,1,0:T(8,128)S(1)}, f32[9,8,128]{2,1,0:T(8,128)S(1)}, u32[]{:S(2)}, u32[]{:S(2)}) collective-permute-start(f32[9,8,128]{2,1,0:T(8,128)S(1)} %get-tuple-element.13), channel_id=1, source_target_pairs={{0,0},{1,25},{4,4},{5,29},{8,8},{9,1},{12,12},{13,5},{16,16},{17,9... | collective-permute-start | bytes 110600 | tf_op jit(solution)/shard_map/ppermute | solution.py:168
  78.9 0.1 collective-permute-start.7
  79.0 4.5 %collective-permute-start.8 = (f32[9,8,128]{2,1,0:T(8,128)S(1)}, f32[9,8,128]{2,1,0:T(8,128)S(1)}, u32[]{:S(2)}, u32[]{:S(2)}) collective-permute-start(f32[9,8,128]{2,1,0:T(8,128)S(1)} %get-tuple-element.15), channel_id=1, source_target_pairs={{0,28},{1,21},{4,0},{5,25},{8,4},{9,29},{12,8},{13,1},{16,12},{17,... | collective-permute-start | bytes 110600 | tf_op jit(solution)/shard_map/ppermute | solution.py:168
  83.5 1.6 %collective-permute-start.9 = (f32[9,8,128]{2,1,0:T(8,128)S(1)}, f32[9,8,128]{2,1,0:T(8,128)S(1)}, u32[]{:S(2)}, u32[]{:S(2)}) collective-permute-start(f32[9,8,128]{2,1,0:T(8,128)S(1)} %get-tuple-element.16), channel_id=1, source_target_pairs={{0,8},{1,17},{4,12},{5,21},{8,16},{9,25},{12,20},{13,29},{16,24},{... | collective-permute-start | bytes 110600 | tf_op jit(solution)/shard_map/ppermute | solution.py:168
  85.1 0.8 collective-permute-done.7
  85.9 4.7 %collective-permute-done.9 = f32[9,8,128]{2,1,0:T(8,128)S(1)} collective-permute-done((f32[9,8,128]{2,1,0:T(8,128)S(1)}, f32[9,8,128]{2,1,0:T(8,128)S(1)}, u32[]{:S(2)}, u32[]{:S(2)}) %collective-permute-start.9) | collective-permute-done | bytes 36896 | tf_op jit(solution)/shard_map/ppermute | solution.py:168
  90.6 0.1 collective-permute-start.10
  90.7 0.1 collective-permute-start.11
  90.8 2.0 %collective-permute-start.12 = (f32[9,8,128]{2,1,0:T(8,128)S(1)}, f32[9,8,128]{2,1,0:T(8,128)S(1)}, u32[]{:S(2)}, u32[]{:S(2)}) collective-permute-start(f32[9,8,128]{2,1,0:T(8,128)S(1)} %add_add_fusion.mine), channel_id=1, source_target_pairs={{0,3},{1,2},{2,1},{3,0},{4,7},{5,6},{6,5},{7,4},{8,11},{9,10},{10,... | collective-permute-start | bytes 110600 | tf_op jit(solution)/shard_map/ppermute | solution.py:170
  92.8 0.6 reduce
  93.5 0.1 collective-permute-done.11.across
  93.6 1.3 %collective-permute-done.12.diagonal = f32[9,8,128]{2,1,0:T(8,128)S(1)} collective-permute-done((f32[9,8,128]{2,1,0:T(8,128)S(1)}, f32[9,8,128]{2,1,0:T(8,128)S(1)}, u32[]{:S(2)}, u32[]{:S(2)}) %collective-permute-start.12) | collective-permute-done | bytes 36896 | tf_op jit(solution)/shard_map/ppermute | solution.py:170
  94.9 0.7 shard_map.44
  (9 shorter events, 0.0 us)
Async XLA Ops:
  0.6 39.2 %copy-start = (bf16[1536,1024]{1,0:T(8,128)(2,1)S(1)}, bf16[1536,1024]{1,0:T(8,128)(2,1)}, u32[]{:S(2)}) copy-start(bf16[1536,1024]{1,0:T(8,128)(2,1)} %docs.3) | copy-start | bytes 9437188
  0.6 39.2 %collective-permute-start.4 = (bf16[1536,1024]{1,0:T(8,128)(2,1)}, bf16[1536,1024]{1,0:T(8,128)(2,1)S(1)}, u32[]{:S(2)}, u32[]{:S(2)}) collective-permute-start(bf16[1536,1024]{1,0:T(8,128)(2,1)} %docs.3), channel_id=1, source_target_pairs={{0,1},{1,0},{2,3},{3,2},{4,5},{5,4},{6,7},{7,6},{8,9},{9,8},{10,11... | collective-permute-start | bytes 9437192 | tf_op jit(solution)/shard_map/ppermute | solution.py:136
  4.0 11.8 %collective-permute-start = (bf16[16,1024]{1,0:T(8,128)(2,1)}, bf16[16,1024]{1,0:T(8,128)(2,1)S(1)}, u32[]{:S(2)}, u32[]{:S(2)}) collective-permute-start(bf16[16,1024]{1,0:T(8,128)(2,1)} %centroids.1), channel_id=1, source_target_pairs={{0,0},{25,1},{4,4},{29,5},{8,8},{1,9},{12,12},{5,13},{16,16},{9,17... | collective-permute-start | bytes 98312 | tf_op jit(solution)/shard_map/ppermute | solution.py:138
  7.3 8.5 %collective-permute-start.1 = (bf16[16,1024]{1,0:T(8,128)(2,1)}, bf16[16,1024]{1,0:T(8,128)(2,1)S(1)}, u32[]{:S(2)}, u32[]{:S(2)}) collective-permute-start(bf16[16,1024]{1,0:T(8,128)(2,1)} %centroids.1), channel_id=1, source_target_pairs={{4,0},{13,1},{8,4},{17,5},{12,8},{21,9},{16,12},{25,13},{20,16},{2... | collective-permute-start | bytes 98312 | tf_op jit(solution)/shard_map/ppermute | solution.py:138
  12.0 6.0 %collective-permute-start.2 = (bf16[16,1024]{1,0:T(8,128)(2,1)}, bf16[16,1024]{1,0:T(8,128)(2,1)S(1)}, u32[]{:S(2)}, u32[]{:S(2)}) collective-permute-start(bf16[16,1024]{1,0:T(8,128)(2,1)} %centroids.1), channel_id=1, source_target_pairs={{28,0},{21,1},{0,4},{25,5},{4,8},{29,9},{8,12},{1,13},{12,16},{5,1... | collective-permute-start | bytes 98312 | tf_op jit(solution)/shard_map/ppermute | solution.py:138
  12.1 6.9 %collective-permute-start.3 = (bf16[16,1024]{1,0:T(8,128)(2,1)}, bf16[16,1024]{1,0:T(8,128)(2,1)S(1)}, u32[]{:S(2)}, u32[]{:S(2)}) collective-permute-start(bf16[16,1024]{1,0:T(8,128)(2,1)} %centroids.1), channel_id=1, source_target_pairs={{8,0},{17,1},{12,4},{21,5},{16,8},{25,9},{20,12},{29,13},{24,16},{... | collective-permute-start | bytes 98312 | tf_op jit(solution)/shard_map/ppermute | solution.py:138
  44.4 1.3 %collective-permute-start.5 = (f32[4,1536]{1,0:T(4,128)S(1)}, f32[4,1536]{1,0:T(4,128)S(1)}, u32[]{:S(2)}, u32[]{:S(2)}) collective-permute-start(f32[4,1536]{1,0:T(4,128)S(1)} %get-tuple-element.11.mine), channel_id=1, source_target_pairs={{0,1},{1,0},{2,3},{3,2},{4,5},{5,4},{6,7},{7,6},{8,9},{9,8},{10,11... | collective-permute-start | bytes 73736 | tf_op jit(solution)/shard_map/ppermute | solution.py:152
  50.2 44.7 %copy-start.1 = (bf16[16,1024]{1,0:T(8,128)(2,1)S(1)}, bf16[16,1024]{1,0:T(8,128)(2,1)}, u32[]{:S(2)}) copy-start(bf16[16,1024]{1,0:T(8,128)(2,1)} %centroids.1) | copy-start | bytes 98308
  50.2 23.2 %all-to-all-start.1 = ((bf16[16,272,128]{2,1,0:T(8,128)(2,1)}), bf16[16,272,128]{2,1,0:T(8,128)(2,1)S(1)}, u32[]{:S(2)}, u32[]{:S(2)}) async-start(bf16[16,272,128]{2,1,0:T(8,128)(2,1)} %get-tuple-element.12), calls=%async_computation.1 | async-start | bytes 2228224 | tf_op jit(solution)/shard_map/all_to_all | solution.py:162
  73.6 11.5 %collective-permute-start.6 = (f32[9,8,128]{2,1,0:T(8,128)S(1)}, f32[9,8,128]{2,1,0:T(8,128)S(1)}, u32[]{:S(2)}, u32[]{:S(2)}) collective-permute-start(f32[9,8,128]{2,1,0:T(8,128)S(1)} %get-tuple-element.13), channel_id=1, source_target_pairs={{0,0},{1,25},{4,4},{5,29},{8,8},{9,1},{12,12},{13,5},{16,16},{17,9... | collective-permute-start | bytes 110600 | tf_op jit(solution)/shard_map/ppermute | solution.py:168
  78.9 7.0 %collective-permute-start.7 = (f32[9,8,128]{2,1,0:T(8,128)S(1)}, f32[9,8,128]{2,1,0:T(8,128)S(1)}, u32[]{:S(2)}, u32[]{:S(2)}) collective-permute-start(f32[9,8,128]{2,1,0:T(8,128)S(1)} %get-tuple-element.14), channel_id=1, source_target_pairs={{0,4},{1,13},{4,8},{5,17},{8,12},{9,21},{12,16},{13,25},{16,20},{1... | collective-permute-start | bytes 110600 | tf_op jit(solution)/shard_map/ppermute | solution.py:168
  79.0 6.9 %collective-permute-start.8 = (f32[9,8,128]{2,1,0:T(8,128)S(1)}, f32[9,8,128]{2,1,0:T(8,128)S(1)}, u32[]{:S(2)}, u32[]{:S(2)}) collective-permute-start(f32[9,8,128]{2,1,0:T(8,128)S(1)} %get-tuple-element.15), channel_id=1, source_target_pairs={{0,28},{1,21},{4,0},{5,25},{8,4},{9,29},{12,8},{13,1},{16,12},{17,... | collective-permute-start | bytes 110600 | tf_op jit(solution)/shard_map/ppermute | solution.py:168
  83.5 7.1 %collective-permute-start.9 = (f32[9,8,128]{2,1,0:T(8,128)S(1)}, f32[9,8,128]{2,1,0:T(8,128)S(1)}, u32[]{:S(2)}, u32[]{:S(2)}) collective-permute-start(f32[9,8,128]{2,1,0:T(8,128)S(1)} %get-tuple-element.16), channel_id=1, source_target_pairs={{0,8},{1,17},{4,12},{5,21},{8,16},{9,25},{12,20},{13,29},{16,24},{... | collective-permute-start | bytes 110600 | tf_op jit(solution)/shard_map/ppermute | solution.py:168
  90.6 2.8 %collective-permute-start.10 = (f32[9,8,128]{2,1,0:T(8,128)S(1)}, f32[9,8,128]{2,1,0:T(8,128)S(1)}, u32[]{:S(2)}, u32[]{:S(2)}) collective-permute-start(f32[9,8,128]{2,1,0:T(8,128)S(1)} %add_add_fusion.mine), channel_id=1, source_target_pairs={{0,1},{1,0},{2,3},{3,2},{4,5},{5,4},{6,7},{7,6},{8,9},{9,8},{10,11... | collective-permute-start | bytes 110600 | tf_op jit(solution)/shard_map/ppermute | solution.py:170
  90.7 2.9 %collective-permute-start.11 = (f32[9,8,128]{2,1,0:T(8,128)S(1)}, f32[9,8,128]{2,1,0:T(8,128)S(1)}, u32[]{:S(2)}, u32[]{:S(2)}) collective-permute-start(f32[9,8,128]{2,1,0:T(8,128)S(1)} %add_add_fusion.mine), channel_id=1, source_target_pairs={{0,2},{1,3},{2,0},{3,1},{4,6},{5,7},{6,4},{7,5},{8,10},{9,11},{10,... | collective-permute-start | bytes 110600 | tf_op jit(solution)/shard_map/ppermute | solution.py:170
  90.8 4.1 %collective-permute-start.12 = (f32[9,8,128]{2,1,0:T(8,128)S(1)}, f32[9,8,128]{2,1,0:T(8,128)S(1)}, u32[]{:S(2)}, u32[]{:S(2)}) collective-permute-start(f32[9,8,128]{2,1,0:T(8,128)S(1)} %add_add_fusion.mine), channel_id=1, source_target_pairs={{0,3},{1,2},{2,1},{3,0},{4,7},{5,6},{6,5},{7,4},{8,11},{9,10},{10,... | collective-permute-start | bytes 110600 | tf_op jit(solution)/shard_map/ppermute | solution.py:170

commit v3 on v2

--- a/solution.py
+++ b/solution.py
@@ -8,10 +8,10 @@
 from jax.experimental.pallas import tpu as pltpu
 from jax.sharding import Mesh, PartitionSpec as P
 
-AXES = ("y", "xh", "z", "xl", "core")
-SIZES = (4, 2, 8, 2, 2)
+AXES = ("y", "xh", "zh", "zl", "xl", "core")
+SIZES = (4, 2, 4, 2, 2, 2)
 SWAP = [(0, 1), (1, 0)]
-OFFSETS = ((0, 1, -1, 2), (-2, 3, -3, 4))
+OFFSETS = ((0, 1), (-1, 2))
 PEERS = 16
 TILE = 512
 MIB = 2**20
@@ -19,10 +19,10 @@
 
 def toward(j, sign):
     pairs = []
-    for z in range(8):
+    for zh in range(4):
         for core in range(2):
-            far = ((z + OFFSETS[core][j]) % 8) * 2 + core
-            near = z * 2 + core
+            far = ((zh + OFFSETS[core][j]) % 4) * 2 + core
+            near = zh * 2 + core
             pairs.append((far, near) if sign > 0 else (near, far))
     return pairs
 
@@ -100,20 +100,16 @@
     counts = jnp.sum(jnp.where(lane == wanted, counts, 0.0), axis=1, keepdims=True)
     for j, out in enumerate(outs):
         for tile in range(8):
-            out[tile] = total[tile * per + j * 8 : tile * per + j * 8 + 8, :]
-        out[8] = jnp.broadcast_to(counts[j * 8 : j * 8 + 8, :], (8, 128))
+            out[tile] = total[tile * per + j * 16 : tile * per + j * 16 + 16, :]
+        out[8] = jnp.broadcast_to(counts[j * 16 : j * 16 + 16, :], (16, 128))
 
 
-def final_kernel(side, mine, core, across, diagonal, centroids, out):
-    same = mine[...] + core[...]
-    far = across[...] + diagonal[...]
-    first = side[0] == 0
-    for half, part in enumerate((jnp.where(first, same, far), jnp.where(first, far, same))):
-        scale = part[8] + 1.0
-        for tile in range(8):
-            lanes = slice(tile * 128, tile * 128 + 128)
-            own = centroids[half * 8 : half * 8 + 8, lanes].astype(jnp.float32)
-            out[half * 8 : half * 8 + 8, lanes] = (part[tile] + own) / scale
+def final_kernel(mine, core, across, diagonal, centroids, out):
+    part = (mine[...] + core[...]) + (across[...] + diagonal[...])
+    scale = part[8] + 1.0
+    for tile in range(8):
+        lanes = slice(tile * 128, tile * 128 + 128)
+        out[:, lanes] = (part[tile] + centroids[:, lanes].astype(jnp.float32)) / scale
 
 
 def call(kernel, outs, vmem, operands, scalars=0, scratch=(), flops=0):
@@ -135,10 +131,10 @@
     beta = 3.0 / math.sqrt(width)
     others = lax.ppermute(documents, "core", SWAP)
 
-    near = jnp.stack([lax.ppermute(centroids, ("z", "core"), toward(j, 1)) for j in range(4)])
-    near = near.reshape(4, 2, 8, width).swapaxes(0, 1).reshape(1, 64, width)
+    near = [lax.ppermute(centroids, ("zh", "core"), toward(j, 1)) for j in range(2)]
+    near = jnp.concatenate(near).reshape(1, 32, width)
     held = lax.all_to_all(
-        jnp.broadcast_to(near, (8, 64, width)), ("y", "xh"), 0, 0, tiled=True
+        jnp.broadcast_to(near, (PEERS, 32, width)), ("y", "xh", "zl"), 0, 0, tiled=True
     ).reshape(512, width)
 
     flops = 2 * 512 * 2 * count * width
@@ -159,13 +155,12 @@
         flops=flops,
     )
 
-    packed = lax.all_to_all(packed, ("y", "xh", "xl"), 0, 0, tiled=True)
-    side = lax.axis_index("xl")
-    place = (lax.axis_index("y") * 2 + lax.axis_index("xh")) * 2 + side
+    packed = lax.all_to_all(packed, ("y", "xh", "zl"), 0, 0, tiled=True)
+    place = (lax.axis_index("y") * 2 + lax.axis_index("xh")) * 2 + lax.axis_index("zl")
     parts = call(
-        split_kernel, [((9, 8, 128), jnp.float32)] * 4, 8, (place.reshape(1), packed), scalars=1
+        split_kernel, [((9, 16, 128), jnp.float32)] * 2, 8, (place.reshape(1), packed), scalars=1
     )
-    part = sum(lax.ppermute(parts[j], ("z", "core"), toward(j, -1)) for j in range(4))
+    part = sum(lax.ppermute(parts[j], ("zh", "core"), toward(j, -1)) for j in range(2))
     diagonal, across, core = (
         lax.ppermute(part, ("xl", "core"), [(i, i ^ bits) for i in range(4)]) for bits in (3, 2, 1)
     )
@@ -173,14 +168,13 @@
         final_kernel,
         [((16, width), jnp.float32)],
         4,
-        (side.reshape(1), part, core, across, diagonal, centroids),
-        scalars=1,
+        (part, core, across, diagonal, centroids),
     )
     return (new_centroids, normalizer.reshape(count))
 
 
 def solution(mesh):
     fine = Mesh(mesh.devices.reshape(SIZES), AXES)
-    in_specs = (P(AXES, None), P(("y", "xh", "z"), None))
-    out_specs = (P(("y", "xh", "z"), None), P(AXES))
+    in_specs = (P(AXES, None), P(AXES[:4], None))
+    out_specs = (P(AXES[:4], None), P(AXES))
     return jax.shard_map(body, mesh=fine, in_specs=in_specs, out_specs=out_specs, check_vma=False)

time: 95.8 us -> 88.9 us (0.928)
  starting transfers between devices: 32.7 us -> 25.6 us
  blocking collectives: 20.7 us -> 22.5 us
  waiting for transfers between devices: 30.7 us -> 29 us
    ppermute x8 -> x4, starting transfers between devices: 23.2 us -> 15.7 us  [the longest x2 8.47 us: body(): lax.ppermute(centroids, ('zh', 'core'), toward(j, 1))]
    all_to_all x1, waiting for transfers between devices: 19.4 us -> 16.3 us  [body(): packed = lax.all_to_all(packed, ('y', 'xh', 'zl'), 0, 0, tiled=True)]
    all_to_all x1, blocking collectives: 20.7 us -> 22.5 us  [body(): lax.all_to_all(jnp.broadcast_to(near, (PEERS, 32, width)), ('y', 'xh', 'z...]
    ppermute x3, waiting for transfers between devices: 1.41 us -> 3 us  [body(): lax.ppermute(part, ('xl', 'core'), [(i, i ^ bits) for i in range(4)])]
    ppermute x8 -> x4, waiting for transfers between devices: 8.76 us -> 8.58 us  [the longest x2 6.8 us: body(): lax.ppermute(parts[j], ('zh', 'core'), toward(j, -1))]
  transfers between devices with their start and end apart: 14 -> 10, of which waited for: 8 -> 7; matrix products, arithmetic and copies ran while one was open for 1% -> 1% of each run, Pallas kernels for 0% -> 0%
where the time goes in v3:
time: 88.9 us; the launch traced here: 88.6 us
  waiting for transfers between devices  29 us (33%)
  starting transfers between devices  25.6 us (29%)
  blocking collectives  22.5 us (25%)
  Pallas kernels  9.89 us (11%)
    all_to_all x1, blocking collectives, body(): lax.all_to_all(jnp.broadcast_to(near, (PEERS, 32, width)), ('y', 'xh', 'z...  22.5 us
    all_to_all x1, waiting for transfers between devices, body(): packed = lax.all_to_all(packed, ('y', 'xh', 'zl'), 0, 0, tiled=True)  16.3 us
    pallas_call x4, Pallas kernels, call(): pl.pallas_call(kernel, out_shape=[jax.ShapeDtypeStruct(shape, dtype) for...  9.89 us
    ppermute x2, starting transfers between devices, body(): lax.ppermute(centroids, ('zh', 'core'), toward(j, 1))  8.47 us
    ppermute x2, starting transfers between devices, body(): lax.ppermute(parts[j], ('zh', 'core'), toward(j, -1))  7.19 us
    ppermute x2, waiting for transfers between devices, body(): lax.ppermute(parts[j], ('zh', 'core'), toward(j, -1))  6.8 us
    all_to_all x1, starting transfers between devices, body(): packed = lax.all_to_all(packed, ('y', 'xh', 'zl'), 0, 0, tiled=True)  4.34 us
    ppermute x1, starting transfers between devices, body(): others = lax.ppermute(documents, 'core', SWAP)  3.33 us
  transfers between devices with their start and end apart: 10, of which 7 were waited for; matrix products, arithmetic and copies ran while one was open for 1% of the time, Pallas kernels for 0%

profile of v3, /device:TPU:1, one launch (start us, length us, event | category | flops | bytes accessed | tf_op | source)
XLA Modules:
  0.0 88.6 jit_solution(6196153683309441615)
XLA Ops:
  0.6 0.0 copy-start
  0.6 3.3 %collective-permute-start.2 = (bf16[1536,1024]{1,0:T(8,128)(2,1)}, bf16[1536,1024]{1,0:T(8,128)(2,1)S(1)}, u32[]{:S(2)}, u32[]{:S(2)}) collective-permute-start(bf16[1536,1024]{1,0:T(8,128)(2,1)} %docs.3), channel_id=1, source_target_pairs={{0,1},{1,0},{2,3},{3,2},{4,5},{5,4},{6,7},{7,6},{8,9},{9,8},{10,11... | collective-permute-start | bytes 9437192 | tf_op jit(solution)/shard_map/ppermute | solution.py:132
  4.0 3.3 %collective-permute-start = (bf16[16,1024]{1,0:T(8,128)(2,1)}, bf16[16,1024]{1,0:T(8,128)(2,1)S(1)}, u32[]{:S(2)}, u32[]{:S(2)}) collective-permute-start(bf16[16,1024]{1,0:T(8,128)(2,1)} %centroids.1), channel_id=1, source_target_pairs={{0,0},{25,1},{8,8},{1,9},{16,16},{9,17},{24,24},{17,25},{2,2},{27,... | collective-permute-start | bytes 98312 | tf_op jit(solution)/shard_map/ppermute | solution.py:134
  7.3 5.2 %collective-permute-start.1 = (bf16[16,1024]{1,0:T(8,128)(2,1)}, bf16[16,1024]{1,0:T(8,128)(2,1)S(1)}, u32[]{:S(2)}, u32[]{:S(2)}) collective-permute-start(bf16[16,1024]{1,0:T(8,128)(2,1)} %centroids.1), channel_id=1, source_target_pairs={{8,0},{17,1},{16,8},{25,9},{24,16},{1,17},{0,24},{9,25},{10,2},{19... | collective-permute-start | bytes 98312 | tf_op jit(solution)/shard_map/ppermute | solution.py:134
  12.4 0.0 collective-permute-done
  12.5 1.8 %collective-permute-done.1 = bf16[16,1024]{1,0:T(8,128)(2,1)S(1)} collective-permute-done((bf16[16,1024]{1,0:T(8,128)(2,1)}, bf16[16,1024]{1,0:T(8,128)(2,1)S(1)}, u32[]{:S(2)}, u32[]{:S(2)}) %collective-permute-start.1) | collective-permute-done | bytes 32800 | tf_op jit(solution)/shard_map/ppermute | solution.py:134
  14.2 0.1 broadcast_in_dim.2
  14.4 22.5 %all_to_all.10 = bf16[16,32,1024]{2,1,0:T(8,128)(2,1)S(1)} all-to-all(bf16[16,32,1024]{2,1,0:T(8,128)(2,1)S(1)} %broadcast_in_dim.2), channel_id=1, replica_groups=mesh['y'=4,'xh'=2,'zh'=4,'zl'=2,'xl'=2,'core'=2] {'y','xh','zl'}, dimensions={0} | all-to-all | bytes 2097152 | tf_op jit(solution)/shard_map/all_to_all | solution.py:136
  36.9 0.0 collective-permute-done.2.others
  36.9 0.0 copy-done
  36.9 4.5 %shard_map.41 = (f32[512,3072]{1,0:T(8,128)S(1)}, f32[4,1536]{1,0:T(4,128)S(1)}) custom-call(bf16[512,1024]{1,0:T(8,128)(2,1)S(1)} %bitcast.2, bf16[1536,1024]{1,0:T(8,128)(2,1)S(1)} %copy-done, bf16[1536,1024]{1,0:T(8,128)(2,1)S(1)} %collective-permute-done.2.others), custom_call_target="tpu_custom_call" | custom-call | flops 3221225472 | bytes 1048576 | tf_op jit(solution)/shard_map/pallas_call | solution.py:118
  41.4 0.1 collective-permute-start.3
  41.5 1.2 %collective-permute-done.3.theirs = f32[4,1536]{1,0:T(4,128)S(1)} collective-permute-done((f32[4,1536]{1,0:T(4,128)S(1)}, f32[4,1536]{1,0:T(4,128)S(1)}, u32[]{:S(2)}, u32[]{:S(2)}) %collective-permute-start.3) | collective-permute-done | bytes 24608 | tf_op jit(solution)/shard_map/ppermute | solution.py:148
  42.7 4.5 %shard_map.42 = (f32[1,1536]{1,0:T(1,128)S(1)}, bf16[16,272,128]{2,1,0:T(8,128)(2,1)}) custom-call(f32[512,3072]{1,0:T(8,128)S(1)} %get-tuple-element.8.logits, f32[4,1536]{1,0:T(4,128)S(1)} %get-tuple-element.9.mine, f32[4,1536]{1,0:T(4,128)S(1)} %collective-permute-done.3.theirs, bf16[1536,1024]{1,0:T(8,128)(2,1)S(1)} %copy-done, ...), custom_call_target="tpu_custom_call" | custom-call | flops 3221225472 | bytes 1048576 | tf_op jit(solution)/shard_map/pallas_call | solution.py:118
  47.2 0.0 copy-start.1
  47.2 4.3 %all-to-all-start.1 = ((bf16[16,272,128]{2,1,0:T(8,128)(2,1)}), bf16[16,272,128]{2,1,0:T(8,128)(2,1)S(1)}, u32[]{:S(2)}, u32[]{:S(2)}) async-start(bf16[16,272,128]{2,1,0:T(8,128)(2,1)} %get-tuple-element.10), calls=%async_computation.1 | async-start | bytes 2228224 | tf_op jit(solution)/shard_map/all_to_all | solution.py:158
  51.6 16.3 %all-to-all-done.1.packed = bf16[16,272,128]{2,1,0:T(8,128)(2,1)S(1)} async-done(((bf16[16,272,128]{2,1,0:T(8,128)(2,1)}), bf16[16,272,128]{2,1,0:T(8,128)(2,1)S(1)}, u32[]{:S(2)}, u32[]{:S(2)}) %all-to-all-start.1) | async-done | bytes 1114144 | tf_op jit(solution)/shard_map/all_to_all | solution.py:158
  67.8 0.2 shard_map.43
  68.0 5.9 %collective-permute-start.4 = (f32[9,16,128]{2,1,0:T(8,128)S(1)}, f32[9,16,128]{2,1,0:T(8,128)S(1)}, u32[]{:S(2)}, u32[]{:S(2)}) collective-permute-start(f32[9,16,128]{2,1,0:T(8,128)S(1)} %get-tuple-element.11), channel_id=1, source_target_pairs={{0,0},{1,25},{8,8},{9,1},{16,16},{17,9},{24,24},{25,17},{2,2},{3,2... | collective-permute-start | bytes 221192 | tf_op jit(solution)/shard_map/ppermute | solution.py:163
  74.0 1.3 %collective-permute-start.5 = (f32[9,16,128]{2,1,0:T(8,128)S(1)}, f32[9,16,128]{2,1,0:T(8,128)S(1)}, u32[]{:S(2)}, u32[]{:S(2)}) collective-permute-start(f32[9,16,128]{2,1,0:T(8,128)S(1)} %get-tuple-element.12), channel_id=1, source_target_pairs={{0,8},{1,17},{8,16},{9,25},{16,24},{17,1},{24,0},{25,9},{2,10},{3,... | collective-permute-start | bytes 221192 | tf_op jit(solution)/shard_map/ppermute | solution.py:163
  75.2 0.7 collective-permute-done.4
  76.0 6.1 %collective-permute-done.5 = f32[9,16,128]{2,1,0:T(8,128)S(1)} collective-permute-done((f32[9,16,128]{2,1,0:T(8,128)S(1)}, f32[9,16,128]{2,1,0:T(8,128)S(1)}, u32[]{:S(2)}, u32[]{:S(2)}) %collective-permute-start.5) | collective-permute-done | bytes 73760 | tf_op jit(solution)/shard_map/ppermute | solution.py:163
  82.1 0.1 collective-permute-start.6
  82.2 0.9 %collective-permute-start.7 = (f32[9,16,128]{2,1,0:T(8,128)S(1)}, f32[9,16,128]{2,1,0:T(8,128)S(1)}, u32[]{:S(2)}, u32[]{:S(2)}) collective-permute-start(f32[9,16,128]{2,1,0:T(8,128)S(1)} %add.11.mine), channel_id=1, source_target_pairs={{0,2},{1,3},{2,0},{3,1},{4,6},{5,7},{6,4},{7,5},{8,10},{9,11},{10,... | collective-permute-start | bytes 221192 | tf_op jit(solution)/shard_map/ppermute | solution.py:165
  83.1 1.2 %collective-permute-start.8 = (f32[9,16,128]{2,1,0:T(8,128)S(1)}, f32[9,16,128]{2,1,0:T(8,128)S(1)}, u32[]{:S(2)}, u32[]{:S(2)}) collective-permute-start(f32[9,16,128]{2,1,0:T(8,128)S(1)} %add.11.mine), channel_id=1, source_target_pairs={{0,3},{1,2},{2,1},{3,0},{4,7},{5,6},{6,5},{7,4},{8,11},{9,10},{10,... | collective-permute-start | bytes 221192 | tf_op jit(solution)/shard_map/ppermute | solution.py:165
  84.3 0.6 reduce
  84.9 0.0 collective-permute-done.6.core
  84.9 0.5 collective-permute-done.7.across
  85.5 2.5 %collective-permute-done.8.diagonal = f32[9,16,128]{2,1,0:T(8,128)S(1)} collective-permute-done((f32[9,16,128]{2,1,0:T(8,128)S(1)}, f32[9,16,128]{2,1,0:T(8,128)S(1)}, u32[]{:S(2)}, u32[]{:S(2)}) %collective-permute-start.8) | collective-permute-done | bytes 73760 | tf_op jit(solution)/shard_map/ppermute | solution.py:165
  87.9 0.0 copy-done.1
  87.9 0.7 shard_map.44
  (2 shorter events, 0.0 us)
Async XLA Ops:
  0.6 36.3 %copy-start = (bf16[1536,1024]{1,0:T(8,128)(2,1)S(1)}, bf16[1536,1024]{1,0:T(8,128)(2,1)}, u32[]{:S(2)}) copy-start(bf16[1536,1024]{1,0:T(8,128)(2,1)} %docs.3) | copy-start | bytes 9437188
  0.6 36.3 %collective-permute-start.2 = (bf16[1536,1024]{1,0:T(8,128)(2,1)}, bf16[1536,1024]{1,0:T(8,128)(2,1)S(1)}, u32[]{:S(2)}, u32[]{:S(2)}) collective-permute-start(bf16[1536,1024]{1,0:T(8,128)(2,1)} %docs.3), channel_id=1, source_target_pairs={{0,1},{1,0},{2,3},{3,2},{4,5},{5,4},{6,7},{7,6},{8,9},{9,8},{10,11... | collective-permute-start | bytes 9437192 | tf_op jit(solution)/shard_map/ppermute | solution.py:132
  4.0 8.5 %collective-permute-start = (bf16[16,1024]{1,0:T(8,128)(2,1)}, bf16[16,1024]{1,0:T(8,128)(2,1)S(1)}, u32[]{:S(2)}, u32[]{:S(2)}) collective-permute-start(bf16[16,1024]{1,0:T(8,128)(2,1)} %centroids.1), channel_id=1, source_target_pairs={{0,0},{25,1},{8,8},{1,9},{16,16},{9,17},{24,24},{17,25},{2,2},{27,... | collective-permute-start | bytes 98312 | tf_op jit(solution)/shard_map/ppermute | solution.py:134
  7.3 7.0 %collective-permute-start.1 = (bf16[16,1024]{1,0:T(8,128)(2,1)}, bf16[16,1024]{1,0:T(8,128)(2,1)S(1)}, u32[]{:S(2)}, u32[]{:S(2)}) collective-permute-start(bf16[16,1024]{1,0:T(8,128)(2,1)} %centroids.1), channel_id=1, source_target_pairs={{8,0},{17,1},{16,8},{25,9},{24,16},{1,17},{0,24},{9,25},{10,2},{19... | collective-permute-start | bytes 98312 | tf_op jit(solution)/shard_map/ppermute | solution.py:134
  41.4 1.3 %collective-permute-start.3 = (f32[4,1536]{1,0:T(4,128)S(1)}, f32[4,1536]{1,0:T(4,128)S(1)}, u32[]{:S(2)}, u32[]{:S(2)}) collective-permute-start(f32[4,1536]{1,0:T(4,128)S(1)} %get-tuple-element.9.mine), channel_id=1, source_target_pairs={{0,1},{1,0},{2,3},{3,2},{4,5},{5,4},{6,7},{7,6},{8,9},{9,8},{10,11... | collective-permute-start | bytes 73736 | tf_op jit(solution)/shard_map/ppermute | solution.py:148
  47.2 40.7 %copy-start.1 = (bf16[16,1024]{1,0:T(8,128)(2,1)S(1)}, bf16[16,1024]{1,0:T(8,128)(2,1)}, u32[]{:S(2)}) copy-start(bf16[16,1024]{1,0:T(8,128)(2,1)} %centroids.1) | copy-start | bytes 98308
  47.2 20.6 %all-to-all-start.1 = ((bf16[16,272,128]{2,1,0:T(8,128)(2,1)}), bf16[16,272,128]{2,1,0:T(8,128)(2,1)S(1)}, u32[]{:S(2)}, u32[]{:S(2)}) async-start(bf16[16,272,128]{2,1,0:T(8,128)(2,1)} %get-tuple-element.10), calls=%async_computation.1 | async-start | bytes 2228224 | tf_op jit(solution)/shard_map/all_to_all | solution.py:158
  68.0 7.9 %collective-permute-start.4 = (f32[9,16,128]{2,1,0:T(8,128)S(1)}, f32[9,16,128]{2,1,0:T(8,128)S(1)}, u32[]{:S(2)}, u32[]{:S(2)}) collective-permute-start(f32[9,16,128]{2,1,0:T(8,128)S(1)} %get-tuple-element.11), channel_id=1, source_target_pairs={{0,0},{1,25},{8,8},{9,1},{16,16},{17,9},{24,24},{25,17},{2,2},{3,2... | collective-permute-start | bytes 221192 | tf_op jit(solution)/shard_map/ppermute | solution.py:163
  74.0 8.1 %collective-permute-start.5 = (f32[9,16,128]{2,1,0:T(8,128)S(1)}, f32[9,16,128]{2,1,0:T(8,128)S(1)}, u32[]{:S(2)}, u32[]{:S(2)}) collective-permute-start(f32[9,16,128]{2,1,0:T(8,128)S(1)} %get-tuple-element.12), channel_id=1, source_target_pairs={{0,8},{1,17},{8,16},{9,25},{16,24},{17,1},{24,0},{25,9},{2,10},{3,... | collective-permute-start | bytes 221192 | tf_op jit(solution)/shard_map/ppermute | solution.py:163
  82.1 2.9 %collective-permute-start.6 = (f32[9,16,128]{2,1,0:T(8,128)S(1)}, f32[9,16,128]{2,1,0:T(8,128)S(1)}, u32[]{:S(2)}, u32[]{:S(2)}) collective-permute-start(f32[9,16,128]{2,1,0:T(8,128)S(1)} %add.11.mine), channel_id=1, source_target_pairs={{0,1},{1,0},{2,3},{3,2},{4,5},{5,4},{6,7},{7,6},{8,9},{9,8},{10,11... | collective-permute-start | bytes 221192 | tf_op jit(solution)/shard_map/ppermute | solution.py:165
  82.2 3.3 %collective-permute-start.7 = (f32[9,16,128]{2,1,0:T(8,128)S(1)}, f32[9,16,128]{2,1,0:T(8,128)S(1)}, u32[]{:S(2)}, u32[]{:S(2)}) collective-permute-start(f32[9,16,128]{2,1,0:T(8,128)S(1)} %add.11.mine), channel_id=1, source_target_pairs={{0,2},{1,3},{2,0},{3,1},{4,6},{5,7},{6,4},{7,5},{8,10},{9,11},{10,... | collective-permute-start | bytes 221192 | tf_op jit(solution)/shard_map/ppermute | solution.py:165
  83.1 4.8 %collective-permute-start.8 = (f32[9,16,128]{2,1,0:T(8,128)S(1)}, f32[9,16,128]{2,1,0:T(8,128)S(1)}, u32[]{:S(2)}, u32[]{:S(2)}) collective-permute-start(f32[9,16,128]{2,1,0:T(8,128)S(1)} %add.11.mine), channel_id=1, source_target_pairs={{0,3},{1,2},{2,1},{3,0},{4,7},{5,6},{6,5},{7,4},{8,11},{9,10},{10,... | collective-permute-start | bytes 221192 | tf_op jit(solution)/shard_map/ppermute | solution.py:165

commit v4 on v0

v4 whole, which is shorter than its diff:
```python
import functools
import math

import jax
import jax.numpy as jnp
from jax import lax
from jax.experimental import pallas as pl
from jax.experimental.pallas import tpu as pltpu
from jax.sharding import PartitionSpec as P

BOTH = ("blk", "dp")
TILE = 512
MIB = 2**20
QUARTERS = [
    [((label - 2 * z) % 4 * 2 + x_hi) * 8 + z for z in range(8) for x_hi in range(2)] for label in range(4)
]


def star(side, sign):
    found = []
    for source in range(256):
        blk, dp = divmod(source, 4)
        y, x_hi, z = blk // 16, blk // 8 % 2, blk % 8
        if side == 2:
            z = (z + sign * (1 - 2 * (dp % 2))) % 8
        else:
            y = (y + sign * (1 - 2 * side)) % 4
        found.append((source, ((y * 2 + x_hi) * 8 + z) * 4 + dp))
    return found


def within(bits):
    return [(i, i ^ bits) for i in range(4)]


def turn_kernel(source, out):
    for start in range(0, source.shape[0], TILE):
        out[:, start : start + TILE] = source[start : start + TILE, :].T


def logits_kernel(beta, old, *refs):
    *refs, logits, stats, held = refs
    before, refs = refs[:old], refs[old:]
    *quarters, docs, others = refs
    count = docs.shape[1]
    for i, quarter in enumerate(quarters):
        held[i * 128 : i * 128 + 128, :] = quarter[...]
    block = held[...]
    wide = block.astype(jnp.float32)
    shift = (0.5 * beta) * jnp.sum(wide * wide, axis=1, keepdims=True)
    for side, source in enumerate((docs, others)):
        for start in range(0, count, TILE):
            columns = slice(start, start + TILE)
            part = jnp.dot(block, source[:, columns], preferred_element_type=jnp.float32)
            part = beta * part - shift
            logits[:, side * count + start : side * count + start + TILE] = part
            top = jnp.max(part, axis=0, keepdims=True)
            for stat in before:
                top = jnp.maximum(top, stat[side : side + 1, columns])
            total = jnp.sum(jnp.exp(part - top), axis=0, keepdims=True)
            for stat in before:
                total += stat[2 + side : 3 + side, columns] * jnp.exp(stat[side : side + 1, columns] - top)
            stats[side : side + 1, columns] = top
            stats[2 + side : 3 + side, columns] = total


def two_rows(counts):
    high = counts.astype(jnp.bfloat16)
    rest = (counts - high.astype(jnp.float32)).astype(jnp.bfloat16)
    return jnp.concatenate([high, rest, jnp.zeros((14, 128), jnp.bfloat16)], axis=0)


def write_sums(low, docs, others, rows, counts, outs):
    count = docs.shape[0]
    for i, out in enumerate(outs):
        row = counts[i : i + 1, :]
        if out.dtype == jnp.float32:
            out[1024:1032, :] = jnp.broadcast_to(row, (8, 128))
        else:
            out[1024:1040, :] = two_rows(row)
    for start in range(0, docs.shape[1], 256):
        columns = slice(start, start + 256)
        sums = jnp.dot(low[rows, :count], docs[:, columns], preferred_element_type=jnp.float32)
        sums += jnp.dot(low[rows, count:], others[:, columns], preferred_element_type=jnp.float32)
        for i, out in enumerate(outs):
            for half in range(2):
                part = sums[i * 128 : i * 128 + 128, half * 128 : half * 128 + 128]
                out[start + half * 128 : start + half * 128 + 128, :] = part.astype(out.dtype)


def weights_kernel(first, second, mine, theirs, docs, others, normalizer, low, rest, up, down):
    count = docs.shape[0]
    counts = jnp.zeros((512, 128), jnp.float32)
    for side in range(2):
        a, b = mine[side : side + 1, :], theirs[1 - side : 2 - side, :]
        top = jnp.maximum(a, b)
        total = mine[2 + side : 3 + side, :] * jnp.exp(a - top)
        total += theirs[3 - side : 4 - side, :] * jnp.exp(b - top)
        norm = top + jnp.log(total)
        if side == 0:
            normalizer[...] = norm
        for start in range(0, count, TILE):
            at = slice(side * count + start, side * count + start + TILE)
            logits = jnp.concatenate([second[:, at], first[:, at]], axis=0)
            weights = jnp.exp(logits - norm[:, start : start + TILE])
            for k in range(0, TILE, 128):
                counts += weights[:, k : k + 128]
            low[:, at] = weights.astype(jnp.bfloat16)
    flat = jnp.sum(counts.T, axis=0, keepdims=True)
    flat = jnp.concatenate([flat[:, i : i + 128] for i in range(0, 512, 128)], axis=0)
    rest[...] = flat[2:4, :]
    write_sums(low, docs, others, slice(0, 256), flat, (up, down))


def rest_kernel(low, counts, docs, others, deep, own):
    write_sums(low, docs, others, slice(256, 512), counts, (deep, own))


def star_kernel(own, up, down, deep, packed):
    counts = own[1024:1025, :]
    for part in (up, down, deep):
        rows = part[1024:1040, :].astype(jnp.float32)
        counts = counts + (rows[0:1, :] + rows[1:2, :])

    def total(tile):
        rows = slice(tile * 128, tile * 128 + 128)
        left = own[rows, :] + up[rows, :].astype(jnp.float32)
        right = down[rows, :].astype(jnp.float32) + deep[rows, :].astype(jnp.float32)
        return (left + right).reshape(16, 8, 128)

    for tile in range(0, 8, 2):
        pair = jnp.concatenate([total(tile), total(tile + 1)], axis=1)
        packed[:, tile * 8 : tile * 8 + 16, :] = pair.astype(jnp.bfloat16)
    slab = two_rows(counts)
    for member in range(16):
        packed[member, 64:80, :] = slab


def group_kernel(place, packed, out):
    total = jnp.sum(packed[...].astype(jnp.float32), axis=0)
    for tile in range(8):
        out[tile] = total[tile * 8 : tile * 8 + 8, :]
    lane = lax.broadcasted_iota(jnp.int32, (8, 128), 1)
    wanted = lax.broadcasted_iota(jnp.int32, (8, 128), 0) + place[0] * 8
    counts = jnp.where(lane == wanted, total[64:65, :] + total[65:66, :], 0.0)
    out[8] = jnp.broadcast_to(jnp.sum(counts, axis=1, keepdims=True), (8, 128))


def final_kernel(core, mine, swapped, across, diagonal, centroids, out):
    same = mine[...] + across[...]
    far = swapped[...] + diagonal[...]
    first = core[0] == 0
    for half, part in enumerate((jnp.where(first, same, far), jnp.where(first, far, same))):
        scale = part[8] + 1.0
        for tile in range(8):
            lanes = slice(tile * 128, tile * 128 + 128)
            held = centroids[:, lanes].astype(jnp.float32)[half * 8 : half * 8 + 8, :]
            out[half * 8 : half * 8 + 8, lanes] = (part[tile] + held) / scale


def call(kernel, outs, vmem, operands, scalars=0, scratch=(), flops=0):
    whole = pl.BlockSpec(memory_space=pltpu.VMEM)
    return pl.pallas_call(
        kernel,
        out_shape=[jax.ShapeDtypeStruct(shape, dtype) for shape, dtype in outs],
        in_specs=[pl.BlockSpec(memory_space=pltpu.SMEM)] * scalars + [whole] * (len(operands) - scalars),
        out_specs=[whole] * len(outs),
        scratch_shapes=scratch,
        compiler_params=pltpu.CompilerParams(vmem_limit_bytes=vmem * MIB),
        cost_estimate=pl.CostEstimate(flops=flops, bytes_accessed=MIB, transcendentals=0),
    )(*operands)


def exchange(part):
    return lax.all_to_all(part, "blk", 0, 0, axis_index_groups=QUARTERS, tiled=True)


def body(documents, centroids):
    count, width = documents.shape
    beta = 3.0 / math.sqrt(width)
    blk = lax.axis_index("blk")
    core = lax.axis_index("dp") % 2
    others = lax.ppermute(documents, "dp", within(1))

    near = lax.dynamic_slice_in_dim(centroids, core * 8, 8, 0).reshape(1, 8, width)
    quarter = exchange(jnp.broadcast_to(near, (16, 8, width))).reshape(128, width)
    quarters = [quarter] + [lax.ppermute(quarter, BOTH, star(side, -1)) for side in range(3)]

    flops = 2 * 512 * 2 * count * width
    turned = [
        call(turn_kernel, [((width, count), jnp.bfloat16)], 10, (part,), flops=flops // 2)[0]
        for part in (documents, others)
    ]
    first, stats = call(
        functools.partial(logits_kernel, beta, 0),
        [((128, 2 * count), jnp.float32), ((4, count), jnp.float32)],
        12,
        (quarters[0], *turned),
        scratch=[pltpu.VMEM((128, width), jnp.bfloat16)],
        flops=flops // 2,
    )
    second, mine = call(
        functools.partial(logits_kernel, beta, 1),
        [((384, 2 * count), jnp.float32), ((4, count), jnp.float32)],
        16,
        (stats, *quarters[1:], *turned),
        scratch=[pltpu.VMEM((384, width), jnp.bfloat16)],
        flops=flops,
    )
    theirs = lax.ppermute(mine, "dp", within(1))
    slab = ((1040, 128), jnp.bfloat16)
    normalizer, low, counts, up, down = call(
        weights_kernel,
        [((1, count), jnp.float32), ((512, 2 * count), jnp.bfloat16), ((2, 128), jnp.float32), slab, slab],
        24,
        (first, second, mine, theirs, documents, others),
        flops=flops,
    )
    deep, own = call(
        rest_kernel, [slab, ((1032, 128), jnp.float32)], 16, (low, counts, documents, others), flops=flops // 2
    )
    sent = (up, down, deep)

    came = [lax.ppermute(part, BOTH, star(side, 1)) for side, part in enumerate(sent)]
    (packed,) = call(star_kernel, [((16, 80, 128), jnp.bfloat16)], 8, (own, *came))
    place = blk % 8 * 2 + blk // 8 % 2
    (part,) = call(
        group_kernel, [((9, 8, 128), jnp.float32)], 4, (place.reshape(1), exchange(packed)), scalars=1
    )
    diagonal, across, swapped = (lax.ppermute(part, "dp", within(bits)) for bits in (3, 2, 1))
    (new_centroids,) = call(
        final_kernel,
        [((16, width), jnp.float32)],
        4,
        (core.reshape(1), part, swapped, across, diagonal, centroids),
        scalars=1,
    )
    return (new_centroids, normalizer.reshape(count))


def solution(mesh):
    in_specs = (P(BOTH, None), P("blk", None))
    out_specs = (P("blk", None), P(BOTH))
    return jax.shard_map(body, mesh=mesh, in_specs=in_specs, out_specs=out_specs, check_vma=False)
```

time: 561 us -> 85.9 us (0.15)
  waiting for transfers between devices: 336 us -> 35.5 us
  blocking collectives: 189 us -> 0 us
  starting transfers between devices: 0.12 us -> 31.8 us
  between operations: 14.5 us -> 0.75 us
  Pallas kernels: 0 us -> 11.9 us
  matrix products: 10 us -> 0 us
  other arithmetic: 8.22 us -> 0.62 us
    unnamed x1 -> x0, blocking collectives: 155 us -> none
    reduce_scatter x1 -> x0, waiting for transfers between devices: 127 us -> none  [body(): lax.psum_scatter(sums, 'blk', scatter_dimension=0, tiled=True)]
    all_gather x1 -> x0, waiting for transfers between devices: 123 us -> none  [body(): lax.all_gather(centroids, 'blk', axis=0, tiled=True)]
    psum x1 -> x0, waiting for transfers between devices: 85.8 us -> none  [body(): own_sums, own_counts = lax.psum((part_sums, part_counts), 'dp')]
    psum x1 -> x0, blocking collectives: 34.2 us -> none  [body(): own_sums, own_counts = lax.psum((part_sums, part_counts), 'dp')]
    all_to_all x0 -> x2, waiting for transfers between devices: none -> 23 us  [exchange(): lax.all_to_all(part, 'blk', 0, 0, axis_index_groups=QUARTERS, tiled=True)]
    ppermute x0 -> x11, starting transfers between devices: none -> 16.4 us  [the longest x3 5.72 us: body(): lax.ppermute(part, 'dp', within(bits))]
    all_to_all x0 -> x2, starting transfers between devices: none -> 15.5 us  [exchange(): lax.all_to_all(part, 'blk', 0, 0, axis_index_groups=QUARTERS, tiled=True)]
  transfers between devices with their start and end apart: 3 -> 13, of which waited for: 3 -> 10; matrix products, arithmetic and copies ran while one was open for 1% -> 2% of each run, Pallas kernels for 0% -> 5%
where the time goes in v4:
time: 85.9 us; the launch traced here: 85.5 us
  waiting for transfers between devices  35.5 us (41%)
  starting transfers between devices  31.8 us (37%)
  Pallas kernels  11.9 us (14%)
  local copies, waits for them, and re-layouts  4.97 us (6%)
    all_to_all x2, waiting for transfers between devices, exchange(): lax.all_to_all(part, 'blk', 0, 0, axis_index_groups=QUARTERS, tiled=True)  23 us
    all_to_all x2, starting transfers between devices, exchange(): lax.all_to_all(part, 'blk', 0, 0, axis_index_groups=QUARTERS, tiled=True)  15.5 us
    pallas_call x9, Pallas kernels, call(): pl.pallas_call(kernel, out_shape=[jax.ShapeDtypeStruct(shape, dtype) for...  11.9 us
    ppermute x3, starting transfers between devices, body(): lax.ppermute(part, 'dp', within(bits))  5.72 us
    ppermute x3, waiting for transfers between devices, body(): lax.ppermute(part, BOTH, star(side, 1))  5.05 us
    ppermute x3, waiting for transfers between devices, body(): lax.ppermute(quarter, BOTH, star(side, -1))  4.75 us
    unnamed x10, local copies, waits for them, and re-layouts  3.54 us
    ppermute x3, starting transfers between devices, body(): lax.ppermute(part, BOTH, star(side, 1))  3.34 us
  transfers between devices with their start and end apart: 13, of which 10 were waited for; matrix products, arithmetic and copies ran while one was open for 2% of the time, Pallas kernels for 5%

profile of v4, /device:TPU:1, one launch (start us, length us, event | category | flops | bytes accessed | tf_op | source)
XLA Modules:
  0.0 85.5 jit_solution(1461133727129557869)
XLA Ops:
  0.6 3.3 %collective-permute-start = (bf16[1536,1024]{1,0:T(8,128)(2,1)}, bf16[1536,1024]{1,0:T(8,128)(2,1)S(1)}, u32[]{:S(2)}, u32[]{:S(2)}) collective-permute-start(bf16[1536,1024]{1,0:T(8,128)(2,1)} %docs.3), channel_id=1, source_target_pairs={{0,1},{1,0},{2,3},{3,2},{4,5},{5,4},{6,7},{7,6},{8,9},{9,8},{10,11... | collective-permute-start | bytes 9437192 | tf_op jit(solution)/shard_map/ppermute | solution.py:183
  4.0 0.7 constant_dynamic-slice_fusion
  4.7 0.7 broadcast_in_dim.2
  5.4 11.2 %all-to-all-start = ((bf16[16,8,1024]{2,1,0:T(8,128)(2,1)}), bf16[16,8,1024]{2,1,0:T(8,128)(2,1)S(1)}, u32[]{:S(2)}, u32[]{:S(2)}) async-start(bf16[16,8,1024]{2,1,0:T(8,128)(2,1)} %broadcast_in_dim.2), calls=%async_computation | async-start | bytes 524288 | tf_op jit(solution)/shard_map/all_to_all | solution.py:175
  16.6 1.9 %copy-done = bf16[1536,1024]{1,0:T(8,128)(2,1)S(1)} copy-done((bf16[1536,1024]{1,0:T(8,128)(2,1)S(1)}, bf16[1536,1024]{1,0:T(8,128)(2,1)}, u32[]{:S(2)}) %copy-start) | copy-done | bytes 3145752
  18.5 0.9 %shard_map.41.refs_1_.refs_4_ = bf16[1024,1536]{1,0:T(8,128)(2,1)S(1)} custom-call(bf16[1536,1024]{1,0:T(8,128)(2,1)S(1)} %copy-done), custom_call_target="tpu_custom_call" | custom-call | flops 1610612736 | bytes 1048576 | tf_op jit(solution)/shard_map/pallas_call | solution.py:163
  19.4 1.6 %copy-done.2 = bf16[1024,1536]{1,0:T(8,128)(2,1)} copy-done((bf16[1024,1536]{1,0:T(8,128)(2,1)}, bf16[1024,1536]{1,0:T(8,128)(2,1)S(1)}, u32[]{:S(2)}) %copy-start.2) | copy-done | bytes 3145752
  21.0 9.7 %all-to-all-done = bf16[16,8,1024]{2,1,0:T(8,128)(2,1)S(1)} async-done(((bf16[16,8,1024]{2,1,0:T(8,128)(2,1)}), bf16[16,8,1024]{2,1,0:T(8,128)(2,1)S(1)}, u32[]{:S(2)}, u32[]{:S(2)}) %all-to-all-start) | async-done | bytes 262176 | tf_op jit(solution)/shard_map/all_to_all | solution.py:175
  30.7 0.6 collective-permute-start.1
  31.3 0.9 %collective-permute-start.2 = (bf16[128,1024]{1,0:T(8,128)(2,1)S(1)}, bf16[128,1024]{1,0:T(8,128)(2,1)S(1)}, u32[]{:S(2)}, u32[]{:S(2)}) collective-permute-start(bf16[128,1024]{1,0:T(8,128)(2,1)S(1)} %bitcast.4), channel_id=1, source_target_pairs={{0,64},{1,65},{2,66},{3,67},{4,68},{5,69},{6,70},{7,71},{8,72},{9,... | collective-permute-start | bytes 786440 | tf_op jit(solution)/shard_map/ppermute | solution.py:187
  32.2 0.9 %shard_map.42.refs_2_.refs_5_ = bf16[1024,1536]{1,0:T(8,128)(2,1)S(1)} custom-call(bf16[1536,1024]{1,0:T(8,128)(2,1)S(1)} %collective-permute-done.source.others), custom_call_target="tpu_custom_call" | custom-call | flops 1610612736 | bytes 1048576 | tf_op jit(solution)/shard_map/pallas_call | solution.py:163
  33.0 1.1 %shard_map.43 = (f32[128,3072]{1,0:T(8,128)S(1)}, f32[4,1536]{1,0:T(4,128)S(1)}) custom-call(bf16[128,1024]{1,0:T(8,128)(2,1)S(1)} %bitcast.6, bf16[1024,1536]{1,0:T(8,128)(2,1)S(1)} %copy-done.3, bf16[1024,1536]{1,0:T(8,128)(2,1)S(1)} %shard_map.42.refs_2_.refs_5_), custom_call_target="tpu_custom_call" | custom-call | flops 1610612736 | bytes 1048576 | tf_op jit(solution)/shard_map/pallas_call | solution.py:163
  34.1 3.0 %collective-permute-done.1.refs_1_ = bf16[128,1024]{1,0:T(8,128)(2,1)S(1)} collective-permute-done((bf16[128,1024]{1,0:T(8,128)(2,1)S(1)}, bf16[128,1024]{1,0:T(8,128)(2,1)S(1)}, u32[]{:S(2)}, u32[]{:S(2)}) %collective-permute-start.1) | collective-permute-done | bytes 262176 | tf_op jit(solution)/shard_map/ppermute | solution.py:187
  37.1 0.6 collective-permute-done.2.refs_2_
  37.7 1.2 %collective-permute-done.3.refs_3_ = bf16[128,1024]{1,0:T(8,128)(2,1)S(1)} collective-permute-done((bf16[128,1024]{1,0:T(8,128)(2,1)S(1)}, bf16[128,1024]{1,0:T(8,128)(2,1)S(1)}, u32[]{:S(2)}, u32[]{:S(2)}) %collective-permute-start.3) | collective-permute-done | bytes 262176 | tf_op jit(solution)/shard_map/ppermute | solution.py:187
  38.9 3.2 %shard_map.44 = (f32[384,3072]{1,0:T(8,128)S(1)}, f32[4,1536]{1,0:T(4,128)S(1)}) custom-call(f32[4,1536]{1,0:T(4,128)S(1)} %get-tuple-element.14.refs_0_, bf16[128,1024]{1,0:T(8,128)(2,1)S(1)} %collective-permute-done.1.refs_1_, bf16[128,1024]{1,0:T(8,128)(2,1)S(1)} %collective-permute-done.2.refs_2_, bf16[128,1024]{1,0:T(8,128)(2,1)S(1)} %collective-permute-done.3.refs_3_, ...), custom_call_target="tpu_custom_call" | custom-call | flops 3221225472 | bytes 1048576 | tf_op jit(solution)/shard_map/pallas_call | solution.py:163
  42.1 2.5 %collective-permute-start.4 = (f32[4,1536]{1,0:T(4,128)S(1)}, f32[4,1536]{1,0:T(4,128)S(1)}, u32[]{:S(2)}, u32[]{:S(2)}) collective-permute-start(f32[4,1536]{1,0:T(4,128)S(1)} %get-tuple-element.16.mine), channel_id=1, source_target_pairs={{0,1},{1,0},{2,3},{3,2},{4,5},{5,4},{6,7},{7,6},{8,9},{9,8},{10,11... | collective-permute-start | bytes 73736 | tf_op jit(solution)/shard_map/ppermute | solution.py:210
  44.6 0.8 collective-permute-done.4.theirs
  45.4 2.4 %shard_map.45 = (f32[1,1536]{1,0:T(1,128)S(1)}, bf16[512,3072]{1,0:T(8,128)(2,1)S(1)}, f32[2,128]{1,0:T(2,128)S(1)}, bf16[1040,128]{1,0:T(8,128)(2,1)S(1)}, bf16[1040,128]{1,0:T(8,128)(2,1)S(1)}) custom-call(f32[128,3072]{1,0:T(8,128)S(1)} %get-tuple-element.13.first, f32[384,3072]{1,0:T(8,128)S(1)} %get-tuple-element.15.second, ...), custom_call_target="tpu_custom_call" | custom-call | flops 3221225472 | bytes 1048576 | tf_op jit(solution)/shard_map/pallas_call | solution.py:163
  47.9 2.7 %collective-permute-start.6 = (bf16[1040,128]{1,0:T(8,128)(2,1)S(1)}, bf16[1040,128]{1,0:T(8,128)(2,1)S(1)}, u32[]{:S(2)}, u32[]{:S(2)}) collective-permute-start(bf16[1040,128]{1,0:T(8,128)(2,1)S(1)} %get-tuple-element.21), channel_id=1, source_target_pairs={{0,192},{1,193},{2,194},{3,195},{4,196},{5,197},{6,198},{7,199},{8... | collective-permute-start | bytes 798728 | tf_op jit(solution)/shard_map/ppermute | solution.py:224
  50.6 1.8 %shard_map.46 = (bf16[1040,128]{1,0:T(8,128)(2,1)S(1)}, f32[1032,128]{1,0:T(8,128)S(1)}) custom-call(bf16[512,3072]{1,0:T(8,128)(2,1)S(1)} %get-tuple-element.17.low, f32[2,128]{1,0:T(2,128)S(1)} %get-tuple-element.18.counts, bf16[1536,1024]{1,0:T(8,128)(2,1)S(1)} %copy-done.1, bf16[1536,1024]{1,0:T(8,128)(2,1)S(1)} %collective-permute-done.source.others), custom_call_target="tpu_custom_call" | custom-call | flops 1610612736 | bytes 1048576 | tf_op jit(solution)/shard_map/pallas_call | solution.py:163
  52.4 0.6 collective-permute-start.7
  53.0 3.8 %collective-permute-done.5.up = bf16[1040,128]{1,0:T(8,128)(2,1)S(1)} collective-permute-done((bf16[1040,128]{1,0:T(8,128)(2,1)S(1)}, bf16[1040,128]{1,0:T(8,128)(2,1)S(1)}, u32[]{:S(2)}, u32[]{:S(2)}) %collective-permute-start.5) | collective-permute-done | bytes 266272 | tf_op jit(solution)/shard_map/ppermute | solution.py:224
  56.7 1.3 %collective-permute-done.7.deep = bf16[1040,128]{1,0:T(8,128)(2,1)S(1)} collective-permute-done((bf16[1040,128]{1,0:T(8,128)(2,1)S(1)}, bf16[1040,128]{1,0:T(8,128)(2,1)S(1)}, u32[]{:S(2)}, u32[]{:S(2)}) %collective-permute-start.7) | collective-permute-done | bytes 266272 | tf_op jit(solution)/shard_map/ppermute | solution.py:224
  58.0 0.9 %shard_map.47 = bf16[16,80,128]{2,1,0:T(8,128)(2,1)} custom-call(f32[1032,128]{1,0:T(8,128)S(1)} %get-tuple-element.19.own, bf16[1040,128]{1,0:T(8,128)(2,1)S(1)} %collective-permute-done.5.up, bf16[1040,128]{1,0:T(8,128)(2,1)S(1)} %collective-permute-done.6.down, bf16[1040,128]{1,0:T(8,128)(2,1)S(1)} %collective-permute-done.7.deep), custom_call_target="tpu_custom_call" | custom-call | bytes 1048576 | tf_op jit(solution)/shard_map/pallas_call | solution.py:163
  58.9 4.3 %all-to-all-start.1 = ((bf16[16,80,128]{2,1,0:T(8,128)(2,1)}), bf16[16,80,128]{2,1,0:T(8,128)(2,1)S(1)}, u32[]{:S(2)}, u32[]{:S(2)}) async-start(bf16[16,80,128]{2,1,0:T(8,128)(2,1)} %shard_map.47), calls=%async_computation.1 | async-start | bytes 655360 | tf_op jit(solution)/shard_map/all_to_all | solution.py:175
  63.2 13.4 %all-to-all-done.1.packed = bf16[16,80,128]{2,1,0:T(8,128)(2,1)S(1)} async-done(((bf16[16,80,128]{2,1,0:T(8,128)(2,1)}), bf16[16,80,128]{2,1,0:T(8,128)(2,1)S(1)}, u32[]{:S(2)}, u32[]{:S(2)}) %all-to-all-start.1) | async-done | bytes 327712 | tf_op jit(solution)/shard_map/all_to_all | solution.py:175
  76.7 4.0 %collective-permute-start.8 = (f32[9,8,128]{2,1,0:T(8,128)S(1)}, f32[9,8,128]{2,1,0:T(8,128)S(1)}, u32[]{:S(2)}, u32[]{:S(2)}) collective-permute-start(f32[9,8,128]{2,1,0:T(8,128)S(1)} %shard_map.48.mine), channel_id=1, source_target_pairs={{0,1},{1,0},{2,3},{3,2},{4,5},{5,4},{6,7},{7,6},{8,9},{9,8},{10,11... | collective-permute-start | bytes 110600 | tf_op jit(solution)/shard_map/ppermute | solution.py:230
  81.1 1.4 %collective-permute-start.10 = (f32[9,8,128]{2,1,0:T(8,128)S(1)}, f32[9,8,128]{2,1,0:T(8,128)S(1)}, u32[]{:S(2)}, u32[]{:S(2)}) collective-permute-start(f32[9,8,128]{2,1,0:T(8,128)S(1)} %shard_map.48.mine), channel_id=1, source_target_pairs={{0,3},{1,2},{2,1},{3,0},{4,7},{5,6},{6,5},{7,4},{8,11},{9,10},{10,... | collective-permute-start | bytes 110600 | tf_op jit(solution)/shard_map/ppermute | solution.py:230
  82.5 0.6 reduce
  83.6 1.3 %collective-permute-done.10.diagonal = f32[9,8,128]{2,1,0:T(8,128)S(1)} collective-permute-done((f32[9,8,128]{2,1,0:T(8,128)S(1)}, f32[9,8,128]{2,1,0:T(8,128)S(1)}, u32[]{:S(2)}, u32[]{:S(2)}) %collective-permute-start.10) | collective-permute-done | bytes 36896 | tf_op jit(solution)/shard_map/ppermute | solution.py:230
  84.9 0.7 shard_map.49
  (16 shorter events, 1.0 us)
Async XLA Ops:
  0.6 31.5 %collective-permute-start = (bf16[1536,1024]{1,0:T(8,128)(2,1)}, bf16[1536,1024]{1,0:T(8,128)(2,1)S(1)}, u32[]{:S(2)}, u32[]{:S(2)}) collective-permute-start(bf16[1536,1024]{1,0:T(8,128)(2,1)} %docs.3), channel_id=1, source_target_pairs={{0,1},{1,0},{2,3},{3,2},{4,5},{5,4},{6,7},{7,6},{8,9},{9,8},{10,11... | collective-permute-start | bytes 9437192 | tf_op jit(solution)/shard_map/ppermute | solution.py:183
  5.4 25.3 %all-to-all-start = ((bf16[16,8,1024]{2,1,0:T(8,128)(2,1)}), bf16[16,8,1024]{2,1,0:T(8,128)(2,1)S(1)}, u32[]{:S(2)}, u32[]{:S(2)}) async-start(bf16[16,8,1024]{2,1,0:T(8,128)(2,1)} %broadcast_in_dim.2), calls=%async_computation | async-start | bytes 524288 | tf_op jit(solution)/shard_map/all_to_all | solution.py:175
  16.6 1.9 %copy-start = (bf16[1536,1024]{1,0:T(8,128)(2,1)S(1)}, bf16[1536,1024]{1,0:T(8,128)(2,1)}, u32[]{:S(2)}) copy-start(bf16[1536,1024]{1,0:T(8,128)(2,1)} %docs.3) | copy-start | bytes 9437188
  19.4 1.7 %copy-start.2 = (bf16[1024,1536]{1,0:T(8,128)(2,1)}, bf16[1024,1536]{1,0:T(8,128)(2,1)S(1)}, u32[]{:S(2)}) copy-start(bf16[1024,1536]{1,0:T(8,128)(2,1)S(1)} %shard_map.41.refs_1_.refs_4_) | copy-start | bytes 9437188
  30.7 2.3 %copy-start.3 = (bf16[1024,1536]{1,0:T(8,128)(2,1)S(1)}, bf16[1024,1536]{1,0:T(8,128)(2,1)}, u32[]{:S(2)}) copy-start(bf16[1024,1536]{1,0:T(8,128)(2,1)} %copy-done.2) | copy-start | bytes 9437188
  30.7 6.4 %collective-permute-start.1 = (bf16[128,1024]{1,0:T(8,128)(2,1)S(1)}, bf16[128,1024]{1,0:T(8,128)(2,1)S(1)}, u32[]{:S(2)}, u32[]{:S(2)}) collective-permute-start(bf16[128,1024]{1,0:T(8,128)(2,1)S(1)} %bitcast.3), channel_id=1, source_target_pairs={{0,192},{1,193},{2,194},{3,195},{4,196},{5,197},{6,198},{7,199},{8... | collective-permute-start | bytes 786440 | tf_op jit(solution)/shard_map/ppermute | solution.py:187
  31.3 6.4 %collective-permute-start.2 = (bf16[128,1024]{1,0:T(8,128)(2,1)S(1)}, bf16[128,1024]{1,0:T(8,128)(2,1)S(1)}, u32[]{:S(2)}, u32[]{:S(2)}) collective-permute-start(bf16[128,1024]{1,0:T(8,128)(2,1)S(1)} %bitcast.4), channel_id=1, source_target_pairs={{0,64},{1,65},{2,66},{3,67},{4,68},{5,69},{6,70},{7,71},{8,72},{9,... | collective-permute-start | bytes 786440 | tf_op jit(solution)/shard_map/ppermute | solution.py:187
  32.1 6.7 %collective-permute-start.3 = (bf16[128,1024]{1,0:T(8,128)(2,1)S(1)}, bf16[128,1024]{1,0:T(8,128)(2,1)S(1)}, u32[]{:S(2)}, u32[]{:S(2)}) collective-permute-start(bf16[128,1024]{1,0:T(8,128)(2,1)S(1)} %bitcast.5), channel_id=1, source_target_pairs={{0,28},{1,5},{2,30},{3,7},{4,0},{5,9},{6,2},{7,11},{8,4},{9,13},{1... | collective-permute-start | bytes 786440 | tf_op jit(solution)/shard_map/ppermute | solution.py:187
  38.9 6.6 %copy-start.1 = (bf16[1536,1024]{1,0:T(8,128)(2,1)S(1)}, bf16[1536,1024]{1,0:T(8,128)(2,1)}, u32[]{:S(2)}) copy-start(bf16[1536,1024]{1,0:T(8,128)(2,1)} %docs.3) | copy-start | bytes 9437188
  42.1 3.4 %collective-permute-start.4 = (f32[4,1536]{1,0:T(4,128)S(1)}, f32[4,1536]{1,0:T(4,128)S(1)}, u32[]{:S(2)}, u32[]{:S(2)}) collective-permute-start(f32[4,1536]{1,0:T(4,128)S(1)} %get-tuple-element.16.mine), channel_id=1, source_target_pairs={{0,1},{1,0},{2,3},{3,2},{4,5},{5,4},{6,7},{7,6},{8,9},{9,8},{10,11... | collective-permute-start | bytes 73736 | tf_op jit(solution)/shard_map/ppermute | solution.py:210
  47.8 8.9 %collective-permute-start.5 = (bf16[1040,128]{1,0:T(8,128)(2,1)S(1)}, bf16[1040,128]{1,0:T(8,128)(2,1)S(1)}, u32[]{:S(2)}, u32[]{:S(2)}) collective-permute-start(bf16[1040,128]{1,0:T(8,128)(2,1)S(1)} %get-tuple-element.20), channel_id=1, source_target_pairs={{0,64},{1,65},{2,66},{3,67},{4,68},{5,69},{6,70},{7,71},{8,72},{9,... | collective-permute-start | bytes 798728 | tf_op jit(solution)/shard_map/ppermute | solution.py:224
  47.9 8.8 %collective-permute-start.6 = (bf16[1040,128]{1,0:T(8,128)(2,1)S(1)}, bf16[1040,128]{1,0:T(8,128)(2,1)S(1)}, u32[]{:S(2)}, u32[]{:S(2)}) collective-permute-start(bf16[1040,128]{1,0:T(8,128)(2,1)S(1)} %get-tuple-element.21), channel_id=1, source_target_pairs={{0,192},{1,193},{2,194},{3,195},{4,196},{5,197},{6,198},{7,199},{8... | collective-permute-start | bytes 798728 | tf_op jit(solution)/shard_map/ppermute | solution.py:224
  50.6 34.3 %copy-start.4 = (bf16[16,1024]{1,0:T(8,128)(2,1)S(1)}, bf16[16,1024]{1,0:T(8,128)(2,1)}, u32[]{:S(2)}) copy-start(bf16[16,1024]{1,0:T(8,128)(2,1)} %centroids.1) | copy-start | bytes 98308
  52.4 5.6 %collective-permute-start.7 = (bf16[1040,128]{1,0:T(8,128)(2,1)S(1)}, bf16[1040,128]{1,0:T(8,128)(2,1)S(1)}, u32[]{:S(2)}, u32[]{:S(2)}) collective-permute-start(bf16[1040,128]{1,0:T(8,128)(2,1)S(1)} %get-tuple-element.22), channel_id=1, source_target_pairs={{0,4},{1,29},{2,6},{3,31},{4,8},{5,1},{6,10},{7,3},{8,12},{9,5},{1... | collective-permute-start | bytes 798728 | tf_op jit(solution)/shard_map/ppermute | solution.py:224
  58.9 17.7 %all-to-all-start.1 = ((bf16[16,80,128]{2,1,0:T(8,128)(2,1)}), bf16[16,80,128]{2,1,0:T(8,128)(2,1)S(1)}, u32[]{:S(2)}, u32[]{:S(2)}) async-start(bf16[16,80,128]{2,1,0:T(8,128)(2,1)} %shard_map.47), calls=%async_computation.1 | async-start | bytes 655360 | tf_op jit(solution)/shard_map/all_to_all | solution.py:175
  76.7 6.3 %collective-permute-start.8 = (f32[9,8,128]{2,1,0:T(8,128)S(1)}, f32[9,8,128]{2,1,0:T(8,128)S(1)}, u32[]{:S(2)}, u32[]{:S(2)}) collective-permute-start(f32[9,8,128]{2,1,0:T(8,128)S(1)} %shard_map.48.mine), channel_id=1, source_target_pairs={{0,1},{1,0},{2,3},{3,2},{4,5},{5,4},{6,7},{7,6},{8,9},{9,8},{10,11... | collective-permute-start | bytes 110600 | tf_op jit(solution)/shard_map/ppermute | solution.py:230
  80.7 2.8 %collective-permute-start.9 = (f32[9,8,128]{2,1,0:T(8,128)S(1)}, f32[9,8,128]{2,1,0:T(8,128)S(1)}, u32[]{:S(2)}, u32[]{:S(2)}) collective-permute-start(f32[9,8,128]{2,1,0:T(8,128)S(1)} %shard_map.48.mine), channel_id=1, source_target_pairs={{0,2},{1,3},{2,0},{3,1},{4,6},{5,7},{6,4},{7,5},{8,10},{9,11},{10,... | collective-permute-start | bytes 110600 | tf_op jit(solution)/shard_map/ppermute | solution.py:230
  81.1 3.8 %collective-permute-start.10 = (f32[9,8,128]{2,1,0:T(8,128)S(1)}, f32[9,8,128]{2,1,0:T(8,128)S(1)}, u32[]{:S(2)}, u32[]{:S(2)}) collective-permute-start(f32[9,8,128]{2,1,0:T(8,128)S(1)} %shard_map.48.mine), channel_id=1, source_target_pairs={{0,3},{1,2},{2,1},{3,0},{4,7},{5,6},{6,5},{7,4},{8,11},{9,10},{10,... | collective-permute-start | bytes 110600 | tf_op jit(solution)/shard_map/ppermute | solution.py:230

commit v5 on v4

--- a/solution.py
+++ b/solution.py
@@ -11,9 +11,19 @@
 BOTH = ("blk", "dp")
 TILE = 512
 MIB = 2**20
-QUARTERS = [
-    [((label - 2 * z) % 4 * 2 + x_hi) * 8 + z for z in range(8) for x_hi in range(2)] for label in range(4)
+FIRST = (5, 5, 4, 4)
+GROUPS = [
+    [
+        (((label - 2 * z) % 4 * 2 + x_hi) * 8 + z % 8) * 4 + (x_hi ^ flip) * 2 + core
+        for z in range(FIRST[label], FIRST[label] + 8)
+        for x_hi in (1, 0)
+    ]
+    for label in range(4)
+    for flip in range(2)
+    for core in range(2)
 ]
+
+TURN = 0
 
 
 def star(side, sign):
@@ -31,6 +41,14 @@
 
 def within(bits):
     return [(i, i ^ bits) for i in range(4)]
+
+
+def repeat_kernel(core, centroids, out):
+    whole = centroids[...].astype(jnp.float32)
+    half = jnp.where(core[0] == 0, whole[:8, :], whole[8:, :])
+    twice = jnp.concatenate([half, half], axis=0).astype(jnp.bfloat16)
+    for start in range(0, 128, 16):
+        out[start : start + 16, :] = twice
 
 
 def turn_kernel(source, out):
@@ -88,7 +106,7 @@
                 out[start + half * 128 : start + half * 128 + 128, :] = part.astype(out.dtype)
 
 
-def weights_kernel(first, second, mine, theirs, docs, others, normalizer, low, rest, up, down):
+def weights_kernel(pair, deep, own, mine, theirs, docs, others, normalizer, low, rest, up, down):
     count = docs.shape[0]
     counts = jnp.zeros((512, 128), jnp.float32)
     for side in range(2):
@@ -101,7 +119,7 @@
             normalizer[...] = norm
         for start in range(0, count, TILE):
             at = slice(side * count + start, side * count + start + TILE)
-            logits = jnp.concatenate([second[:, at], first[:, at]], axis=0)
+            logits = jnp.concatenate([pair[:, at], deep[:, at], own[:, at]], axis=0)
             weights = jnp.exp(logits - norm[:, start : start + TILE])
             for k in range(0, TILE, 128):
                 counts += weights[:, k : k + 128]
@@ -112,8 +130,9 @@
     write_sums(low, docs, others, slice(0, 256), flat, (up, down))
 
 
-def rest_kernel(low, counts, docs, others, deep, own):
-    write_sums(low, docs, others, slice(256, 512), counts, (deep, own))
+def rest_kernel(index, low, counts, docs, others, out):
+    rows = slice(256 + 128 * index, 384 + 128 * index)
+    write_sums(low, docs, others, rows, counts[index : index + 1, :], (out,))
 
 
 def star_kernel(own, up, down, deep, packed):
@@ -126,7 +145,8 @@
         rows = slice(tile * 128, tile * 128 + 128)
         left = own[rows, :] + up[rows, :].astype(jnp.float32)
         right = down[rows, :].astype(jnp.float32) + deep[rows, :].astype(jnp.float32)
-        return (left + right).reshape(16, 8, 128)
+        result = (left + right).reshape(16, 8, 128)
+        return jnp.concatenate([result[TURN:], result[:TURN]], axis=0) if TURN else result
 
     for tile in range(0, 8, 2):
         pair = jnp.concatenate([total(tile), total(tile + 1)], axis=1)
@@ -146,16 +166,20 @@
     out[8] = jnp.broadcast_to(jnp.sum(counts, axis=1, keepdims=True), (8, 128))
 
 
-def final_kernel(core, mine, swapped, across, diagonal, centroids, out):
-    same = mine[...] + across[...]
-    far = swapped[...] + diagonal[...]
+def finish_kernel(core, mine, across, centroids, out):
+    part = mine[...] + across[...]
+    scale = part[8] + 1.0
+    for tile in range(8):
+        lanes = slice(tile * 128, tile * 128 + 128)
+        held = centroids[:, lanes].astype(jnp.float32)
+        held = jnp.where(core[0] == 0, held[:8, :], held[8:, :])
+        out[:, lanes] = (part[tile] + held) / scale
+
+
+def join_kernel(core, mine, other, out):
     first = core[0] == 0
-    for half, part in enumerate((jnp.where(first, same, far), jnp.where(first, far, same))):
-        scale = part[8] + 1.0
-        for tile in range(8):
-            lanes = slice(tile * 128, tile * 128 + 128)
-            held = centroids[:, lanes].astype(jnp.float32)[half * 8 : half * 8 + 8, :]
-            out[half * 8 : half * 8 + 8, lanes] = (part[tile] + held) / scale
+    out[:8, :] = jnp.where(first, mine[...], other[...])
+    out[8:, :] = jnp.where(first, other[...], mine[...])
 
 
 def call(kernel, outs, vmem, operands, scalars=0, scratch=(), flops=0):
@@ -171,8 +195,9 @@
     )(*operands)
 
 
-def exchange(part):
-    return lax.all_to_all(part, "blk", 0, 0, axis_index_groups=QUARTERS, tiled=True)
+def exchange(part, turn=0):
+    groups = [group[turn:] + group[:turn] for group in GROUPS]
+    return lax.all_to_all(part, BOTH, 0, 0, axis_index_groups=groups, tiled=True)
 
 
 def body(documents, centroids):
@@ -191,49 +216,60 @@
         call(turn_kernel, [((width, count), jnp.bfloat16)], 10, (part,), flops=flops // 2)[0]
         for part in (documents, others)
     ]
-    first, stats = call(
-        functools.partial(logits_kernel, beta, 0),
-        [((128, 2 * count), jnp.float32), ((4, count), jnp.float32)],
-        12,
-        (quarters[0], *turned),
-        scratch=[pltpu.VMEM((128, width), jnp.bfloat16)],
-        flops=flops // 2,
-    )
-    second, mine = call(
-        functools.partial(logits_kernel, beta, 1),
-        [((384, 2 * count), jnp.float32), ((4, count), jnp.float32)],
-        16,
-        (stats, *quarters[1:], *turned),
-        scratch=[pltpu.VMEM((384, width), jnp.bfloat16)],
-        flops=flops,
-    )
+    own, up, down, deep = quarters
+    logits, stats = [], []
+    for held in ((own,), (deep,), (up, down)):
+        rows = 128 * len(held)
+        part, stat = call(
+            functools.partial(logits_kernel, beta, len(stats[-1:])),
+            [((rows, 2 * count), jnp.float32), ((4, count), jnp.float32)],
+            14,
+            (*stats[-1:], *held, *turned),
+            scratch=[pltpu.VMEM((rows, width), jnp.bfloat16)],
+            flops=flops * rows // 512 // 8,
+        )
+        logits.append(part)
+        stats.append(stat)
+    mine = stats[-1]
     theirs = lax.ppermute(mine, "dp", within(1))
     slab = ((1040, 128), jnp.bfloat16)
     normalizer, low, counts, up, down = call(
         weights_kernel,
         [((1, count), jnp.float32), ((512, 2 * count), jnp.bfloat16), ((2, 128), jnp.float32), slab, slab],
         24,
-        (first, second, mine, theirs, documents, others),
+        (*logits[::-1], mine, theirs, documents, others),
         flops=flops,
     )
-    deep, own = call(
-        rest_kernel, [slab, ((1032, 128), jnp.float32)], 16, (low, counts, documents, others), flops=flops // 2
+    (deep,), (own,) = (
+        call(
+            functools.partial(rest_kernel, index),
+            [out],
+            16,
+            (low, counts, documents, others),
+            flops=flops // 64,
+        )
+        for index, out in enumerate((slab, ((1032, 128), jnp.float32)))
     )
     sent = (up, down, deep)
 
     came = [lax.ppermute(part, BOTH, star(side, 1)) for side, part in enumerate(sent)]
     (packed,) = call(star_kernel, [((16, 80, 128), jnp.bfloat16)], 8, (own, *came))
-    place = blk % 8 * 2 + blk // 8 % 2
+    label = (blk // 16 + 2 * blk) % 4
+    place = (blk - jnp.asarray(FIRST)[label]) % 8 * 2 + 1 - blk // 8 % 2
     (part,) = call(
-        group_kernel, [((9, 8, 128), jnp.float32)], 4, (place.reshape(1), exchange(packed)), scalars=1
-    )
-    diagonal, across, swapped = (lax.ppermute(part, "dp", within(bits)) for bits in (3, 2, 1))
+        group_kernel, [((9, 8, 128), jnp.float32)], 4, (place.reshape(1), exchange(packed, TURN)), scalars=1
+    )
+    across = lax.ppermute(part, "dp", within(2))
+    (half,) = call(
+        finish_kernel,
+        [((8, width), jnp.float32)],
+        4,
+        (core.reshape(1), part, across, centroids),
+        scalars=1,
+    )
+    other = lax.ppermute(half, "dp", within(1))
     (new_centroids,) = call(
-        final_kernel,
-        [((16, width), jnp.float32)],
-        4,
-        (core.reshape(1), part, swapped, across, diagonal, centroids),
-        scalars=1,
+        join_kernel, [((16, width), jnp.float32)], 4, (core.reshape(1), half, other), scalars=1
     )
     return (new_centroids, normalizer.reshape(count))
 

time: 85.9 us -> 80.3 us (0.935)
  blocking collectives: 0 us -> 19.3 us
  waiting for transfers between devices: 35.5 us -> 16.8 us
  starting transfers between devices: 31.8 us -> 26.7 us
  local copies, waits for them, and re-layouts: 4.97 us -> 3.23 us
    all_to_all x0 -> x1, blocking collectives: none -> 19.3 us  [exchange(): lax.all_to_all(part, BOTH, 0, 0, axis_index_groups=groups, tiled=True)]
    all_to_all x2 -> x1, waiting for transfers between devices: 23 us -> 7.22 us  [exchange(): lax.all_to_all(part, BOTH, 0, 0, axis_index_groups=groups, tiled=True)]
    all_to_all x2 -> x1, starting transfers between devices: 15.5 us -> 10.3 us  [exchange(): lax.all_to_all(part, BOTH, 0, 0, axis_index_groups=groups, tiled=True)]
    ppermute x3 -> x2, starting transfers between devices: 5.72 us -> 2.37 us  [the longest x1 2.35 us: body(): other = lax.ppermute(half, 'dp', within(1))]
    ppermute x3, waiting for transfers between devices: 4.75 us -> 1.73 us  [body(): lax.ppermute(quarter, BOTH, star(side, -1))]
    ppermute x3, starting transfers between devices: 3.34 us -> 5.48 us  [body(): lax.ppermute(part, BOTH, star(side, 1))]
    ppermute x3, starting transfers between devices: 1.47 us -> 3.34 us  [body(): lax.ppermute(quarter, BOTH, star(side, -1))]
    unnamed x10 -> x8, local copies, waits for them, and re-layouts: 3.54 us -> 1.9 us
  transfers between devices with their start and end apart: 13 -> 11, of which waited for: 10 -> 6; matrix products, arithmetic and copies ran while one was open for 2% -> 2% of each run, Pallas kernels for 5% -> 6%
where the time goes in v5:
time: 80.3 us; the launch traced here: 80 us
  starting transfers between devices  26.7 us (33%)
  blocking collectives  19.3 us (24%)
  waiting for transfers between devices  16.8 us (21%)
  Pallas kernels  11.9 us (15%)
  local copies, waits for them, and re-layouts  3.23 us (4%)
  between operations  1.41 us (2%)
    all_to_all x1, blocking collectives, exchange(): lax.all_to_all(part, BOTH, 0, 0, axis_index_groups=groups, tiled=True)  19.3 us
    pallas_call x12, Pallas kernels, call(): pl.pallas_call(kernel, out_shape=[jax.ShapeDtypeStruct(shape, dtype) for...  11.9 us
    all_to_all x1, starting transfers between devices, exchange(): lax.all_to_all(part, BOTH, 0, 0, axis_index_groups=groups, tiled=True)  10.3 us
    all_to_all x1, waiting for transfers between devices, exchange(): lax.all_to_all(part, BOTH, 0, 0, axis_index_groups=groups, tiled=True)  7.22 us
    ppermute x3, starting transfers between devices, body(): lax.ppermute(part, BOTH, star(side, 1))  5.48 us
    ppermute x3, waiting for transfers between devices, body(): lax.ppermute(part, BOTH, star(side, 1))  3.98 us
    ppermute x3, starting transfers between devices, body(): lax.ppermute(quarter, BOTH, star(side, -1))  3.34 us
    ppermute x1, starting transfers between devices, body(): others = lax.ppermute(documents, 'dp', within(1))  3.33 us
  transfers between devices with their start and end apart: 11, of which 6 were waited for; matrix products, arithmetic and copies ran while one was open for 2% of the time, Pallas kernels for 6%

profile of v5, /device:TPU:1, one launch (start us, length us, event | category | flops | bytes accessed | tf_op | source)
XLA Modules:
  0.0 80.0 jit_solution(1070664259556129547)
XLA Ops:
  0.6 3.3 %collective-permute-start = (bf16[1536,1024]{1,0:T(8,128)(2,1)}, bf16[1536,1024]{1,0:T(8,128)(2,1)S(1)}, u32[]{:S(2)}, u32[]{:S(2)}) collective-permute-start(bf16[1536,1024]{1,0:T(8,128)(2,1)} %docs.5), channel_id=1, source_target_pairs={{0,1},{1,0},{2,3},{3,2},{4,5},{5,4},{6,7},{7,6},{8,9},{9,8},{10,11... | collective-permute-start | bytes 9437192 | tf_op jit(solution)/shard_map/ppermute | solution.py:208
  4.0 0.7 constant_dynamic-slice_fusion
  4.7 19.3 %all_to_all.10 = bf16[16,8,1024]{2,1,0:T(8,128)(2,1)S(1)} all-to-all(bf16[16,8,1024]{2,1,0:T(8,128)(2,1)S(1)} %broadcast_in_dim.2), channel_id=1, replica_groups={{182,148,58,24,190,156,34,0,166,132,42,8,174,140,50,16},{183,149,59,25,..., dimensions={0} | all-to-all | bytes 524288 | tf_op jit(solution)/shard_map/all_to_all | solution.py:200
  24.0 0.6 collective-permute-start.3
  24.6 2.4 %collective-permute-start.2 = (bf16[128,1024]{1,0:T(8,128)(2,1)S(1)}, bf16[128,1024]{1,0:T(8,128)(2,1)S(1)}, u32[]{:S(2)}, u32[]{:S(2)}) collective-permute-start(bf16[128,1024]{1,0:T(8,128)(2,1)S(1)} %bitcast.5), channel_id=1, source_target_pairs={{0,192},{1,193},{2,194},{3,195},{4,196},{5,197},{6,198},{7,199},{8... | collective-permute-start | bytes 786440 | tf_op jit(solution)/shard_map/ppermute | solution.py:212
  27.1 0.3 collective-permute-start.1
  27.4 1.9 %copy-done = bf16[1536,1024]{1,0:T(8,128)(2,1)S(1)} copy-done((bf16[1536,1024]{1,0:T(8,128)(2,1)S(1)}, bf16[1536,1024]{1,0:T(8,128)(2,1)}, u32[]{:S(2)}) %copy-start) | copy-done | bytes 3145752
  29.2 0.9 %shard_map.50.refs_1_.refs_2_.refs_3_ = bf16[1024,1536]{1,0:T(8,128)(2,1)S(1)} custom-call(bf16[1536,1024]{1,0:T(8,128)(2,1)S(1)} %copy-done), custom_call_target="tpu_custom_call" | custom-call | flops 1610612736 | bytes 1048576 | tf_op jit(solution)/shard_map/pallas_call | solution.py:187
  30.1 0.9 %shard_map.51.refs_2_.refs_3_.refs_4_ = bf16[1024,1536]{1,0:T(8,128)(2,1)S(1)} custom-call(bf16[1536,1024]{1,0:T(8,128)(2,1)S(1)} %collective-permute-done.source.others), custom_call_target="tpu_custom_call" | custom-call | flops 1610612736 | bytes 1048576 | tf_op jit(solution)/shard_map/pallas_call | solution.py:187
  31.0 1.1 %shard_map.52 = (f32[128,3072]{1,0:T(8,128)S(1)}, f32[4,1536]{1,0:T(4,128)S(1)}) custom-call(bf16[128,1024]{1,0:T(8,128)(2,1)S(1)} %bitcast.7, bf16[1024,1536]{1,0:T(8,128)(2,1)S(1)} %shard_map.50.refs_1_.refs_2_.refs_3_, bf16[1024,1536]{1,0:T(8,128)(2,1)S(1)} %shard_map.51.refs_2_.refs_3_.refs_4_), custom_call_target="tpu_custom_call" | custom-call | flops 100663296 | bytes 1048576 | tf_op jit(solution)/shard_map/pallas_call | solution.py:187
  32.1 1.7 %collective-permute-done.1.refs_1_ = bf16[128,1024]{1,0:T(8,128)(2,1)S(1)} collective-permute-done((bf16[128,1024]{1,0:T(8,128)(2,1)S(1)}, bf16[128,1024]{1,0:T(8,128)(2,1)S(1)}, u32[]{:S(2)}, u32[]{:S(2)}) %collective-permute-start.1) | collective-permute-done | bytes 262176 | tf_op jit(solution)/shard_map/ppermute | solution.py:212
  33.8 1.1 %shard_map.53 = (f32[128,3072]{1,0:T(8,128)S(1)}, f32[4,1536]{1,0:T(4,128)S(1)}) custom-call(f32[4,1536]{1,0:T(4,128)S(1)} %get-tuple-element.13.refs_0_, bf16[128,1024]{1,0:T(8,128)(2,1)S(1)} %collective-permute-done.1.refs_1_, bf16[1024,1536]{1,0:T(8,128)(2,1)S(1)} %shard_map.50.refs_1_.refs_2_.refs_3_, ...), custom_call_target="tpu_custom_call" | custom-call | flops 100663296 | bytes 1048576 | tf_op jit(solution)/shard_map/pallas_call | solution.py:187
  34.9 2.0 %shard_map.54 = (f32[256,3072]{1,0:T(8,128)S(1)}, f32[4,1536]{1,0:T(4,128)S(1)}) custom-call(f32[4,1536]{1,0:T(4,128)S(1)} %get-tuple-element.14.refs_0_, bf16[128,1024]{1,0:T(8,128)(2,1)S(1)} %collective-permute-done.2.refs_1_, bf16[128,1024]{1,0:T(8,128)(2,1)S(1)} %collective-permute-done.3.refs_2_, ...), custom_call_target="tpu_custom_call" | custom-call | flops 201326592 | bytes 1048576 | tf_op jit(solution)/shard_map/pallas_call | solution.py:187
  36.9 1.9 %collective-permute-start.4 = (f32[4,1536]{1,0:T(4,128)S(1)}, f32[4,1536]{1,0:T(4,128)S(1)}, u32[]{:S(2)}, u32[]{:S(2)}) collective-permute-start(f32[4,1536]{1,0:T(4,128)S(1)} %get-tuple-element.18.mine), channel_id=1, source_target_pairs={{0,1},{1,0},{2,3},{3,2},{4,5},{5,4},{6,7},{7,6},{8,9},{9,8},{10,11... | collective-permute-start | bytes 73736 | tf_op jit(solution)/shard_map/ppermute | solution.py:234
  38.8 0.8 %collective-permute-done.4.theirs = f32[4,1536]{1,0:T(4,128)S(1)} collective-permute-done((f32[4,1536]{1,0:T(4,128)S(1)}, f32[4,1536]{1,0:T(4,128)S(1)}, u32[]{:S(2)}, u32[]{:S(2)}) %collective-permute-start.4) | collective-permute-done | bytes 24608 | tf_op jit(solution)/shard_map/ppermute | solution.py:234
  39.7 2.3 %shard_map.55 = (f32[1,1536]{1,0:T(1,128)S(1)}, bf16[512,3072]{1,0:T(8,128)(2,1)S(1)}, f32[2,128]{1,0:T(2,128)S(1)}, bf16[1040,128]{1,0:T(8,128)(2,1)S(1)}, bf16[1040,128]{1,0:T(8,128)(2,1)S(1)}) custom-call(f32[256,3072]{1,0:T(8,128)S(1)} %get-tuple-element.15.pair, f32[128,3072]{1,0:T(8,128)S(1)} %get-tuple-element.16.deep, ...), custom_call_target="tpu_custom_call" | custom-call | flops 3221225472 | bytes 1048576 | tf_op jit(solution)/shard_map/pallas_call | solution.py:187
  42.0 1.0 %shard_map.57 = bf16[1040,128]{1,0:T(8,128)(2,1)S(1)} custom-call(bf16[512,3072]{1,0:T(8,128)(2,1)S(1)} %get-tuple-element.19.low, f32[2,128]{1,0:T(2,128)S(1)} %get-tuple-element.20.counts, bf16[1536,1024]{1,0:T(8,128)(2,1)S(1)} %copy-done.1, bf16[1536,1024]{1,0:T(8,128)(2,1)S(1)} %collective-permute-done.source.others), custom_call_target="tpu_custom_call" | custom-call | flops 50331648 | bytes 1048576 | tf_op jit(solution)/shard_map/pallas_call | solution.py:187
  43.1 2.8 %collective-permute-start.7 = (bf16[1040,128]{1,0:T(8,128)(2,1)S(1)}, bf16[1040,128]{1,0:T(8,128)(2,1)S(1)}, u32[]{:S(2)}, u32[]{:S(2)}) collective-permute-start(bf16[1040,128]{1,0:T(8,128)(2,1)S(1)} %shard_map.57), channel_id=1, source_target_pairs={{0,4},{1,29},{2,6},{3,31},{4,8},{5,1},{6,10},{7,3},{8,12},{9,5},{1... | collective-permute-start | bytes 798728 | tf_op jit(solution)/shard_map/ppermute | solution.py:255
  45.9 2.7 %collective-permute-start.6 = (bf16[1040,128]{1,0:T(8,128)(2,1)S(1)}, bf16[1040,128]{1,0:T(8,128)(2,1)S(1)}, u32[]{:S(2)}, u32[]{:S(2)}) collective-permute-start(bf16[1040,128]{1,0:T(8,128)(2,1)S(1)} %get-tuple-element.22), channel_id=1, source_target_pairs={{0,192},{1,193},{2,194},{3,195},{4,196},{5,197},{6,198},{7,199},{8... | collective-permute-start | bytes 798728 | tf_op jit(solution)/shard_map/ppermute | solution.py:255
  48.5 1.0 %shard_map.56.own = f32[1032,128]{1,0:T(8,128)S(1)} custom-call(bf16[512,3072]{1,0:T(8,128)(2,1)S(1)} %get-tuple-element.19.low, f32[2,128]{1,0:T(2,128)S(1)} %get-tuple-element.20.counts, bf16[1536,1024]{1,0:T(8,128)(2,1)S(1)} %copy-done.1, bf16[1536,1024]{1,0:T(8,128)(2,1)S(1)} %collective-permute-done.source.others), custom_call_target="tpu_custom_call" | custom-call | flops 50331648 | bytes 1048576 | tf_op jit(solution)/shard_map/pallas_call | solution.py:187
  49.6 4.0 %collective-permute-done.5.up = bf16[1040,128]{1,0:T(8,128)(2,1)S(1)} collective-permute-done((bf16[1040,128]{1,0:T(8,128)(2,1)S(1)}, bf16[1040,128]{1,0:T(8,128)(2,1)S(1)}, u32[]{:S(2)}, u32[]{:S(2)}) %collective-permute-start.5) | collective-permute-done | bytes 266272 | tf_op jit(solution)/shard_map/ppermute | solution.py:255
  53.5 0.9 %shard_map.58 = bf16[16,80,128]{2,1,0:T(8,128)(2,1)} custom-call(f32[1032,128]{1,0:T(8,128)S(1)} %shard_map.56.own, bf16[1040,128]{1,0:T(8,128)(2,1)S(1)} %collective-permute-done.5.up, bf16[1040,128]{1,0:T(8,128)(2,1)S(1)} %collective-permute-done.6.down, bf16[1040,128]{1,0:T(8,128)(2,1)S(1)} %collective-permute-done.7.deep), custom_call_target="tpu_custom_call" | custom-call | bytes 1048576 | tf_op jit(solution)/shard_map/pallas_call | solution.py:187
  54.4 10.3 %all-to-all-start.1 = ((bf16[16,80,128]{2,1,0:T(8,128)(2,1)}), bf16[16,80,128]{2,1,0:T(8,128)(2,1)S(1)}, u32[]{:S(2)}, u32[]{:S(2)}) async-start(bf16[16,80,128]{2,1,0:T(8,128)(2,1)} %shard_map.58), calls=%async_computation.1 | async-start | bytes 655360 | tf_op jit(solution)/shard_map/all_to_all | solution.py:200
  64.7 0.6 dynamic_slice.6
  66.0 7.2 %all-to-all-done.1.packed = bf16[16,80,128]{2,1,0:T(8,128)(2,1)S(1)} async-done(((bf16[16,80,128]{2,1,0:T(8,128)(2,1)}), bf16[16,80,128]{2,1,0:T(8,128)(2,1)S(1)}, u32[]{:S(2)}, u32[]{:S(2)}) %all-to-all-start.1) | async-done | bytes 327712 | tf_op jit(solution)/shard_map/all_to_all | solution.py:200
  73.2 0.1 shard_map.59.mine
  73.3 0.0 collective-permute-start.8
  73.3 2.8 %collective-permute-done.8.across = f32[9,8,128]{2,1,0:T(8,128)S(1)} collective-permute-done((f32[9,8,128]{2,1,0:T(8,128)S(1)}, f32[9,8,128]{2,1,0:T(8,128)S(1)}, u32[]{:S(2)}, u32[]{:S(2)}) %collective-permute-start.8) | collective-permute-done | bytes 36896 | tf_op jit(solution)/shard_map/ppermute | solution.py:262
  76.2 2.4 %collective-permute-start.9 = (f32[8,1024]{1,0:T(8,128)S(1)}, f32[8,1024]{1,0:T(8,128)S(1)}, u32[]{:S(2)}, u32[]{:S(2)}) collective-permute-start(f32[8,1024]{1,0:T(8,128)S(1)} %shard_map.60.mine), channel_id=1, source_target_pairs={{0,1},{1,0},{2,3},{3,2},{4,5},{5,4},{6,7},{7,6},{8,9},{9,8},{10,11... | collective-permute-start | bytes 98312 | tf_op jit(solution)/shard_map/ppermute | solution.py:270
  78.5 0.6 reduce
  79.1 0.2 collective-permute-done.9.other
  79.4 0.6 shard_map.61
  (15 shorter events, 0.1 us)
Async XLA Ops:
  0.6 29.5 %collective-permute-start = (bf16[1536,1024]{1,0:T(8,128)(2,1)}, bf16[1536,1024]{1,0:T(8,128)(2,1)S(1)}, u32[]{:S(2)}, u32[]{:S(2)}) collective-permute-start(bf16[1536,1024]{1,0:T(8,128)(2,1)} %docs.5), channel_id=1, source_target_pairs={{0,1},{1,0},{2,3},{3,2},{4,5},{5,4},{6,7},{7,6},{8,9},{9,8},{10,11... | collective-permute-start | bytes 9437192 | tf_op jit(solution)/shard_map/ppermute | solution.py:208
  24.0 10.9 %collective-permute-start.3 = (bf16[128,1024]{1,0:T(8,128)(2,1)S(1)}, bf16[128,1024]{1,0:T(8,128)(2,1)S(1)}, u32[]{:S(2)}, u32[]{:S(2)}) collective-permute-start(bf16[128,1024]{1,0:T(8,128)(2,1)S(1)} %bitcast.4), channel_id=1, source_target_pairs={{0,64},{1,65},{2,66},{3,67},{4,68},{5,69},{6,70},{7,71},{8,72},{9,... | collective-permute-start | bytes 786440 | tf_op jit(solution)/shard_map/ppermute | solution.py:212
  24.6 10.3 %collective-permute-start.2 = (bf16[128,1024]{1,0:T(8,128)(2,1)S(1)}, bf16[128,1024]{1,0:T(8,128)(2,1)S(1)}, u32[]{:S(2)}, u32[]{:S(2)}) collective-permute-start(bf16[128,1024]{1,0:T(8,128)(2,1)S(1)} %bitcast.5), channel_id=1, source_target_pairs={{0,192},{1,193},{2,194},{3,195},{4,196},{5,197},{6,198},{7,199},{8... | collective-permute-start | bytes 786440 | tf_op jit(solution)/shard_map/ppermute | solution.py:212
  27.1 6.7 %collective-permute-start.1 = (bf16[128,1024]{1,0:T(8,128)(2,1)S(1)}, bf16[128,1024]{1,0:T(8,128)(2,1)S(1)}, u32[]{:S(2)}, u32[]{:S(2)}) collective-permute-start(bf16[128,1024]{1,0:T(8,128)(2,1)S(1)} %bitcast.6), channel_id=1, source_target_pairs={{0,28},{1,5},{2,30},{3,7},{4,0},{5,9},{6,2},{7,11},{8,4},{9,13},{1... | collective-permute-start | bytes 786440 | tf_op jit(solution)/shard_map/ppermute | solution.py:212
  27.4 1.9 %copy-start = (bf16[1536,1024]{1,0:T(8,128)(2,1)S(1)}, bf16[1536,1024]{1,0:T(8,128)(2,1)}, u32[]{:S(2)}) copy-start(bf16[1536,1024]{1,0:T(8,128)(2,1)} %docs.5) | copy-start | bytes 9437188
  34.9 4.7 %copy-start.1 = (bf16[1536,1024]{1,0:T(8,128)(2,1)S(1)}, bf16[1536,1024]{1,0:T(8,128)(2,1)}, u32[]{:S(2)}) copy-start(bf16[1536,1024]{1,0:T(8,128)(2,1)} %docs.5) | copy-start | bytes 9437188
  36.9 2.7 %collective-permute-start.4 = (f32[4,1536]{1,0:T(4,128)S(1)}, f32[4,1536]{1,0:T(4,128)S(1)}, u32[]{:S(2)}, u32[]{:S(2)}) collective-permute-start(f32[4,1536]{1,0:T(4,128)S(1)} %get-tuple-element.18.mine), channel_id=1, source_target_pairs={{0,1},{1,0},{2,3},{3,2},{4,5},{5,4},{6,7},{7,6},{8,9},{9,8},{10,11... | collective-permute-start | bytes 73736 | tf_op jit(solution)/shard_map/ppermute | solution.py:234
  43.1 6.5 %collective-permute-start.7 = (bf16[1040,128]{1,0:T(8,128)(2,1)S(1)}, bf16[1040,128]{1,0:T(8,128)(2,1)S(1)}, u32[]{:S(2)}, u32[]{:S(2)}) collective-permute-start(bf16[1040,128]{1,0:T(8,128)(2,1)S(1)} %shard_map.57), channel_id=1, source_target_pairs={{0,4},{1,29},{2,6},{3,31},{4,8},{5,1},{6,10},{7,3},{8,12},{9,5},{1... | collective-permute-start | bytes 798728 | tf_op jit(solution)/shard_map/ppermute | solution.py:255
  45.9 7.7 %collective-permute-start.5 = (bf16[1040,128]{1,0:T(8,128)(2,1)S(1)}, bf16[1040,128]{1,0:T(8,128)(2,1)S(1)}, u32[]{:S(2)}, u32[]{:S(2)}) collective-permute-start(bf16[1040,128]{1,0:T(8,128)(2,1)S(1)} %get-tuple-element.21), channel_id=1, source_target_pairs={{0,64},{1,65},{2,66},{3,67},{4,68},{5,69},{6,70},{7,71},{8,72},{9,... | collective-permute-start | bytes 798728 | tf_op jit(solution)/shard_map/ppermute | solution.py:255
  45.9 18.8 %copy-start.3 = (s32[4]{0:T(128)S(1)}, s32[4]{0:T(128)}, u32[]{:S(2)}) copy-start(s32[4]{0:T(128)} %constant.72.clone) | copy-start | bytes 52
  45.9 30.3 %copy-start.2 = (bf16[16,1024]{1,0:T(8,128)(2,1)S(1)}, bf16[16,1024]{1,0:T(8,128)(2,1)}, u32[]{:S(2)}) copy-start(bf16[16,1024]{1,0:T(8,128)(2,1)} %centroids.1) | copy-start | bytes 98308
  45.9 7.7 %collective-permute-start.6 = (bf16[1040,128]{1,0:T(8,128)(2,1)S(1)}, bf16[1040,128]{1,0:T(8,128)(2,1)S(1)}, u32[]{:S(2)}, u32[]{:S(2)}) collective-permute-start(bf16[1040,128]{1,0:T(8,128)(2,1)S(1)} %get-tuple-element.22), channel_id=1, source_target_pairs={{0,192},{1,193},{2,194},{3,195},{4,196},{5,197},{6,198},{7,199},{8... | collective-permute-start | bytes 798728 | tf_op jit(solution)/shard_map/ppermute | solution.py:255
  54.4 18.8 %all-to-all-start.1 = ((bf16[16,80,128]{2,1,0:T(8,128)(2,1)}), bf16[16,80,128]{2,1,0:T(8,128)(2,1)S(1)}, u32[]{:S(2)}, u32[]{:S(2)}) async-start(bf16[16,80,128]{2,1,0:T(8,128)(2,1)} %shard_map.58), calls=%async_computation.1 | async-start | bytes 655360 | tf_op jit(solution)/shard_map/all_to_all | solution.py:200
  73.3 2.8 %collective-permute-start.8 = (f32[9,8,128]{2,1,0:T(8,128)S(1)}, f32[9,8,128]{2,1,0:T(8,128)S(1)}, u32[]{:S(2)}, u32[]{:S(2)}) collective-permute-start(f32[9,8,128]{2,1,0:T(8,128)S(1)} %shard_map.59.mine), channel_id=1, source_target_pairs={{0,2},{1,3},{2,0},{3,1},{4,6},{5,7},{6,4},{7,5},{8,10},{9,11},{10,... | collective-permute-start | bytes 110600 | tf_op jit(solution)/shard_map/ppermute | solution.py:262
  76.2 3.2 %collective-permute-start.9 = (f32[8,1024]{1,0:T(8,128)S(1)}, f32[8,1024]{1,0:T(8,128)S(1)}, u32[]{:S(2)}, u32[]{:S(2)}) collective-permute-start(f32[8,1024]{1,0:T(8,128)S(1)} %shard_map.60.mine), channel_id=1, source_target_pairs={{0,1},{1,0},{2,3},{3,2},{4,5},{5,4},{6,7},{7,6},{8,9},{9,8},{10,11... | collective-permute-start | bytes 98312 | tf_op jit(solution)/shard_map/ppermute | solution.py:270

commit v6 on v5

--- a/solution.py
+++ b/solution.py
@@ -106,7 +106,7 @@
                 out[start + half * 128 : start + half * 128 + 128, :] = part.astype(out.dtype)
 
 
-def weights_kernel(pair, deep, own, mine, theirs, docs, others, normalizer, low, rest, up, down):
+def weights_kernel(pair, deep, own, mine, theirs, docs, others, normalizer, low, rest, up, down, third):
     count = docs.shape[0]
     counts = jnp.zeros((512, 128), jnp.float32)
     for side in range(2):
@@ -126,13 +126,12 @@
             low[:, at] = weights.astype(jnp.bfloat16)
     flat = jnp.sum(counts.T, axis=0, keepdims=True)
     flat = jnp.concatenate([flat[:, i : i + 128] for i in range(0, 512, 128)], axis=0)
-    rest[...] = flat[2:4, :]
-    write_sums(low, docs, others, slice(0, 256), flat, (up, down))
-
-
-def rest_kernel(index, low, counts, docs, others, out):
-    rows = slice(256 + 128 * index, 384 + 128 * index)
-    write_sums(low, docs, others, rows, counts[index : index + 1, :], (out,))
+    rest[...] = flat[3:4, :]
+    write_sums(low, docs, others, slice(0, 384), flat, (up, down, third))
+
+
+def rest_kernel(low, counts, docs, others, own):
+    write_sums(low, docs, others, slice(384, 512), counts, (own,))
 
 
 def star_kernel(own, up, down, deep, packed):
@@ -213,7 +212,7 @@
 
     flops = 2 * 512 * 2 * count * width
     turned = [
-        call(turn_kernel, [((width, count), jnp.bfloat16)], 10, (part,), flops=flops // 2)[0]
+        call(turn_kernel, [((width, count), jnp.bfloat16)], 10, (part,), flops=flops // 64)[0]
         for part in (documents, others)
     ]
     own, up, down, deep = quarters
@@ -233,22 +232,15 @@
     mine = stats[-1]
     theirs = lax.ppermute(mine, "dp", within(1))
     slab = ((1040, 128), jnp.bfloat16)
-    normalizer, low, counts, up, down = call(
+    normalizer, low, counts, up, down, deep = call(
         weights_kernel,
-        [((1, count), jnp.float32), ((512, 2 * count), jnp.bfloat16), ((2, 128), jnp.float32), slab, slab],
+        [((1, count), jnp.float32), ((512, 2 * count), jnp.bfloat16), ((1, 128), jnp.float32), slab, slab, slab],
         24,
         (*logits[::-1], mine, theirs, documents, others),
         flops=flops,
     )
-    (deep,), (own,) = (
-        call(
-            functools.partial(rest_kernel, index),
-            [out],
-            16,
-            (low, counts, documents, others),
-            flops=flops // 64,
-        )
-        for index, out in enumerate((slab, ((1032, 128), jnp.float32)))
+    (own,) = call(
+        rest_kernel, [((1032, 128), jnp.float32)], 16, (low, counts, documents, others), flops=flops // 4
     )
     sent = (up, down, deep)
 

time: 80.3 us -> 78.5 us (0.978)
  waiting for transfers between devices: 16.8 us -> 13.9 us
  starting transfers between devices: 26.7 us -> 28.2 us
    ppermute x3, waiting for transfers between devices: 1.73 us -> 0.01 us  [body(): lax.ppermute(quarter, BOTH, star(side, -1))]
    ppermute x1, starting transfers between devices: 1.88 us -> 3.6 us  [body(): theirs = lax.ppermute(mine, 'dp', within(1))]
    ppermute x3, starting transfers between devices: 5.48 us -> 3.88 us  [body(): lax.ppermute(part, BOTH, star(side, 1))]
    ppermute x1, starting transfers between devices: 2.35 us -> 3.75 us  [body(): other = lax.ppermute(half, 'dp', within(1))]
    all_to_all x1, waiting for transfers between devices: 7.22 us -> 5.82 us  [exchange(): lax.all_to_all(part, BOTH, 0, 0, axis_index_groups=groups, tiled=True)]
    pallas_call x12 -> x11, Pallas kernels: 11.9 us -> 11.5 us  [call(): pl.pallas_call(kernel, out_shape=[jax.ShapeDtypeStruct(shape, dtype) for...]
  transfers between devices with their start and end apart: 11 -> 11, of which waited for: 6 -> 5; matrix products, arithmetic and copies ran while one was open for 2% -> 2% of each run, Pallas kernels for 6% -> 6%
where the time goes in v6:
time: 78.5 us; the launch traced here: 78.2 us
  starting transfers between devices  28.2 us (36%)
  blocking collectives  19.3 us (25%)
  waiting for transfers between devices  13.9 us (18%)
  Pallas kernels  11.5 us (15%)
  local copies, waits for them, and re-layouts  3.23 us (4%)
  between operations  1.41 us (2%)
    all_to_all x1, blocking collectives, exchange(): lax.all_to_all(part, BOTH, 0, 0, axis_index_groups=groups, tiled=True)  19.3 us
    pallas_call x11, Pallas kernels, call(): pl.pallas_call(kernel, out_shape=[jax.ShapeDtypeStruct(shape, dtype) for...  11.5 us
    all_to_all x1, starting transfers between devices, exchange(): lax.all_to_all(part, BOTH, 0, 0, axis_index_groups=groups, tiled=True)  10.3 us
    all_to_all x1, waiting for transfers between devices, exchange(): lax.all_to_all(part, BOTH, 0, 0, axis_index_groups=groups, tiled=True)  5.82 us
    ppermute x3, waiting for transfers between devices, body(): lax.ppermute(part, BOTH, star(side, 1))  4.21 us
    ppermute x3, starting transfers between devices, body(): lax.ppermute(part, BOTH, star(side, 1))  3.88 us
    ppermute x1, starting transfers between devices, body(): other = lax.ppermute(half, 'dp', within(1))  3.75 us
    ppermute x1, starting transfers between devices, body(): theirs = lax.ppermute(mine, 'dp', within(1))  3.6 us
  transfers between devices with their start and end apart: 11, of which 5 were waited for; matrix products, arithmetic and copies ran while one was open for 2% of the time, Pallas kernels for 6%

profile of v6, /device:TPU:1, one launch (start us, length us, event | category | flops | bytes accessed | tf_op | source)
XLA Modules:
  0.0 78.2 jit_solution(1135866458014150415)
XLA Ops:
  0.6 3.3 %collective-permute-start = (bf16[1536,1024]{1,0:T(8,128)(2,1)}, bf16[1536,1024]{1,0:T(8,128)(2,1)S(1)}, u32[]{:S(2)}, u32[]{:S(2)}) collective-permute-start(bf16[1536,1024]{1,0:T(8,128)(2,1)} %docs.3), channel_id=1, source_target_pairs={{0,1},{1,0},{2,3},{3,2},{4,5},{5,4},{6,7},{7,6},{8,9},{9,8},{10,11... | collective-permute-start | bytes 9437192 | tf_op jit(solution)/shard_map/ppermute | solution.py:207
  4.0 0.7 constant_dynamic-slice_fusion
  4.7 19.3 %all_to_all.10 = bf16[16,8,1024]{2,1,0:T(8,128)(2,1)S(1)} all-to-all(bf16[16,8,1024]{2,1,0:T(8,128)(2,1)S(1)} %broadcast_in_dim.2), channel_id=1, replica_groups={{182,148,58,24,190,156,34,0,166,132,42,8,174,140,50,16},{183,149,59,25,..., dimensions={0} | all-to-all | bytes 524288 | tf_op jit(solution)/shard_map/all_to_all | solution.py:199
  24.0 0.3 collective-permute-start.1
  24.3 1.4 %collective-permute-start.3 = (bf16[128,1024]{1,0:T(8,128)(2,1)S(1)}, bf16[128,1024]{1,0:T(8,128)(2,1)S(1)}, u32[]{:S(2)}, u32[]{:S(2)}) collective-permute-start(bf16[128,1024]{1,0:T(8,128)(2,1)S(1)} %bitcast.5), channel_id=1, source_target_pairs={{0,64},{1,65},{2,66},{3,67},{4,68},{5,69},{6,70},{7,71},{8,72},{9,... | collective-permute-start | bytes 786440 | tf_op jit(solution)/shard_map/ppermute | solution.py:211
  25.7 1.7 %collective-permute-start.2 = (bf16[128,1024]{1,0:T(8,128)(2,1)S(1)}, bf16[128,1024]{1,0:T(8,128)(2,1)S(1)}, u32[]{:S(2)}, u32[]{:S(2)}) collective-permute-start(bf16[128,1024]{1,0:T(8,128)(2,1)S(1)} %bitcast.6), channel_id=1, source_target_pairs={{0,192},{1,193},{2,194},{3,195},{4,196},{5,197},{6,198},{7,199},{8... | collective-permute-start | bytes 786440 | tf_op jit(solution)/shard_map/ppermute | solution.py:211
  27.4 1.9 %copy-done = bf16[1536,1024]{1,0:T(8,128)(2,1)S(1)} copy-done((bf16[1536,1024]{1,0:T(8,128)(2,1)S(1)}, bf16[1536,1024]{1,0:T(8,128)(2,1)}, u32[]{:S(2)}) %copy-start) | copy-done | bytes 3145752
  29.2 0.9 %shard_map.50.refs_1_.refs_2_.refs_3_ = bf16[1024,1536]{1,0:T(8,128)(2,1)S(1)} custom-call(bf16[1536,1024]{1,0:T(8,128)(2,1)S(1)} %copy-done), custom_call_target="tpu_custom_call" | custom-call | flops 50331648 | bytes 1048576 | tf_op jit(solution)/shard_map/pallas_call | solution.py:186
  30.1 0.9 %shard_map.51.refs_2_.refs_3_.refs_4_ = bf16[1024,1536]{1,0:T(8,128)(2,1)S(1)} custom-call(bf16[1536,1024]{1,0:T(8,128)(2,1)S(1)} %collective-permute-done.source.others), custom_call_target="tpu_custom_call" | custom-call | flops 50331648 | bytes 1048576 | tf_op jit(solution)/shard_map/pallas_call | solution.py:186
  31.0 1.1 %shard_map.52 = (f32[128,3072]{1,0:T(8,128)S(1)}, f32[4,1536]{1,0:T(4,128)S(1)}) custom-call(bf16[128,1024]{1,0:T(8,128)(2,1)S(1)} %bitcast.7, bf16[1024,1536]{1,0:T(8,128)(2,1)S(1)} %shard_map.50.refs_1_.refs_2_.refs_3_, bf16[1024,1536]{1,0:T(8,128)(2,1)S(1)} %shard_map.51.refs_2_.refs_3_.refs_4_), custom_call_target="tpu_custom_call" | custom-call | flops 100663296 | bytes 1048576 | tf_op jit(solution)/shard_map/pallas_call | solution.py:186
  32.1 1.1 %shard_map.53 = (f32[128,3072]{1,0:T(8,128)S(1)}, f32[4,1536]{1,0:T(4,128)S(1)}) custom-call(f32[4,1536]{1,0:T(4,128)S(1)} %get-tuple-element.14.refs_0_, bf16[128,1024]{1,0:T(8,128)(2,1)S(1)} %collective-permute-done.1.refs_1_, bf16[1024,1536]{1,0:T(8,128)(2,1)S(1)} %shard_map.50.refs_1_.refs_2_.refs_3_, ...), custom_call_target="tpu_custom_call" | custom-call | flops 100663296 | bytes 1048576 | tf_op jit(solution)/shard_map/pallas_call | solution.py:186
  33.2 0.0 copy-start.1
  33.2 2.0 %shard_map.54 = (f32[256,3072]{1,0:T(8,128)S(1)}, f32[4,1536]{1,0:T(4,128)S(1)}) custom-call(f32[4,1536]{1,0:T(4,128)S(1)} %get-tuple-element.15.refs_0_, bf16[128,1024]{1,0:T(8,128)(2,1)S(1)} %collective-permute-done.2.refs_1_, bf16[128,1024]{1,0:T(8,128)(2,1)S(1)} %collective-permute-done.3.refs_2_, ...), custom_call_target="tpu_custom_call" | custom-call | flops 201326592 | bytes 1048576 | tf_op jit(solution)/shard_map/pallas_call | solution.py:186
  35.2 3.6 %collective-permute-start.4 = (f32[4,1536]{1,0:T(4,128)S(1)}, f32[4,1536]{1,0:T(4,128)S(1)}, u32[]{:S(2)}, u32[]{:S(2)}) collective-permute-start(f32[4,1536]{1,0:T(4,128)S(1)} %get-tuple-element.19.mine), channel_id=1, source_target_pairs={{0,1},{1,0},{2,3},{3,2},{4,5},{5,4},{6,7},{7,6},{8,9},{9,8},{10,11... | collective-permute-start | bytes 73736 | tf_op jit(solution)/shard_map/ppermute | solution.py:233
  38.8 0.8 %collective-permute-done.4.theirs = f32[4,1536]{1,0:T(4,128)S(1)} collective-permute-done((f32[4,1536]{1,0:T(4,128)S(1)}, f32[4,1536]{1,0:T(4,128)S(1)}, u32[]{:S(2)}, u32[]{:S(2)}) %collective-permute-start.4) | collective-permute-done | bytes 24608 | tf_op jit(solution)/shard_map/ppermute | solution.py:233
  39.7 2.9 %shard_map.55 = (f32[1,1536]{1,0:T(1,128)S(1)}, bf16[512,3072]{1,0:T(8,128)(2,1)S(1)}, f32[1,128]{1,0:T(1,128)S(1)}, bf16[1040,128]{1,0:T(8,128)(2,1)S(1)}, bf16...) custom-call(f32[256,3072]{1,0:T(8,128)S(1)} %get-tuple-element.16.pair, f32[128,3072]{1,0:T(8,128)S(1)} %get-tuple-element.17.deep, ...), custom_call_target="tpu_custom_call" | custom-call | flops 3221225472 | bytes 1048576 | tf_op jit(solution)/shard_map/pallas_call | solution.py:186
  42.6 0.3 collective-permute-start.5
  42.9 2.7 %collective-permute-start.6 = (bf16[1040,128]{1,0:T(8,128)(2,1)S(1)}, bf16[1040,128]{1,0:T(8,128)(2,1)S(1)}, u32[]{:S(2)}, u32[]{:S(2)}) collective-permute-start(bf16[1040,128]{1,0:T(8,128)(2,1)S(1)} %get-tuple-element.23), channel_id=1, source_target_pairs={{0,192},{1,193},{2,194},{3,195},{4,196},{5,197},{6,198},{7,199},{8... | collective-permute-start | bytes 798728 | tf_op jit(solution)/shard_map/ppermute | solution.py:247
  45.5 1.0 %collective-permute-start.7 = (bf16[1040,128]{1,0:T(8,128)(2,1)S(1)}, bf16[1040,128]{1,0:T(8,128)(2,1)S(1)}, u32[]{:S(2)}, u32[]{:S(2)}) collective-permute-start(bf16[1040,128]{1,0:T(8,128)(2,1)S(1)} %get-tuple-element.24), channel_id=1, source_target_pairs={{0,4},{1,29},{2,6},{3,31},{4,8},{5,1},{6,10},{7,3},{8,12},{9,5},{1... | collective-permute-start | bytes 798728 | tf_op jit(solution)/shard_map/ppermute | solution.py:247
  46.5 1.0 %shard_map.56.own = f32[1032,128]{1,0:T(8,128)S(1)} custom-call(bf16[512,3072]{1,0:T(8,128)(2,1)S(1)} %get-tuple-element.20.low, f32[1,128]{1,0:T(1,128)S(1)} %get-tuple-element.21.counts, bf16[1536,1024]{1,0:T(8,128)(2,1)S(1)} %copy-done.1, bf16[1536,1024]{1,0:T(8,128)(2,1)S(1)} %collective-permute-done.source.others), custom_call_target="tpu_custom_call" | custom-call | flops 805306368 | bytes 1048576 | tf_op jit(solution)/shard_map/pallas_call | solution.py:186
  47.5 4.2 %collective-permute-done.5.up = bf16[1040,128]{1,0:T(8,128)(2,1)S(1)} collective-permute-done((bf16[1040,128]{1,0:T(8,128)(2,1)S(1)}, bf16[1040,128]{1,0:T(8,128)(2,1)S(1)}, u32[]{:S(2)}, u32[]{:S(2)}) %collective-permute-start.5) | collective-permute-done | bytes 266272 | tf_op jit(solution)/shard_map/ppermute | solution.py:247
  51.7 0.9 %shard_map.57 = bf16[16,80,128]{2,1,0:T(8,128)(2,1)} custom-call(f32[1032,128]{1,0:T(8,128)S(1)} %shard_map.56.own, bf16[1040,128]{1,0:T(8,128)(2,1)S(1)} %collective-permute-done.5.up, bf16[1040,128]{1,0:T(8,128)(2,1)S(1)} %collective-permute-done.6.down, bf16[1040,128]{1,0:T(8,128)(2,1)S(1)} %collective-permute-done.7.deep), custom_call_target="tpu_custom_call" | custom-call | bytes 1048576 | tf_op jit(solution)/shard_map/pallas_call | solution.py:186
  52.6 10.3 %all-to-all-start.1 = ((bf16[16,80,128]{2,1,0:T(8,128)(2,1)}), bf16[16,80,128]{2,1,0:T(8,128)(2,1)S(1)}, u32[]{:S(2)}, u32[]{:S(2)}) async-start(bf16[16,80,128]{2,1,0:T(8,128)(2,1)} %shard_map.57), calls=%async_computation.1 | async-start | bytes 655360 | tf_op jit(solution)/shard_map/all_to_all | solution.py:199
  62.9 0.6 dynamic_slice.6
  64.1 5.8 %all-to-all-done.1.packed = bf16[16,80,128]{2,1,0:T(8,128)(2,1)S(1)} async-done(((bf16[16,80,128]{2,1,0:T(8,128)(2,1)}), bf16[16,80,128]{2,1,0:T(8,128)(2,1)S(1)}, u32[]{:S(2)}, u32[]{:S(2)}) %all-to-all-start.1) | async-done | bytes 327712 | tf_op jit(solution)/shard_map/all_to_all | solution.py:199
  70.0 0.1 shard_map.58.mine
  70.1 0.0 collective-permute-start.8
  70.1 2.8 %collective-permute-done.8.across = f32[9,8,128]{2,1,0:T(8,128)S(1)} collective-permute-done((f32[9,8,128]{2,1,0:T(8,128)S(1)}, f32[9,8,128]{2,1,0:T(8,128)S(1)}, u32[]{:S(2)}, u32[]{:S(2)}) %collective-permute-start.8) | collective-permute-done | bytes 36896 | tf_op jit(solution)/shard_map/ppermute | solution.py:254
  72.9 3.8 %collective-permute-start.9 = (f32[8,1024]{1,0:T(8,128)S(1)}, f32[8,1024]{1,0:T(8,128)S(1)}, u32[]{:S(2)}, u32[]{:S(2)}) collective-permute-start(f32[8,1024]{1,0:T(8,128)S(1)} %shard_map.59.mine), channel_id=1, source_target_pairs={{0,1},{1,0},{2,3},{3,2},{4,5},{5,4},{6,7},{7,6},{8,9},{9,8},{10,11... | collective-permute-start | bytes 98312 | tf_op jit(solution)/shard_map/ppermute | solution.py:262
  76.7 0.6 reduce
  77.3 0.2 collective-permute-done.9.other
  77.6 0.6 shard_map.60
  (14 shorter events, 0.1 us)
Async XLA Ops:
  0.6 29.5 %collective-permute-start = (bf16[1536,1024]{1,0:T(8,128)(2,1)}, bf16[1536,1024]{1,0:T(8,128)(2,1)S(1)}, u32[]{:S(2)}, u32[]{:S(2)}) collective-permute-start(bf16[1536,1024]{1,0:T(8,128)(2,1)} %docs.3), channel_id=1, source_target_pairs={{0,1},{1,0},{2,3},{3,2},{4,5},{5,4},{6,7},{7,6},{8,9},{9,8},{10,11... | collective-permute-start | bytes 9437192 | tf_op jit(solution)/shard_map/ppermute | solution.py:207
  24.0 8.1 %collective-permute-start.1 = (bf16[128,1024]{1,0:T(8,128)(2,1)S(1)}, bf16[128,1024]{1,0:T(8,128)(2,1)S(1)}, u32[]{:S(2)}, u32[]{:S(2)}) collective-permute-start(bf16[128,1024]{1,0:T(8,128)(2,1)S(1)} %bitcast.4), channel_id=1, source_target_pairs={{0,28},{1,5},{2,30},{3,7},{4,0},{5,9},{6,2},{7,11},{8,4},{9,13},{1... | collective-permute-start | bytes 786440 | tf_op jit(solution)/shard_map/ppermute | solution.py:211
  24.3 8.9 %collective-permute-start.3 = (bf16[128,1024]{1,0:T(8,128)(2,1)S(1)}, bf16[128,1024]{1,0:T(8,128)(2,1)S(1)}, u32[]{:S(2)}, u32[]{:S(2)}) collective-permute-start(bf16[128,1024]{1,0:T(8,128)(2,1)S(1)} %bitcast.5), channel_id=1, source_target_pairs={{0,64},{1,65},{2,66},{3,67},{4,68},{5,69},{6,70},{7,71},{8,72},{9,... | collective-permute-start | bytes 786440 | tf_op jit(solution)/shard_map/ppermute | solution.py:211
  25.7 7.5 %collective-permute-start.2 = (bf16[128,1024]{1,0:T(8,128)(2,1)S(1)}, bf16[128,1024]{1,0:T(8,128)(2,1)S(1)}, u32[]{:S(2)}, u32[]{:S(2)}) collective-permute-start(bf16[128,1024]{1,0:T(8,128)(2,1)S(1)} %bitcast.6), channel_id=1, source_target_pairs={{0,192},{1,193},{2,194},{3,195},{4,196},{5,197},{6,198},{7,199},{8... | collective-permute-start | bytes 786440 | tf_op jit(solution)/shard_map/ppermute | solution.py:211
  27.4 1.9 %copy-start = (bf16[1536,1024]{1,0:T(8,128)(2,1)S(1)}, bf16[1536,1024]{1,0:T(8,128)(2,1)}, u32[]{:S(2)}) copy-start(bf16[1536,1024]{1,0:T(8,128)(2,1)} %docs.3) | copy-start | bytes 9437188
  33.2 6.5 %copy-start.1 = (bf16[1536,1024]{1,0:T(8,128)(2,1)S(1)}, bf16[1536,1024]{1,0:T(8,128)(2,1)}, u32[]{:S(2)}) copy-start(bf16[1536,1024]{1,0:T(8,128)(2,1)} %docs.3) | copy-start | bytes 9437188
  35.2 4.4 %collective-permute-start.4 = (f32[4,1536]{1,0:T(4,128)S(1)}, f32[4,1536]{1,0:T(4,128)S(1)}, u32[]{:S(2)}, u32[]{:S(2)}) collective-permute-start(f32[4,1536]{1,0:T(4,128)S(1)} %get-tuple-element.19.mine), channel_id=1, source_target_pairs={{0,1},{1,0},{2,3},{3,2},{4,5},{5,4},{6,7},{7,6},{8,9},{9,8},{10,11... | collective-permute-start | bytes 73736 | tf_op jit(solution)/shard_map/ppermute | solution.py:233
  42.6 9.1 %collective-permute-start.5 = (bf16[1040,128]{1,0:T(8,128)(2,1)S(1)}, bf16[1040,128]{1,0:T(8,128)(2,1)S(1)}, u32[]{:S(2)}, u32[]{:S(2)}) collective-permute-start(bf16[1040,128]{1,0:T(8,128)(2,1)S(1)} %get-tuple-element.22), channel_id=1, source_target_pairs={{0,64},{1,65},{2,66},{3,67},{4,68},{5,69},{6,70},{7,71},{8,72},{9,... | collective-permute-start | bytes 798728 | tf_op jit(solution)/shard_map/ppermute | solution.py:247
  42.9 8.8 %collective-permute-start.6 = (bf16[1040,128]{1,0:T(8,128)(2,1)S(1)}, bf16[1040,128]{1,0:T(8,128)(2,1)S(1)}, u32[]{:S(2)}, u32[]{:S(2)}) collective-permute-start(bf16[1040,128]{1,0:T(8,128)(2,1)S(1)} %get-tuple-element.23), channel_id=1, source_target_pairs={{0,192},{1,193},{2,194},{3,195},{4,196},{5,197},{6,198},{7,199},{8... | collective-permute-start | bytes 798728 | tf_op jit(solution)/shard_map/ppermute | solution.py:247
  45.5 6.2 %collective-permute-start.7 = (bf16[1040,128]{1,0:T(8,128)(2,1)S(1)}, bf16[1040,128]{1,0:T(8,128)(2,1)S(1)}, u32[]{:S(2)}, u32[]{:S(2)}) collective-permute-start(bf16[1040,128]{1,0:T(8,128)(2,1)S(1)} %get-tuple-element.24), channel_id=1, source_target_pairs={{0,4},{1,29},{2,6},{3,31},{4,8},{5,1},{6,10},{7,3},{8,12},{9,5},{1... | collective-permute-start | bytes 798728 | tf_op jit(solution)/shard_map/ppermute | solution.py:247
  46.5 16.4 %copy-start.3 = (s32[4]{0:T(128)S(1)}, s32[4]{0:T(128)}, u32[]{:S(2)}) copy-start(s32[4]{0:T(128)} %constant.72.clone) | copy-start | bytes 52
  46.5 26.4 %copy-start.2 = (bf16[16,1024]{1,0:T(8,128)(2,1)S(1)}, bf16[16,1024]{1,0:T(8,128)(2,1)}, u32[]{:S(2)}) copy-start(bf16[16,1024]{1,0:T(8,128)(2,1)} %centroids.1) | copy-start | bytes 98308
  52.6 17.4 %all-to-all-start.1 = ((bf16[16,80,128]{2,1,0:T(8,128)(2,1)}), bf16[16,80,128]{2,1,0:T(8,128)(2,1)S(1)}, u32[]{:S(2)}, u32[]{:S(2)}) async-start(bf16[16,80,128]{2,1,0:T(8,128)(2,1)} %shard_map.57), calls=%async_computation.1 | async-start | bytes 655360 | tf_op jit(solution)/shard_map/all_to_all | solution.py:199
  70.1 2.8 %collective-permute-start.8 = (f32[9,8,128]{2,1,0:T(8,128)S(1)}, f32[9,8,128]{2,1,0:T(8,128)S(1)}, u32[]{:S(2)}, u32[]{:S(2)}) collective-permute-start(f32[9,8,128]{2,1,0:T(8,128)S(1)} %shard_map.58.mine), channel_id=1, source_target_pairs={{0,2},{1,3},{2,0},{3,1},{4,6},{5,7},{6,4},{7,5},{8,10},{9,11},{10,... | collective-permute-start | bytes 110600 | tf_op jit(solution)/shard_map/ppermute | solution.py:254
  72.9 4.6 %collective-permute-start.9 = (f32[8,1024]{1,0:T(8,128)S(1)}, f32[8,1024]{1,0:T(8,128)S(1)}, u32[]{:S(2)}, u32[]{:S(2)}) collective-permute-start(f32[8,1024]{1,0:T(8,128)S(1)} %shard_map.59.mine), channel_id=1, source_target_pairs={{0,1},{1,0},{2,3},{3,2},{4,5},{5,4},{6,7},{7,6},{8,9},{9,8},{10,11... | collective-permute-start | bytes 98312 | tf_op jit(solution)/shard_map/ppermute | solution.py:262

commit v7 on v6

--- a/solution.py
+++ b/solution.py
@@ -23,8 +23,6 @@
     for core in range(2)
 ]
 
-TURN = 0
-
 
 def star(side, sign):
     found = []
@@ -41,14 +39,6 @@
 
 def within(bits):
     return [(i, i ^ bits) for i in range(4)]
-
-
-def repeat_kernel(core, centroids, out):
-    whole = centroids[...].astype(jnp.float32)
-    half = jnp.where(core[0] == 0, whole[:8, :], whole[8:, :])
-    twice = jnp.concatenate([half, half], axis=0).astype(jnp.bfloat16)
-    for start in range(0, 128, 16):
-        out[start : start + 16, :] = twice
 
 
 def turn_kernel(source, out):
@@ -88,7 +78,7 @@
     return jnp.concatenate([high, rest, jnp.zeros((14, 128), jnp.bfloat16)], axis=0)
 
 
-def write_sums(low, docs, others, rows, counts, outs):
+def write_sums(low, docs, others, counts, outs):
     count = docs.shape[0]
     for i, out in enumerate(outs):
         row = counts[i : i + 1, :]
@@ -98,40 +88,43 @@
             out[1024:1040, :] = two_rows(row)
     for start in range(0, docs.shape[1], 256):
         columns = slice(start, start + 256)
-        sums = jnp.dot(low[rows, :count], docs[:, columns], preferred_element_type=jnp.float32)
-        sums += jnp.dot(low[rows, count:], others[:, columns], preferred_element_type=jnp.float32)
+        sums = jnp.dot(low[:, :count], docs[:, columns], preferred_element_type=jnp.float32)
+        sums += jnp.dot(low[:, count:], others[:, columns], preferred_element_type=jnp.float32)
         for i, out in enumerate(outs):
             for half in range(2):
                 part = sums[i * 128 : i * 128 + 128, half * 128 : half * 128 + 128]
                 out[start + half * 128 : start + half * 128 + 128, :] = part.astype(out.dtype)
 
 
-def weights_kernel(pair, deep, own, mine, theirs, docs, others, normalizer, low, rest, up, down, third):
-    count = docs.shape[0]
-    counts = jnp.zeros((512, 128), jnp.float32)
+def weigh(logits, norms, low):
+    count = norms.shape[1]
+    counts = jnp.zeros((low.shape[0], 128), jnp.float32)
+    for side in range(2):
+        for start in range(0, count, TILE):
+            at = slice(side * count + start, side * count + start + TILE)
+            part = jnp.concatenate([ref[:, at] for ref in logits], axis=0)
+            weights = jnp.exp(part - norms[side : side + 1, start : start + TILE])
+            for k in range(0, TILE, 128):
+                counts += weights[:, k : k + 128]
+            low[:, at] = weights.astype(jnp.bfloat16)
+    flat = jnp.sum(counts.T, axis=0, keepdims=True)
+    return jnp.concatenate([flat[:, i : i + 128] for i in range(0, flat.shape[1], 128)], axis=0)
+
+
+def sent_kernel(pair, deep, mine, theirs, docs, others, normalizer, norms, *refs):
+    *outs, low = refs
     for side in range(2):
         a, b = mine[side : side + 1, :], theirs[1 - side : 2 - side, :]
         top = jnp.maximum(a, b)
         total = mine[2 + side : 3 + side, :] * jnp.exp(a - top)
         total += theirs[3 - side : 4 - side, :] * jnp.exp(b - top)
-        norm = top + jnp.log(total)
-        if side == 0:
-            normalizer[...] = norm
-        for start in range(0, count, TILE):
-            at = slice(side * count + start, side * count + start + TILE)
-            logits = jnp.concatenate([pair[:, at], deep[:, at], own[:, at]], axis=0)
-            weights = jnp.exp(logits - norm[:, start : start + TILE])
-            for k in range(0, TILE, 128):
-                counts += weights[:, k : k + 128]
-            low[:, at] = weights.astype(jnp.bfloat16)
-    flat = jnp.sum(counts.T, axis=0, keepdims=True)
-    flat = jnp.concatenate([flat[:, i : i + 128] for i in range(0, 512, 128)], axis=0)
-    rest[...] = flat[3:4, :]
-    write_sums(low, docs, others, slice(0, 384), flat, (up, down, third))
-
-
-def rest_kernel(low, counts, docs, others, own):
-    write_sums(low, docs, others, slice(384, 512), counts, (own,))
+        norms[side : side + 1, :] = top + jnp.log(total)
+    normalizer[...] = norms[0:1, :]
+    write_sums(low, docs, others, weigh((pair, deep), norms, low), outs)
+
+
+def own_kernel(own, norms, docs, others, out, low):
+    write_sums(low, docs, others, weigh((own,), norms, low), (out,))
 
 
 def star_kernel(own, up, down, deep, packed):
@@ -144,8 +137,7 @@
         rows = slice(tile * 128, tile * 128 + 128)
         left = own[rows, :] + up[rows, :].astype(jnp.float32)
         right = down[rows, :].astype(jnp.float32) + deep[rows, :].astype(jnp.float32)
-        result = (left + right).reshape(16, 8, 128)
-        return jnp.concatenate([result[TURN:], result[:TURN]], axis=0) if TURN else result
+        return (left + right).reshape(16, 8, 128)
 
     for tile in range(0, 8, 2):
         pair = jnp.concatenate([total(tile), total(tile + 1)], axis=1)
@@ -194,9 +186,8 @@
     )(*operands)
 
 
-def exchange(part, turn=0):
-    groups = [group[turn:] + group[:turn] for group in GROUPS]
-    return lax.all_to_all(part, BOTH, 0, 0, axis_index_groups=groups, tiled=True)
+def exchange(part):
+    return lax.all_to_all(part, BOTH, 0, 0, axis_index_groups=GROUPS, tiled=True)
 
 
 def body(documents, centroids):
@@ -232,15 +223,21 @@
     mine = stats[-1]
     theirs = lax.ppermute(mine, "dp", within(1))
     slab = ((1040, 128), jnp.bfloat16)
-    normalizer, low, counts, up, down, deep = call(
-        weights_kernel,
-        [((1, count), jnp.float32), ((512, 2 * count), jnp.bfloat16), ((1, 128), jnp.float32), slab, slab, slab],
+    normalizer, norms, up, down, deep = call(
+        sent_kernel,
+        [((1, count), jnp.float32), ((2, count), jnp.float32), slab, slab, slab],
         24,
-        (*logits[::-1], mine, theirs, documents, others),
+        (logits[2], logits[1], mine, theirs, documents, others),
+        scratch=[pltpu.VMEM((384, 2 * count), jnp.bfloat16)],
         flops=flops,
     )
     (own,) = call(
-        rest_kernel, [((1032, 128), jnp.float32)], 16, (low, counts, documents, others), flops=flops // 4
+        own_kernel,
+        [((1032, 128), jnp.float32)],
+        16,
+        (logits[0], norms, documents, others),
+        scratch=[pltpu.VMEM((128, 2 * count), jnp.bfloat16)],
+        flops=flops // 4,
     )
     sent = (up, down, deep)
 
@@ -249,7 +246,7 @@
     label = (blk // 16 + 2 * blk) % 4
     place = (blk - jnp.asarray(FIRST)[label]) % 8 * 2 + 1 - blk // 8 % 2
     (part,) = call(
-        group_kernel, [((9, 8, 128), jnp.float32)], 4, (place.reshape(1), exchange(packed, TURN)), scalars=1
+        group_kernel, [((9, 8, 128), jnp.float32)], 4, (place.reshape(1), exchange(packed)), scalars=1
     )
     across = lax.ppermute(part, "dp", within(2))
     (half,) = call(

time: 78.5 us -> 78 us (level)
  transfers between devices with their start and end apart: 11 -> 11, of which waited for: 5 -> 5; matrix products, arithmetic and copies ran while one was open for 2% -> 3% of each run, Pallas kernels for 6% -> 6%
where the time goes in v7:
time: 78 us; the launch traced here: 77.7 us
  starting transfers between devices  28.4 us (36%)
  blocking collectives  19.3 us (25%)
  waiting for transfers between devices  13.5 us (17%)
  Pallas kernels  11.2 us (14%)
  local copies, waits for them, and re-layouts  3.23 us (4%)
  between operations  1.41 us (2%)
    all_to_all x1, blocking collectives, exchange(): lax.all_to_all(part, BOTH, 0, 0, axis_index_groups=GROUPS, tiled=True)  19.3 us
    pallas_call x11, Pallas kernels, call(): pl.pallas_call(kernel, out_shape=[jax.ShapeDtypeStruct(shape, dtype) for...  11.2 us
    all_to_all x1, starting transfers between devices, exchange(): lax.all_to_all(part, BOTH, 0, 0, axis_index_groups=GROUPS, tiled=True)  10.3 us
    all_to_all x1, waiting for transfers between devices, exchange(): lax.all_to_all(part, BOTH, 0, 0, axis_index_groups=GROUPS, tiled=True)  5.43 us
    ppermute x3, waiting for transfers between devices, body(): lax.ppermute(part, BOTH, star(side, 1))  4.19 us
    ppermute x1, starting transfers between devices, body(): other = lax.ppermute(half, 'dp', within(1))  4.14 us
    ppermute x3, starting transfers between devices, body(): lax.ppermute(part, BOTH, star(side, 1))  3.7 us
    ppermute x1, starting transfers between devices, body(): theirs = lax.ppermute(mine, 'dp', within(1))  3.6 us
  transfers between devices with their start and end apart: 11, of which 5 were waited for; matrix products, arithmetic and copies ran while one was open for 3% of the time, Pallas kernels for 6%

profile of v7, /device:TPU:1, one launch (start us, length us, event | category | flops | bytes accessed | tf_op | source)
XLA Modules:
  0.0 77.7 jit_solution(6440470966316331347)
XLA Ops:
  0.6 3.3 %collective-permute-start = (bf16[1536,1024]{1,0:T(8,128)(2,1)}, bf16[1536,1024]{1,0:T(8,128)(2,1)S(1)}, u32[]{:S(2)}, u32[]{:S(2)}) collective-permute-start(bf16[1536,1024]{1,0:T(8,128)(2,1)} %docs.3), channel_id=1, source_target_pairs={{0,1},{1,0},{2,3},{3,2},{4,5},{5,4},{6,7},{7,6},{8,9},{9,8},{10,11... | collective-permute-start | bytes 9437192 | tf_op jit(solution)/shard_map/ppermute | solution.py:198
  4.0 0.7 constant_dynamic-slice_fusion
  4.7 19.3 %all_to_all.10 = bf16[16,8,1024]{2,1,0:T(8,128)(2,1)S(1)} all-to-all(bf16[16,8,1024]{2,1,0:T(8,128)(2,1)S(1)} %broadcast_in_dim.2), channel_id=1, replica_groups={{182,148,58,24,190,156,34,0,166,132,42,8,174,140,50,16},{183,149,59,25,..., dimensions={0} | all-to-all | bytes 524288 | tf_op jit(solution)/shard_map/all_to_all | solution.py:190
  24.0 0.3 collective-permute-start.1
  24.3 1.4 %collective-permute-start.3 = (bf16[128,1024]{1,0:T(8,128)(2,1)S(1)}, bf16[128,1024]{1,0:T(8,128)(2,1)S(1)}, u32[]{:S(2)}, u32[]{:S(2)}) collective-permute-start(bf16[128,1024]{1,0:T(8,128)(2,1)S(1)} %bitcast.5), channel_id=1, source_target_pairs={{0,64},{1,65},{2,66},{3,67},{4,68},{5,69},{6,70},{7,71},{8,72},{9,... | collective-permute-start | bytes 786440 | tf_op jit(solution)/shard_map/ppermute | solution.py:202
  25.7 1.7 %collective-permute-start.2 = (bf16[128,1024]{1,0:T(8,128)(2,1)S(1)}, bf16[128,1024]{1,0:T(8,128)(2,1)S(1)}, u32[]{:S(2)}, u32[]{:S(2)}) collective-permute-start(bf16[128,1024]{1,0:T(8,128)(2,1)S(1)} %bitcast.6), channel_id=1, source_target_pairs={{0,192},{1,193},{2,194},{3,195},{4,196},{5,197},{6,198},{7,199},{8... | collective-permute-start | bytes 786440 | tf_op jit(solution)/shard_map/ppermute | solution.py:202
  27.4 1.9 %copy-done = bf16[1536,1024]{1,0:T(8,128)(2,1)S(1)} copy-done((bf16[1536,1024]{1,0:T(8,128)(2,1)S(1)}, bf16[1536,1024]{1,0:T(8,128)(2,1)}, u32[]{:S(2)}) %copy-start) | copy-done | bytes 3145752
  29.2 0.9 %shard_map.50.refs_1_.refs_2_.refs_3_ = bf16[1024,1536]{1,0:T(8,128)(2,1)S(1)} custom-call(bf16[1536,1024]{1,0:T(8,128)(2,1)S(1)} %copy-done), custom_call_target="tpu_custom_call" | custom-call | flops 50331648 | bytes 1048576 | tf_op jit(solution)/shard_map/pallas_call | solution.py:178
  30.1 0.9 %shard_map.51.refs_2_.refs_3_.refs_4_ = bf16[1024,1536]{1,0:T(8,128)(2,1)S(1)} custom-call(bf16[1536,1024]{1,0:T(8,128)(2,1)S(1)} %collective-permute-done.source.others), custom_call_target="tpu_custom_call" | custom-call | flops 50331648 | bytes 1048576 | tf_op jit(solution)/shard_map/pallas_call | solution.py:178
  31.0 1.1 %shard_map.52 = (f32[128,3072]{1,0:T(8,128)S(1)}, f32[4,1536]{1,0:T(4,128)S(1)}) custom-call(bf16[128,1024]{1,0:T(8,128)(2,1)S(1)} %bitcast.7, bf16[1024,1536]{1,0:T(8,128)(2,1)S(1)} %shard_map.50.refs_1_.refs_2_.refs_3_, bf16[1024,1536]{1,0:T(8,128)(2,1)S(1)} %shard_map.51.refs_2_.refs_3_.refs_4_), custom_call_target="tpu_custom_call" | custom-call | flops 100663296 | bytes 1048576 | tf_op jit(solution)/shard_map/pallas_call | solution.py:178
  32.1 1.1 %shard_map.53 = (f32[128,3072]{1,0:T(8,128)S(1)}, f32[4,1536]{1,0:T(4,128)S(1)}) custom-call(f32[4,1536]{1,0:T(4,128)S(1)} %get-tuple-element.14.refs_0_, bf16[128,1024]{1,0:T(8,128)(2,1)S(1)} %collective-permute-done.1.refs_1_, bf16[1024,1536]{1,0:T(8,128)(2,1)S(1)} %shard_map.50.refs_1_.refs_2_.refs_3_, ...), custom_call_target="tpu_custom_call" | custom-call | flops 100663296 | bytes 1048576 | tf_op jit(solution)/shard_map/pallas_call | solution.py:178
  33.2 0.0 copy-start.1
  33.2 2.0 %shard_map.54 = (f32[256,3072]{1,0:T(8,128)S(1)}, f32[4,1536]{1,0:T(4,128)S(1)}) custom-call(f32[4,1536]{1,0:T(4,128)S(1)} %get-tuple-element.15.refs_0_, bf16[128,1024]{1,0:T(8,128)(2,1)S(1)} %collective-permute-done.2.refs_1_, bf16[128,1024]{1,0:T(8,128)(2,1)S(1)} %collective-permute-done.3.refs_2_, ...), custom_call_target="tpu_custom_call" | custom-call | flops 201326592 | bytes 1048576 | tf_op jit(solution)/shard_map/pallas_call | solution.py:178
  35.2 3.6 %collective-permute-start.4 = (f32[4,1536]{1,0:T(4,128)S(1)}, f32[4,1536]{1,0:T(4,128)S(1)}, u32[]{:S(2)}, u32[]{:S(2)}) collective-permute-start(f32[4,1536]{1,0:T(4,128)S(1)} %get-tuple-element.18.mine), channel_id=1, source_target_pairs={{0,1},{1,0},{2,3},{3,2},{4,5},{5,4},{6,7},{7,6},{8,9},{9,8},{10,11... | collective-permute-start | bytes 73736 | tf_op jit(solution)/shard_map/ppermute | solution.py:224
  38.8 0.8 %collective-permute-done.4.theirs = f32[4,1536]{1,0:T(4,128)S(1)} collective-permute-done((f32[4,1536]{1,0:T(4,128)S(1)}, f32[4,1536]{1,0:T(4,128)S(1)}, u32[]{:S(2)}, u32[]{:S(2)}) %collective-permute-start.4) | collective-permute-done | bytes 24608 | tf_op jit(solution)/shard_map/ppermute | solution.py:224
  39.7 2.7 %shard_map.55 = (f32[1,1536]{1,0:T(1,128)S(1)}, f32[2,1536]{1,0:T(2,128)S(1)}, bf16[1040,128]{1,0:T(8,128)(2,1)S(1)}, bf16[1040,128]{1,0:T(8,128)(2,1)S(1)}, bf16[1040,128]{1,0:T(8,128)(2,1)S(1)}) custom-call(f32[256,3072]{1,0:T(8,128)S(1)} %get-tuple-element.16.pair, f32[128,3072]{1,0:T(8,128)S(1)} %get-tuple-element.17.deep, ...), custom_call_target="tpu_custom_call" | custom-call | flops 3221225472 | bytes 1048576 | tf_op jit(solution)/shard_map/pallas_call | solution.py:178
  42.3 0.1 collective-permute-start.5
  42.4 2.7 %collective-permute-start.6 = (bf16[1040,128]{1,0:T(8,128)(2,1)S(1)}, bf16[1040,128]{1,0:T(8,128)(2,1)S(1)}, u32[]{:S(2)}, u32[]{:S(2)}) collective-permute-start(bf16[1040,128]{1,0:T(8,128)(2,1)S(1)} %get-tuple-element.21), channel_id=1, source_target_pairs={{0,192},{1,193},{2,194},{3,195},{4,196},{5,197},{6,198},{7,199},{8... | collective-permute-start | bytes 798728 | tf_op jit(solution)/shard_map/ppermute | solution.py:244
  45.1 0.9 %collective-permute-start.7 = (bf16[1040,128]{1,0:T(8,128)(2,1)S(1)}, bf16[1040,128]{1,0:T(8,128)(2,1)S(1)}, u32[]{:S(2)}, u32[]{:S(2)}) collective-permute-start(bf16[1040,128]{1,0:T(8,128)(2,1)S(1)} %get-tuple-element.22), channel_id=1, source_target_pairs={{0,4},{1,29},{2,6},{3,31},{4,8},{5,1},{6,10},{7,3},{8,12},{9,5},{1... | collective-permute-start | bytes 798728 | tf_op jit(solution)/shard_map/ppermute | solution.py:244
  46.0 1.0 %shard_map.56.own = f32[1032,128]{1,0:T(8,128)S(1)} custom-call(f32[128,3072]{1,0:T(8,128)S(1)} %get-tuple-element.13.own, f32[2,1536]{1,0:T(2,128)S(1)} %get-tuple-element.19.norms, bf16[1536,1024]{1,0:T(8,128)(2,1)S(1)} %copy-done.1, bf16[1536,1024]{1,0:T(8,128)(2,1)S(1)} %collective-permute-done.source.others), custom_call_target="tpu_custom_call" | custom-call | flops 805306368 | bytes 1048576 | tf_op jit(solution)/shard_map/pallas_call | solution.py:178
  47.1 4.2 %collective-permute-done.5.up = bf16[1040,128]{1,0:T(8,128)(2,1)S(1)} collective-permute-done((bf16[1040,128]{1,0:T(8,128)(2,1)S(1)}, bf16[1040,128]{1,0:T(8,128)(2,1)S(1)}, u32[]{:S(2)}, u32[]{:S(2)}) %collective-permute-start.5) | collective-permute-done | bytes 266272 | tf_op jit(solution)/shard_map/ppermute | solution.py:244
  51.2 0.9 %shard_map.57 = bf16[16,80,128]{2,1,0:T(8,128)(2,1)} custom-call(f32[1032,128]{1,0:T(8,128)S(1)} %shard_map.56.own, bf16[1040,128]{1,0:T(8,128)(2,1)S(1)} %collective-permute-done.5.up, bf16[1040,128]{1,0:T(8,128)(2,1)S(1)} %collective-permute-done.6.down, bf16[1040,128]{1,0:T(8,128)(2,1)S(1)} %collective-permute-done.7.deep), custom_call_target="tpu_custom_call" | custom-call | bytes 1048576 | tf_op jit(solution)/shard_map/pallas_call | solution.py:178
  52.1 10.3 %all-to-all-start.1 = ((bf16[16,80,128]{2,1,0:T(8,128)(2,1)}), bf16[16,80,128]{2,1,0:T(8,128)(2,1)S(1)}, u32[]{:S(2)}, u32[]{:S(2)}) async-start(bf16[16,80,128]{2,1,0:T(8,128)(2,1)} %shard_map.57), calls=%async_computation.1 | async-start | bytes 655360 | tf_op jit(solution)/shard_map/all_to_all | solution.py:190
  62.4 0.6 dynamic_slice.6
  63.7 5.4 %all-to-all-done.1.packed = bf16[16,80,128]{2,1,0:T(8,128)(2,1)S(1)} async-done(((bf16[16,80,128]{2,1,0:T(8,128)(2,1)}), bf16[16,80,128]{2,1,0:T(8,128)(2,1)S(1)}, u32[]{:S(2)}, u32[]{:S(2)}) %all-to-all-start.1) | async-done | bytes 327712 | tf_op jit(solution)/shard_map/all_to_all | solution.py:190
  69.1 0.1 shard_map.58.mine
  69.2 0.0 collective-permute-start.8
  69.3 2.8 %collective-permute-done.8.across = f32[9,8,128]{2,1,0:T(8,128)S(1)} collective-permute-done((f32[9,8,128]{2,1,0:T(8,128)S(1)}, f32[9,8,128]{2,1,0:T(8,128)S(1)}, u32[]{:S(2)}, u32[]{:S(2)}) %collective-permute-start.8) | collective-permute-done | bytes 36896 | tf_op jit(solution)/shard_map/ppermute | solution.py:251
  72.1 4.1 %collective-permute-start.9 = (f32[8,1024]{1,0:T(8,128)S(1)}, f32[8,1024]{1,0:T(8,128)S(1)}, u32[]{:S(2)}, u32[]{:S(2)}) collective-permute-start(f32[8,1024]{1,0:T(8,128)S(1)} %shard_map.59.mine), channel_id=1, source_target_pairs={{0,1},{1,0},{2,3},{3,2},{4,5},{5,4},{6,7},{7,6},{8,9},{9,8},{10,11... | collective-permute-start | bytes 98312 | tf_op jit(solution)/shard_map/ppermute | solution.py:259
  76.2 0.6 reduce
  76.8 0.2 collective-permute-done.9.other
  77.1 0.6 shard_map.60
  (14 shorter events, 0.1 us)
Async XLA Ops:
  0.6 29.5 %collective-permute-start = (bf16[1536,1024]{1,0:T(8,128)(2,1)}, bf16[1536,1024]{1,0:T(8,128)(2,1)S(1)}, u32[]{:S(2)}, u32[]{:S(2)}) collective-permute-start(bf16[1536,1024]{1,0:T(8,128)(2,1)} %docs.3), channel_id=1, source_target_pairs={{0,1},{1,0},{2,3},{3,2},{4,5},{5,4},{6,7},{7,6},{8,9},{9,8},{10,11... | collective-permute-start | bytes 9437192 | tf_op jit(solution)/shard_map/ppermute | solution.py:198
  24.0 8.1 %collective-permute-start.1 = (bf16[128,1024]{1,0:T(8,128)(2,1)S(1)}, bf16[128,1024]{1,0:T(8,128)(2,1)S(1)}, u32[]{:S(2)}, u32[]{:S(2)}) collective-permute-start(bf16[128,1024]{1,0:T(8,128)(2,1)S(1)} %bitcast.4), channel_id=1, source_target_pairs={{0,28},{1,5},{2,30},{3,7},{4,0},{5,9},{6,2},{7,11},{8,4},{9,13},{1... | collective-permute-start | bytes 786440 | tf_op jit(solution)/shard_map/ppermute | solution.py:202
  24.3 8.9 %collective-permute-start.3 = (bf16[128,1024]{1,0:T(8,128)(2,1)S(1)}, bf16[128,1024]{1,0:T(8,128)(2,1)S(1)}, u32[]{:S(2)}, u32[]{:S(2)}) collective-permute-start(bf16[128,1024]{1,0:T(8,128)(2,1)S(1)} %bitcast.5), channel_id=1, source_target_pairs={{0,64},{1,65},{2,66},{3,67},{4,68},{5,69},{6,70},{7,71},{8,72},{9,... | collective-permute-start | bytes 786440 | tf_op jit(solution)/shard_map/ppermute | solution.py:202
  25.7 7.5 %collective-permute-start.2 = (bf16[128,1024]{1,0:T(8,128)(2,1)S(1)}, bf16[128,1024]{1,0:T(8,128)(2,1)S(1)}, u32[]{:S(2)}, u32[]{:S(2)}) collective-permute-start(bf16[128,1024]{1,0:T(8,128)(2,1)S(1)} %bitcast.6), channel_id=1, source_target_pairs={{0,192},{1,193},{2,194},{3,195},{4,196},{5,197},{6,198},{7,199},{8... | collective-permute-start | bytes 786440 | tf_op jit(solution)/shard_map/ppermute | solution.py:202
  27.4 1.9 %copy-start = (bf16[1536,1024]{1,0:T(8,128)(2,1)S(1)}, bf16[1536,1024]{1,0:T(8,128)(2,1)}, u32[]{:S(2)}) copy-start(bf16[1536,1024]{1,0:T(8,128)(2,1)} %docs.3) | copy-start | bytes 9437188
  33.2 6.5 %copy-start.1 = (bf16[1536,1024]{1,0:T(8,128)(2,1)S(1)}, bf16[1536,1024]{1,0:T(8,128)(2,1)}, u32[]{:S(2)}) copy-start(bf16[1536,1024]{1,0:T(8,128)(2,1)} %docs.3) | copy-start | bytes 9437188
  35.2 4.4 %collective-permute-start.4 = (f32[4,1536]{1,0:T(4,128)S(1)}, f32[4,1536]{1,0:T(4,128)S(1)}, u32[]{:S(2)}, u32[]{:S(2)}) collective-permute-start(f32[4,1536]{1,0:T(4,128)S(1)} %get-tuple-element.18.mine), channel_id=1, source_target_pairs={{0,1},{1,0},{2,3},{3,2},{4,5},{5,4},{6,7},{7,6},{8,9},{9,8},{10,11... | collective-permute-start | bytes 73736 | tf_op jit(solution)/shard_map/ppermute | solution.py:224
  42.3 8.9 %collective-permute-start.5 = (bf16[1040,128]{1,0:T(8,128)(2,1)S(1)}, bf16[1040,128]{1,0:T(8,128)(2,1)S(1)}, u32[]{:S(2)}, u32[]{:S(2)}) collective-permute-start(bf16[1040,128]{1,0:T(8,128)(2,1)S(1)} %get-tuple-element.20), channel_id=1, source_target_pairs={{0,64},{1,65},{2,66},{3,67},{4,68},{5,69},{6,70},{7,71},{8,72},{9,... | collective-permute-start | bytes 798728 | tf_op jit(solution)/shard_map/ppermute | solution.py:244
  42.4 8.8 %collective-permute-start.6 = (bf16[1040,128]{1,0:T(8,128)(2,1)S(1)}, bf16[1040,128]{1,0:T(8,128)(2,1)S(1)}, u32[]{:S(2)}, u32[]{:S(2)}) collective-permute-start(bf16[1040,128]{1,0:T(8,128)(2,1)S(1)} %get-tuple-element.21), channel_id=1, source_target_pairs={{0,192},{1,193},{2,194},{3,195},{4,196},{5,197},{6,198},{7,199},{8... | collective-permute-start | bytes 798728 | tf_op jit(solution)/shard_map/ppermute | solution.py:244
  45.1 6.2 %collective-permute-start.7 = (bf16[1040,128]{1,0:T(8,128)(2,1)S(1)}, bf16[1040,128]{1,0:T(8,128)(2,1)S(1)}, u32[]{:S(2)}, u32[]{:S(2)}) collective-permute-start(bf16[1040,128]{1,0:T(8,128)(2,1)S(1)} %get-tuple-element.22), channel_id=1, source_target_pairs={{0,4},{1,29},{2,6},{3,31},{4,8},{5,1},{6,10},{7,3},{8,12},{9,5},{1... | collective-permute-start | bytes 798728 | tf_op jit(solution)/shard_map/ppermute | solution.py:244
  46.0 16.4 %copy-start.3 = (s32[4]{0:T(128)S(1)}, s32[4]{0:T(128)}, u32[]{:S(2)}) copy-start(s32[4]{0:T(128)} %constant.72.clone) | copy-start | bytes 52
  46.0 26.0 %copy-start.2 = (bf16[16,1024]{1,0:T(8,128)(2,1)S(1)}, bf16[16,1024]{1,0:T(8,128)(2,1)}, u32[]{:S(2)}) copy-start(bf16[16,1024]{1,0:T(8,128)(2,1)} %centroids.1) | copy-start | bytes 98308
  52.1 17.0 %all-to-all-start.1 = ((bf16[16,80,128]{2,1,0:T(8,128)(2,1)}), bf16[16,80,128]{2,1,0:T(8,128)(2,1)S(1)}, u32[]{:S(2)}, u32[]{:S(2)}) async-start(bf16[16,80,128]{2,1,0:T(8,128)(2,1)} %shard_map.57), calls=%async_computation.1 | async-start | bytes 655360 | tf_op jit(solution)/shard_map/all_to_all | solution.py:190
  69.2 2.8 %collective-permute-start.8 = (f32[9,8,128]{2,1,0:T(8,128)S(1)}, f32[9,8,128]{2,1,0:T(8,128)S(1)}, u32[]{:S(2)}, u32[]{:S(2)}) collective-permute-start(f32[9,8,128]{2,1,0:T(8,128)S(1)} %shard_map.58.mine), channel_id=1, source_target_pairs={{0,2},{1,3},{2,0},{3,1},{4,6},{5,7},{6,4},{7,5},{8,10},{9,11},{10,... | collective-permute-start | bytes 110600 | tf_op jit(solution)/shard_map/ppermute | solution.py:251
  72.1 5.0 %collective-permute-start.9 = (f32[8,1024]{1,0:T(8,128)S(1)}, f32[8,1024]{1,0:T(8,128)S(1)}, u32[]{:S(2)}, u32[]{:S(2)}) collective-permute-start(f32[8,1024]{1,0:T(8,128)S(1)} %shard_map.59.mine), channel_id=1, source_target_pairs={{0,1},{1,0},{2,3},{3,2},{4,5},{5,4},{6,7},{7,6},{8,9},{9,8},{10,11... | collective-permute-start | bytes 98312 | tf_op jit(solution)/shard_map/ppermute | solution.py:259

commit v8 on v7

--- a/solution.py
+++ b/solution.py
@@ -195,10 +195,11 @@
     beta = 3.0 / math.sqrt(width)
     blk = lax.axis_index("blk")
     core = lax.axis_index("dp") % 2
-    others = lax.ppermute(documents, "dp", within(1))
 
     near = lax.dynamic_slice_in_dim(centroids, core * 8, 8, 0).reshape(1, 8, width)
     quarter = exchange(jnp.broadcast_to(near, (16, 8, width))).reshape(128, width)
+    held_docs, quarter = lax.optimization_barrier((documents, quarter))
+    others = lax.ppermute(held_docs, "dp", within(1))
     quarters = [quarter] + [lax.ppermute(quarter, BOTH, star(side, -1)) for side in range(3)]
 
     flops = 2 * 512 * 2 * count * width

time: 78 us -> 77.5 us (level)
  starting transfers between devices: 28.4 us -> 26.1 us
  blocking collectives: 19.3 us -> 21.3 us
    all_to_all x1, blocking collectives: 19.3 us -> 21.3 us  [exchange(): lax.all_to_all(part, BOTH, 0, 0, axis_index_groups=GROUPS, tiled=True)]
    ppermute x1, starting transfers between devices: 3.33 us -> 1.62 us  [body(): others = lax.ppermute(held_docs, 'dp', within(1))]
    ppermute x1, starting transfers between devices: 3.6 us -> 2.46 us  [body(): theirs = lax.ppermute(mine, 'dp', within(1))]
  transfers between devices with their start and end apart: 11 -> 11, of which waited for: 5 -> 5; matrix products, arithmetic and copies ran while one was open for 3% -> 2% of each run, Pallas kernels for 6% -> 6%
where the time goes in v8:
time: 77.5 us; the launch traced here: 77.2 us
  starting transfers between devices  26.1 us (34%)
  blocking collectives  21.3 us (27%)
  waiting for transfers between devices  13.3 us (17%)
  Pallas kernels  11.2 us (14%)
  local copies, waits for them, and re-layouts  3.23 us (4%)
  between operations  1.43 us (2%)
    all_to_all x1, blocking collectives, exchange(): lax.all_to_all(part, BOTH, 0, 0, axis_index_groups=GROUPS, tiled=True)  21.3 us
    pallas_call x11, Pallas kernels, call(): pl.pallas_call(kernel, out_shape=[jax.ShapeDtypeStruct(shape, dtype) for...  11.2 us
    all_to_all x1, starting transfers between devices, exchange(): lax.all_to_all(part, BOTH, 0, 0, axis_index_groups=GROUPS, tiled=True)  10.3 us
    all_to_all x1, waiting for transfers between devices, exchange(): lax.all_to_all(part, BOTH, 0, 0, axis_index_groups=GROUPS, tiled=True)  5.87 us
    ppermute x3, starting transfers between devices, body(): lax.ppermute(part, BOTH, star(side, 1))  4.31 us
    ppermute x1, starting transfers between devices, body(): other = lax.ppermute(half, 'dp', within(1))  3.94 us
    ppermute x3, waiting for transfers between devices, body(): lax.ppermute(part, BOTH, star(side, 1))  3.58 us
    ppermute x3, starting transfers between devices, body(): lax.ppermute(quarter, BOTH, star(side, -1))  3.43 us
  transfers between devices with their start and end apart: 11, of which 5 were waited for; matrix products, arithmetic and copies ran while one was open for 2% of the time, Pallas kernels for 6%

profile of v8, /device:TPU:1, one launch (start us, length us, event | category | flops | bytes accessed | tf_op | source)
XLA Modules:
  0.0 77.2 jit_solution(7220125344957636980)
XLA Ops:
  0.6 0.7 constant_dynamic-slice_fusion
  1.4 21.3 %all_to_all.10 = bf16[16,8,1024]{2,1,0:T(8,128)(2,1)S(1)} all-to-all(bf16[16,8,1024]{2,1,0:T(8,128)(2,1)S(1)} %broadcast_in_dim.2), channel_id=1, replica_groups={{182,148,58,24,190,156,34,0,166,132,42,8,174,140,50,16},{183,149,59,25,..., dimensions={0} | all-to-all | bytes 524288 | tf_op jit(solution)/shard_map/all_to_all | solution.py:190
  22.7 1.6 %collective-permute-start = (bf16[1536,1024]{1,0:T(8,128)(2,1)}, bf16[1536,1024]{1,0:T(8,128)(2,1)S(1)}, u32[]{:S(2)}, u32[]{:S(2)}) collective-permute-start(bf16[1536,1024]{1,0:T(8,128)(2,1)} %docs.3), channel_id=1, source_target_pairs={{0,1},{1,0},{2,3},{3,2},{4,5},{5,4},{6,7},{7,6},{8,9},{9,8},{10,11... | collective-permute-start | bytes 9437192 | tf_op jit(solution)/shard_map/ppermute | solution.py:202
  24.3 0.7 collective-permute-start.1
  25.1 0.9 %collective-permute-start.3 = (bf16[128,1024]{1,0:T(8,128)(2,1)S(1)}, bf16[128,1024]{1,0:T(8,128)(2,1)S(1)}, u32[]{:S(2)}, u32[]{:S(2)}) collective-permute-start(bf16[128,1024]{1,0:T(8,128)(2,1)S(1)} %bitcast.5), channel_id=1, source_target_pairs={{0,64},{1,65},{2,66},{3,67},{4,68},{5,69},{6,70},{7,71},{8,72},{9,... | collective-permute-start | bytes 786440 | tf_op jit(solution)/shard_map/ppermute | solution.py:203
  26.0 1.8 %collective-permute-start.2 = (bf16[128,1024]{1,0:T(8,128)(2,1)S(1)}, bf16[128,1024]{1,0:T(8,128)(2,1)S(1)}, u32[]{:S(2)}, u32[]{:S(2)}) collective-permute-start(bf16[128,1024]{1,0:T(8,128)(2,1)S(1)} %bitcast.6), channel_id=1, source_target_pairs={{0,192},{1,193},{2,194},{3,195},{4,196},{5,197},{6,198},{7,199},{8... | collective-permute-start | bytes 786440 | tf_op jit(solution)/shard_map/ppermute | solution.py:203
  27.7 1.9 %copy-done = bf16[1536,1024]{1,0:T(8,128)(2,1)S(1)} copy-done((bf16[1536,1024]{1,0:T(8,128)(2,1)S(1)}, bf16[1536,1024]{1,0:T(8,128)(2,1)}, u32[]{:S(2)}) %copy-start) | copy-done | bytes 3145752
  29.6 0.9 %shard_map.50.refs_1_.refs_2_.refs_3_ = bf16[1024,1536]{1,0:T(8,128)(2,1)S(1)} custom-call(bf16[1536,1024]{1,0:T(8,128)(2,1)S(1)} %copy-done), custom_call_target="tpu_custom_call" | custom-call | flops 50331648 | bytes 1048576 | tf_op jit(solution)/shard_map/pallas_call | solution.py:178
  30.5 0.9 %shard_map.51.refs_2_.refs_3_.refs_4_ = bf16[1024,1536]{1,0:T(8,128)(2,1)S(1)} custom-call(bf16[1536,1024]{1,0:T(8,128)(2,1)S(1)} %collective-permute-done.source.others), custom_call_target="tpu_custom_call" | custom-call | flops 50331648 | bytes 1048576 | tf_op jit(solution)/shard_map/pallas_call | solution.py:178
  31.4 1.1 %shard_map.52 = (f32[128,3072]{1,0:T(8,128)S(1)}, f32[4,1536]{1,0:T(4,128)S(1)}) custom-call(bf16[128,1024]{1,0:T(8,128)(2,1)S(1)} %bitcast.7, bf16[1024,1536]{1,0:T(8,128)(2,1)S(1)} %shard_map.50.refs_1_.refs_2_.refs_3_, bf16[1024,1536]{1,0:T(8,128)(2,1)S(1)} %shard_map.51.refs_2_.refs_3_.refs_4_), custom_call_target="tpu_custom_call" | custom-call | flops 100663296 | bytes 1048576 | tf_op jit(solution)/shard_map/pallas_call | solution.py:178
  32.5 1.1 %shard_map.53 = (f32[128,3072]{1,0:T(8,128)S(1)}, f32[4,1536]{1,0:T(4,128)S(1)}) custom-call(f32[4,1536]{1,0:T(4,128)S(1)} %get-tuple-element.18.refs_0_, bf16[128,1024]{1,0:T(8,128)(2,1)S(1)} %collective-permute-done.1.refs_1_, bf16[1024,1536]{1,0:T(8,128)(2,1)S(1)} %shard_map.50.refs_1_.refs_2_.refs_3_, ...), custom_call_target="tpu_custom_call" | custom-call | flops 100663296 | bytes 1048576 | tf_op jit(solution)/shard_map/pallas_call | solution.py:178
  33.6 0.0 copy-start.1
  33.6 2.0 %shard_map.54 = (f32[256,3072]{1,0:T(8,128)S(1)}, f32[4,1536]{1,0:T(4,128)S(1)}) custom-call(f32[4,1536]{1,0:T(4,128)S(1)} %get-tuple-element.19.refs_0_, bf16[128,1024]{1,0:T(8,128)(2,1)S(1)} %collective-permute-done.2.refs_1_, bf16[128,1024]{1,0:T(8,128)(2,1)S(1)} %collective-permute-done.3.refs_2_, ...), custom_call_target="tpu_custom_call" | custom-call | flops 201326592 | bytes 1048576 | tf_op jit(solution)/shard_map/pallas_call | solution.py:178
  35.6 2.5 %collective-permute-start.4 = (f32[4,1536]{1,0:T(4,128)S(1)}, f32[4,1536]{1,0:T(4,128)S(1)}, u32[]{:S(2)}, u32[]{:S(2)}) collective-permute-start(f32[4,1536]{1,0:T(4,128)S(1)} %get-tuple-element.22.mine), channel_id=1, source_target_pairs={{0,1},{1,0},{2,3},{3,2},{4,5},{5,4},{6,7},{7,6},{8,9},{9,8},{10,11... | collective-permute-start | bytes 73736 | tf_op jit(solution)/shard_map/ppermute | solution.py:225
  38.1 0.8 %collective-permute-done.4.theirs = f32[4,1536]{1,0:T(4,128)S(1)} collective-permute-done((f32[4,1536]{1,0:T(4,128)S(1)}, f32[4,1536]{1,0:T(4,128)S(1)}, u32[]{:S(2)}, u32[]{:S(2)}) %collective-permute-start.4) | collective-permute-done | bytes 24608 | tf_op jit(solution)/shard_map/ppermute | solution.py:225
  38.9 2.7 %shard_map.55 = (f32[1,1536]{1,0:T(1,128)S(1)}, f32[2,1536]{1,0:T(2,128)S(1)}, bf16[1040,128]{1,0:T(8,128)(2,1)S(1)}, bf16[1040,128]{1,0:T(8,128)(2,1)S(1)}, bf16[1040,128]{1,0:T(8,128)(2,1)S(1)}) custom-call(f32[256,3072]{1,0:T(8,128)S(1)} %get-tuple-element.20.pair, f32[128,3072]{1,0:T(8,128)S(1)} %get-tuple-element.21.deep, ...), custom_call_target="tpu_custom_call" | custom-call | flops 3221225472 | bytes 1048576 | tf_op jit(solution)/shard_map/pallas_call | solution.py:178
  41.6 0.1 collective-permute-start.5
  41.7 2.7 %collective-permute-start.6 = (bf16[1040,128]{1,0:T(8,128)(2,1)S(1)}, bf16[1040,128]{1,0:T(8,128)(2,1)S(1)}, u32[]{:S(2)}, u32[]{:S(2)}) collective-permute-start(bf16[1040,128]{1,0:T(8,128)(2,1)S(1)} %get-tuple-element.25), channel_id=1, source_target_pairs={{0,192},{1,193},{2,194},{3,195},{4,196},{5,197},{6,198},{7,199},{8... | collective-permute-start | bytes 798728 | tf_op jit(solution)/shard_map/ppermute | solution.py:245
  44.3 1.6 %collective-permute-start.7 = (bf16[1040,128]{1,0:T(8,128)(2,1)S(1)}, bf16[1040,128]{1,0:T(8,128)(2,1)S(1)}, u32[]{:S(2)}, u32[]{:S(2)}) collective-permute-start(bf16[1040,128]{1,0:T(8,128)(2,1)S(1)} %get-tuple-element.26), channel_id=1, source_target_pairs={{0,4},{1,29},{2,6},{3,31},{4,8},{5,1},{6,10},{7,3},{8,12},{9,5},{1... | collective-permute-start | bytes 798728 | tf_op jit(solution)/shard_map/ppermute | solution.py:245
  45.9 1.0 %shard_map.56.own = f32[1032,128]{1,0:T(8,128)S(1)} custom-call(f32[128,3072]{1,0:T(8,128)S(1)} %get-tuple-element.17.own, f32[2,1536]{1,0:T(2,128)S(1)} %get-tuple-element.23.norms, bf16[1536,1024]{1,0:T(8,128)(2,1)S(1)} %copy-done.1, bf16[1536,1024]{1,0:T(8,128)(2,1)S(1)} %collective-permute-done.source.others), custom_call_target="tpu_custom_call" | custom-call | flops 805306368 | bytes 1048576 | tf_op jit(solution)/shard_map/pallas_call | solution.py:178
  46.9 3.6 %collective-permute-done.5.up = bf16[1040,128]{1,0:T(8,128)(2,1)S(1)} collective-permute-done((bf16[1040,128]{1,0:T(8,128)(2,1)S(1)}, bf16[1040,128]{1,0:T(8,128)(2,1)S(1)}, u32[]{:S(2)}, u32[]{:S(2)}) %collective-permute-start.5) | collective-permute-done | bytes 266272 | tf_op jit(solution)/shard_map/ppermute | solution.py:245
  50.5 0.9 %shard_map.57 = bf16[16,80,128]{2,1,0:T(8,128)(2,1)} custom-call(f32[1032,128]{1,0:T(8,128)S(1)} %shard_map.56.own, bf16[1040,128]{1,0:T(8,128)(2,1)S(1)} %collective-permute-done.5.up, bf16[1040,128]{1,0:T(8,128)(2,1)S(1)} %collective-permute-done.6.down, bf16[1040,128]{1,0:T(8,128)(2,1)S(1)} %collective-permute-done.7.deep), custom_call_target="tpu_custom_call" | custom-call | bytes 1048576 | tf_op jit(solution)/shard_map/pallas_call | solution.py:178
  51.4 10.3 %all-to-all-start.1 = ((bf16[16,80,128]{2,1,0:T(8,128)(2,1)}), bf16[16,80,128]{2,1,0:T(8,128)(2,1)S(1)}, u32[]{:S(2)}, u32[]{:S(2)}) async-start(bf16[16,80,128]{2,1,0:T(8,128)(2,1)} %shard_map.57), calls=%async_computation.1 | async-start | bytes 655360 | tf_op jit(solution)/shard_map/all_to_all | solution.py:190
  61.7 0.6 dynamic_slice.6
  62.9 5.9 %all-to-all-done.1.packed = bf16[16,80,128]{2,1,0:T(8,128)(2,1)S(1)} async-done(((bf16[16,80,128]{2,1,0:T(8,128)(2,1)}), bf16[16,80,128]{2,1,0:T(8,128)(2,1)S(1)}, u32[]{:S(2)}, u32[]{:S(2)}) %all-to-all-start.1) | async-done | bytes 327712 | tf_op jit(solution)/shard_map/all_to_all | solution.py:190
  68.8 0.1 shard_map.58.mine
  68.9 0.0 collective-permute-start.8
  69.0 2.8 %collective-permute-done.8.across = f32[9,8,128]{2,1,0:T(8,128)S(1)} collective-permute-done((f32[9,8,128]{2,1,0:T(8,128)S(1)}, f32[9,8,128]{2,1,0:T(8,128)S(1)}, u32[]{:S(2)}, u32[]{:S(2)}) %collective-permute-start.8) | collective-permute-done | bytes 36896 | tf_op jit(solution)/shard_map/ppermute | solution.py:252
  71.8 3.9 %collective-permute-start.9 = (f32[8,1024]{1,0:T(8,128)S(1)}, f32[8,1024]{1,0:T(8,128)S(1)}, u32[]{:S(2)}, u32[]{:S(2)}) collective-permute-start(f32[8,1024]{1,0:T(8,128)S(1)} %shard_map.59.mine), channel_id=1, source_target_pairs={{0,1},{1,0},{2,3},{3,2},{4,5},{5,4},{6,7},{7,6},{8,9},{9,8},{10,11... | collective-permute-start | bytes 98312 | tf_op jit(solution)/shard_map/ppermute | solution.py:260
  75.7 0.6 reduce
  76.3 0.2 collective-permute-done.9.other
  76.6 0.6 shard_map.60
  (14 shorter events, 0.1 us)
Async XLA Ops:
  22.7 7.8 %collective-permute-start = (bf16[1536,1024]{1,0:T(8,128)(2,1)}, bf16[1536,1024]{1,0:T(8,128)(2,1)S(1)}, u32[]{:S(2)}, u32[]{:S(2)}) collective-permute-start(bf16[1536,1024]{1,0:T(8,128)(2,1)} %docs.3), channel_id=1, source_target_pairs={{0,1},{1,0},{2,3},{3,2},{4,5},{5,4},{6,7},{7,6},{8,9},{9,8},{10,11... | collective-permute-start | bytes 9437192 | tf_op jit(solution)/shard_map/ppermute | solution.py:202
  24.3 8.2 %collective-permute-start.1 = (bf16[128,1024]{1,0:T(8,128)(2,1)S(1)}, bf16[128,1024]{1,0:T(8,128)(2,1)S(1)}, u32[]{:S(2)}, u32[]{:S(2)}) collective-permute-start(bf16[128,1024]{1,0:T(8,128)(2,1)S(1)} %bitcast.4), channel_id=1, source_target_pairs={{0,28},{1,5},{2,30},{3,7},{4,0},{5,9},{6,2},{7,11},{8,4},{9,13},{1... | collective-permute-start | bytes 786440 | tf_op jit(solution)/shard_map/ppermute | solution.py:203
  25.1 8.5 %collective-permute-start.3 = (bf16[128,1024]{1,0:T(8,128)(2,1)S(1)}, bf16[128,1024]{1,0:T(8,128)(2,1)S(1)}, u32[]{:S(2)}, u32[]{:S(2)}) collective-permute-start(bf16[128,1024]{1,0:T(8,128)(2,1)S(1)} %bitcast.5), channel_id=1, source_target_pairs={{0,64},{1,65},{2,66},{3,67},{4,68},{5,69},{6,70},{7,71},{8,72},{9,... | collective-permute-start | bytes 786440 | tf_op jit(solution)/shard_map/ppermute | solution.py:203
  26.0 7.6 %collective-permute-start.2 = (bf16[128,1024]{1,0:T(8,128)(2,1)S(1)}, bf16[128,1024]{1,0:T(8,128)(2,1)S(1)}, u32[]{:S(2)}, u32[]{:S(2)}) collective-permute-start(bf16[128,1024]{1,0:T(8,128)(2,1)S(1)} %bitcast.6), channel_id=1, source_target_pairs={{0,192},{1,193},{2,194},{3,195},{4,196},{5,197},{6,198},{7,199},{8... | collective-permute-start | bytes 786440 | tf_op jit(solution)/shard_map/ppermute | solution.py:203
  27.7 1.9 %copy-start = (bf16[1536,1024]{1,0:T(8,128)(2,1)S(1)}, bf16[1536,1024]{1,0:T(8,128)(2,1)}, u32[]{:S(2)}) copy-start(bf16[1536,1024]{1,0:T(8,128)(2,1)} %docs.3) | copy-start | bytes 9437188
  33.6 5.3 %copy-start.1 = (bf16[1536,1024]{1,0:T(8,128)(2,1)S(1)}, bf16[1536,1024]{1,0:T(8,128)(2,1)}, u32[]{:S(2)}) copy-start(bf16[1536,1024]{1,0:T(8,128)(2,1)} %docs.3) | copy-start | bytes 9437188
  35.6 3.3 %collective-permute-start.4 = (f32[4,1536]{1,0:T(4,128)S(1)}, f32[4,1536]{1,0:T(4,128)S(1)}, u32[]{:S(2)}, u32[]{:S(2)}) collective-permute-start(f32[4,1536]{1,0:T(4,128)S(1)} %get-tuple-element.22.mine), channel_id=1, source_target_pairs={{0,1},{1,0},{2,3},{3,2},{4,5},{5,4},{6,7},{7,6},{8,9},{9,8},{10,11... | collective-permute-start | bytes 73736 | tf_op jit(solution)/shard_map/ppermute | solution.py:225
  41.6 8.9 %collective-permute-start.5 = (bf16[1040,128]{1,0:T(8,128)(2,1)S(1)}, bf16[1040,128]{1,0:T(8,128)(2,1)S(1)}, u32[]{:S(2)}, u32[]{:S(2)}) collective-permute-start(bf16[1040,128]{1,0:T(8,128)(2,1)S(1)} %get-tuple-element.24), channel_id=1, source_target_pairs={{0,64},{1,65},{2,66},{3,67},{4,68},{5,69},{6,70},{7,71},{8,72},{9,... | collective-permute-start | bytes 798728 | tf_op jit(solution)/shard_map/ppermute | solution.py:245
  41.7 8.8 %collective-permute-start.6 = (bf16[1040,128]{1,0:T(8,128)(2,1)S(1)}, bf16[1040,128]{1,0:T(8,128)(2,1)S(1)}, u32[]{:S(2)}, u32[]{:S(2)}) collective-permute-start(bf16[1040,128]{1,0:T(8,128)(2,1)S(1)} %get-tuple-element.25), channel_id=1, source_target_pairs={{0,192},{1,193},{2,194},{3,195},{4,196},{5,197},{6,198},{7,199},{8... | collective-permute-start | bytes 798728 | tf_op jit(solution)/shard_map/ppermute | solution.py:245
  44.3 6.2 %collective-permute-start.7 = (bf16[1040,128]{1,0:T(8,128)(2,1)S(1)}, bf16[1040,128]{1,0:T(8,128)(2,1)S(1)}, u32[]{:S(2)}, u32[]{:S(2)}) collective-permute-start(bf16[1040,128]{1,0:T(8,128)(2,1)S(1)} %get-tuple-element.26), channel_id=1, source_target_pairs={{0,4},{1,29},{2,6},{3,31},{4,8},{5,1},{6,10},{7,3},{8,12},{9,5},{1... | collective-permute-start | bytes 798728 | tf_op jit(solution)/shard_map/ppermute | solution.py:245
  45.9 15.8 %copy-start.3 = (s32[4]{0:T(128)S(1)}, s32[4]{0:T(128)}, u32[]{:S(2)}) copy-start(s32[4]{0:T(128)} %constant.72.clone) | copy-start | bytes 52
  45.9 25.9 %copy-start.2 = (bf16[16,1024]{1,0:T(8,128)(2,1)S(1)}, bf16[16,1024]{1,0:T(8,128)(2,1)}, u32[]{:S(2)}) copy-start(bf16[16,1024]{1,0:T(8,128)(2,1)} %centroids.1) | copy-start | bytes 98308
  51.4 17.4 %all-to-all-start.1 = ((bf16[16,80,128]{2,1,0:T(8,128)(2,1)}), bf16[16,80,128]{2,1,0:T(8,128)(2,1)S(1)}, u32[]{:S(2)}, u32[]{:S(2)}) async-start(bf16[16,80,128]{2,1,0:T(8,128)(2,1)} %shard_map.57), calls=%async_computation.1 | async-start | bytes 655360 | tf_op jit(solution)/shard_map/all_to_all | solution.py:190
  68.9 2.8 %collective-permute-start.8 = (f32[9,8,128]{2,1,0:T(8,128)S(1)}, f32[9,8,128]{2,1,0:T(8,128)S(1)}, u32[]{:S(2)}, u32[]{:S(2)}) collective-permute-start(f32[9,8,128]{2,1,0:T(8,128)S(1)} %shard_map.58.mine), channel_id=1, source_target_pairs={{0,2},{1,3},{2,0},{3,1},{4,6},{5,7},{6,4},{7,5},{8,10},{9,11},{10,... | collective-permute-start | bytes 110600 | tf_op jit(solution)/shard_map/ppermute | solution.py:252
  71.8 4.8 %collective-permute-start.9 = (f32[8,1024]{1,0:T(8,128)S(1)}, f32[8,1024]{1,0:T(8,128)S(1)}, u32[]{:S(2)}, u32[]{:S(2)}) collective-permute-start(f32[8,1024]{1,0:T(8,128)S(1)} %shard_map.59.mine), channel_id=1, source_target_pairs={{0,1},{1,0},{2,3},{3,2},{4,5},{5,4},{6,7},{7,6},{8,9},{9,8},{10,11... | collective-permute-start | bytes 98312 | tf_op jit(solution)/shard_map/ppermute | solution.py:260

commit v9 on v8

--- a/solution.py
+++ b/solution.py
@@ -204,7 +204,7 @@
 
     flops = 2 * 512 * 2 * count * width
     turned = [
-        call(turn_kernel, [((width, count), jnp.bfloat16)], 10, (part,), flops=flops // 64)[0]
+        call(turn_kernel, [((width, count), jnp.bfloat16)], 10, (part,), flops=flops // 16)[0]
         for part in (documents, others)
     ]
     own, up, down, deep = quarters

time: 77.5 us -> 77.5 us (level)
  no operation moved by 1% of the time
where the time goes in v9:
time: 77.5 us; the launch traced here: 77.2 us
  starting transfers between devices  26.1 us (34%)
  blocking collectives  21.3 us (27%)
  waiting for transfers between devices  13.3 us (17%)
  Pallas kernels  11.2 us (14%)
  local copies, waits for them, and re-layouts  3.23 us (4%)
  between operations  1.43 us (2%)
    all_to_all x1, blocking collectives, exchange(): lax.all_to_all(part, BOTH, 0, 0, axis_index_groups=GROUPS, tiled=True)  21.3 us
    pallas_call x11, Pallas kernels, call(): pl.pallas_call(kernel, out_shape=[jax.ShapeDtypeStruct(shape, dtype) for...  11.2 us
    all_to_all x1, starting transfers between devices, exchange(): lax.all_to_all(part, BOTH, 0, 0, axis_index_groups=GROUPS, tiled=True)  10.3 us
    all_to_all x1, waiting for transfers between devices, exchange(): lax.all_to_all(part, BOTH, 0, 0, axis_index_groups=GROUPS, tiled=True)  5.87 us
    ppermute x3, starting transfers between devices, body(): lax.ppermute(part, BOTH, star(side, 1))  4.31 us
    ppermute x1, starting transfers between devices, body(): other = lax.ppermute(half, 'dp', within(1))  3.94 us
    ppermute x3, waiting for transfers between devices, body(): lax.ppermute(part, BOTH, star(side, 1))  3.58 us
    ppermute x3, starting transfers between devices, body(): lax.ppermute(quarter, BOTH, star(side, -1))  3.43 us
  transfers between devices with their start and end apart: 11, of which 5 were waited for; matrix products, arithmetic and copies ran while one was open for 2% of the time, Pallas kernels for 6%

profile of v9, /device:TPU:1, one launch (start us, length us, event | category | flops | bytes accessed | tf_op | source)
XLA Modules:
  0.0 77.2 jit_solution(7220125344957636980)
XLA Ops:
  0.6 0.7 constant_dynamic-slice_fusion
  1.4 21.3 %all_to_all.10 = bf16[16,8,1024]{2,1,0:T(8,128)(2,1)S(1)} all-to-all(bf16[16,8,1024]{2,1,0:T(8,128)(2,1)S(1)} %broadcast_in_dim.2), channel_id=1, replica_groups={{182,148,58,24,190,156,34,0,166,132,42,8,174,140,50,16},{183,149,59,25,..., dimensions={0} | all-to-all | bytes 524288 | tf_op jit(solution)/shard_map/all_to_all | solution.py:190
  22.7 1.6 %collective-permute-start = (bf16[1536,1024]{1,0:T(8,128)(2,1)}, bf16[1536,1024]{1,0:T(8,128)(2,1)S(1)}, u32[]{:S(2)}, u32[]{:S(2)}) collective-permute-start(bf16[1536,1024]{1,0:T(8,128)(2,1)} %docs.3), channel_id=1, source_target_pairs={{0,1},{1,0},{2,3},{3,2},{4,5},{5,4},{6,7},{7,6},{8,9},{9,8},{10,11... | collective-permute-start | bytes 9437192 | tf_op jit(solution)/shard_map/ppermute | solution.py:202
  24.3 0.7 collective-permute-start.1
  25.1 0.9 %collective-permute-start.3 = (bf16[128,1024]{1,0:T(8,128)(2,1)S(1)}, bf16[128,1024]{1,0:T(8,128)(2,1)S(1)}, u32[]{:S(2)}, u32[]{:S(2)}) collective-permute-start(bf16[128,1024]{1,0:T(8,128)(2,1)S(1)} %bitcast.5), channel_id=1, source_target_pairs={{0,64},{1,65},{2,66},{3,67},{4,68},{5,69},{6,70},{7,71},{8,72},{9,... | collective-permute-start | bytes 786440 | tf_op jit(solution)/shard_map/ppermute | solution.py:203
  26.0 1.8 %collective-permute-start.2 = (bf16[128,1024]{1,0:T(8,128)(2,1)S(1)}, bf16[128,1024]{1,0:T(8,128)(2,1)S(1)}, u32[]{:S(2)}, u32[]{:S(2)}) collective-permute-start(bf16[128,1024]{1,0:T(8,128)(2,1)S(1)} %bitcast.6), channel_id=1, source_target_pairs={{0,192},{1,193},{2,194},{3,195},{4,196},{5,197},{6,198},{7,199},{8... | collective-permute-start | bytes 786440 | tf_op jit(solution)/shard_map/ppermute | solution.py:203
  27.7 1.9 %copy-done = bf16[1536,1024]{1,0:T(8,128)(2,1)S(1)} copy-done((bf16[1536,1024]{1,0:T(8,128)(2,1)S(1)}, bf16[1536,1024]{1,0:T(8,128)(2,1)}, u32[]{:S(2)}) %copy-start) | copy-done | bytes 3145752
  29.6 0.9 %shard_map.50.refs_1_.refs_2_.refs_3_ = bf16[1024,1536]{1,0:T(8,128)(2,1)S(1)} custom-call(bf16[1536,1024]{1,0:T(8,128)(2,1)S(1)} %copy-done), custom_call_target="tpu_custom_call" | custom-call | flops 201326592 | bytes 1048576 | tf_op jit(solution)/shard_map/pallas_call | solution.py:178
  30.5 0.9 %shard_map.51.refs_2_.refs_3_.refs_4_ = bf16[1024,1536]{1,0:T(8,128)(2,1)S(1)} custom-call(bf16[1536,1024]{1,0:T(8,128)(2,1)S(1)} %collective-permute-done.source.others), custom_call_target="tpu_custom_call" | custom-call | flops 201326592 | bytes 1048576 | tf_op jit(solution)/shard_map/pallas_call | solution.py:178
  31.4 1.1 %shard_map.52 = (f32[128,3072]{1,0:T(8,128)S(1)}, f32[4,1536]{1,0:T(4,128)S(1)}) custom-call(bf16[128,1024]{1,0:T(8,128)(2,1)S(1)} %bitcast.7, bf16[1024,1536]{1,0:T(8,128)(2,1)S(1)} %shard_map.50.refs_1_.refs_2_.refs_3_, bf16[1024,1536]{1,0:T(8,128)(2,1)S(1)} %shard_map.51.refs_2_.refs_3_.refs_4_), custom_call_target="tpu_custom_call" | custom-call | flops 100663296 | bytes 1048576 | tf_op jit(solution)/shard_map/pallas_call | solution.py:178
  32.5 1.1 %shard_map.53 = (f32[128,3072]{1,0:T(8,128)S(1)}, f32[4,1536]{1,0:T(4,128)S(1)}) custom-call(f32[4,1536]{1,0:T(4,128)S(1)} %get-tuple-element.18.refs_0_, bf16[128,1024]{1,0:T(8,128)(2,1)S(1)} %collective-permute-done.1.refs_1_, bf16[1024,1536]{1,0:T(8,128)(2,1)S(1)} %shard_map.50.refs_1_.refs_2_.refs_3_, ...), custom_call_target="tpu_custom_call" | custom-call | flops 100663296 | bytes 1048576 | tf_op jit(solution)/shard_map/pallas_call | solution.py:178
  33.6 0.0 copy-start.1
  33.6 2.0 %shard_map.54 = (f32[256,3072]{1,0:T(8,128)S(1)}, f32[4,1536]{1,0:T(4,128)S(1)}) custom-call(f32[4,1536]{1,0:T(4,128)S(1)} %get-tuple-element.19.refs_0_, bf16[128,1024]{1,0:T(8,128)(2,1)S(1)} %collective-permute-done.2.refs_1_, bf16[128,1024]{1,0:T(8,128)(2,1)S(1)} %collective-permute-done.3.refs_2_, ...), custom_call_target="tpu_custom_call" | custom-call | flops 201326592 | bytes 1048576 | tf_op jit(solution)/shard_map/pallas_call | solution.py:178
  35.6 2.5 %collective-permute-start.4 = (f32[4,1536]{1,0:T(4,128)S(1)}, f32[4,1536]{1,0:T(4,128)S(1)}, u32[]{:S(2)}, u32[]{:S(2)}) collective-permute-start(f32[4,1536]{1,0:T(4,128)S(1)} %get-tuple-element.22.mine), channel_id=1, source_target_pairs={{0,1},{1,0},{2,3},{3,2},{4,5},{5,4},{6,7},{7,6},{8,9},{9,8},{10,11... | collective-permute-start | bytes 73736 | tf_op jit(solution)/shard_map/ppermute | solution.py:225
  38.1 0.8 %collective-permute-done.4.theirs = f32[4,1536]{1,0:T(4,128)S(1)} collective-permute-done((f32[4,1536]{1,0:T(4,128)S(1)}, f32[4,1536]{1,0:T(4,128)S(1)}, u32[]{:S(2)}, u32[]{:S(2)}) %collective-permute-start.4) | collective-permute-done | bytes 24608 | tf_op jit(solution)/shard_map/ppermute | solution.py:225
  38.9 2.7 %shard_map.55 = (f32[1,1536]{1,0:T(1,128)S(1)}, f32[2,1536]{1,0:T(2,128)S(1)}, bf16[1040,128]{1,0:T(8,128)(2,1)S(1)}, bf16[1040,128]{1,0:T(8,128)(2,1)S(1)}, bf16[1040,128]{1,0:T(8,128)(2,1)S(1)}) custom-call(f32[256,3072]{1,0:T(8,128)S(1)} %get-tuple-element.20.pair, f32[128,3072]{1,0:T(8,128)S(1)} %get-tuple-element.21.deep, ...), custom_call_target="tpu_custom_call" | custom-call | flops 3221225472 | bytes 1048576 | tf_op jit(solution)/shard_map/pallas_call | solution.py:178
  41.6 0.1 collective-permute-start.5
  41.7 2.7 %collective-permute-start.6 = (bf16[1040,128]{1,0:T(8,128)(2,1)S(1)}, bf16[1040,128]{1,0:T(8,128)(2,1)S(1)}, u32[]{:S(2)}, u32[]{:S(2)}) collective-permute-start(bf16[1040,128]{1,0:T(8,128)(2,1)S(1)} %get-tuple-element.25), channel_id=1, source_target_pairs={{0,192},{1,193},{2,194},{3,195},{4,196},{5,197},{6,198},{7,199},{8... | collective-permute-start | bytes 798728 | tf_op jit(solution)/shard_map/ppermute | solution.py:245
  44.3 1.6 %collective-permute-start.7 = (bf16[1040,128]{1,0:T(8,128)(2,1)S(1)}, bf16[1040,128]{1,0:T(8,128)(2,1)S(1)}, u32[]{:S(2)}, u32[]{:S(2)}) collective-permute-start(bf16[1040,128]{1,0:T(8,128)(2,1)S(1)} %get-tuple-element.26), channel_id=1, source_target_pairs={{0,4},{1,29},{2,6},{3,31},{4,8},{5,1},{6,10},{7,3},{8,12},{9,5},{1... | collective-permute-start | bytes 798728 | tf_op jit(solution)/shard_map/ppermute | solution.py:245
  45.9 1.0 %shard_map.56.own = f32[1032,128]{1,0:T(8,128)S(1)} custom-call(f32[128,3072]{1,0:T(8,128)S(1)} %get-tuple-element.17.own, f32[2,1536]{1,0:T(2,128)S(1)} %get-tuple-element.23.norms, bf16[1536,1024]{1,0:T(8,128)(2,1)S(1)} %copy-done.1, bf16[1536,1024]{1,0:T(8,128)(2,1)S(1)} %collective-permute-done.source.others), custom_call_target="tpu_custom_call" | custom-call | flops 805306368 | bytes 1048576 | tf_op jit(solution)/shard_map/pallas_call | solution.py:178
  46.9 3.6 %collective-permute-done.5.up = bf16[1040,128]{1,0:T(8,128)(2,1)S(1)} collective-permute-done((bf16[1040,128]{1,0:T(8,128)(2,1)S(1)}, bf16[1040,128]{1,0:T(8,128)(2,1)S(1)}, u32[]{:S(2)}, u32[]{:S(2)}) %collective-permute-start.5) | collective-permute-done | bytes 266272 | tf_op jit(solution)/shard_map/ppermute | solution.py:245
  50.5 0.9 %shard_map.57 = bf16[16,80,128]{2,1,0:T(8,128)(2,1)} custom-call(f32[1032,128]{1,0:T(8,128)S(1)} %shard_map.56.own, bf16[1040,128]{1,0:T(8,128)(2,1)S(1)} %collective-permute-done.5.up, bf16[1040,128]{1,0:T(8,128)(2,1)S(1)} %collective-permute-done.6.down, bf16[1040,128]{1,0:T(8,128)(2,1)S(1)} %collective-permute-done.7.deep), custom_call_target="tpu_custom_call" | custom-call | bytes 1048576 | tf_op jit(solution)/shard_map/pallas_call | solution.py:178
  51.4 10.3 %all-to-all-start.1 = ((bf16[16,80,128]{2,1,0:T(8,128)(2,1)}), bf16[16,80,128]{2,1,0:T(8,128)(2,1)S(1)}, u32[]{:S(2)}, u32[]{:S(2)}) async-start(bf16[16,80,128]{2,1,0:T(8,128)(2,1)} %shard_map.57), calls=%async_computation.1 | async-start | bytes 655360 | tf_op jit(solution)/shard_map/all_to_all | solution.py:190
  61.7 0.6 dynamic_slice.6
  62.9 5.9 %all-to-all-done.1.packed = bf16[16,80,128]{2,1,0:T(8,128)(2,1)S(1)} async-done(((bf16[16,80,128]{2,1,0:T(8,128)(2,1)}), bf16[16,80,128]{2,1,0:T(8,128)(2,1)S(1)}, u32[]{:S(2)}, u32[]{:S(2)}) %all-to-all-start.1) | async-done | bytes 327712 | tf_op jit(solution)/shard_map/all_to_all | solution.py:190
  68.8 0.1 shard_map.58.mine
  68.9 0.0 collective-permute-start.8
  69.0 2.8 %collective-permute-done.8.across = f32[9,8,128]{2,1,0:T(8,128)S(1)} collective-permute-done((f32[9,8,128]{2,1,0:T(8,128)S(1)}, f32[9,8,128]{2,1,0:T(8,128)S(1)}, u32[]{:S(2)}, u32[]{:S(2)}) %collective-permute-start.8) | collective-permute-done | bytes 36896 | tf_op jit(solution)/shard_map/ppermute | solution.py:252
  71.8 3.9 %collective-permute-start.9 = (f32[8,1024]{1,0:T(8,128)S(1)}, f32[8,1024]{1,0:T(8,128)S(1)}, u32[]{:S(2)}, u32[]{:S(2)}) collective-permute-start(f32[8,1024]{1,0:T(8,128)S(1)} %shard_map.59.mine), channel_id=1, source_target_pairs={{0,1},{1,0},{2,3},{3,2},{4,5},{5,4},{6,7},{7,6},{8,9},{9,8},{10,11... | collective-permute-start | bytes 98312 | tf_op jit(solution)/shard_map/ppermute | solution.py:260
  75.7 0.6 reduce
  76.3 0.2 collective-permute-done.9.other
  76.6 0.6 shard_map.60
  (14 shorter events, 0.1 us)
Async XLA Ops:
  22.7 7.8 %collective-permute-start = (bf16[1536,1024]{1,0:T(8,128)(2,1)}, bf16[1536,1024]{1,0:T(8,128)(2,1)S(1)}, u32[]{:S(2)}, u32[]{:S(2)}) collective-permute-start(bf16[1536,1024]{1,0:T(8,128)(2,1)} %docs.3), channel_id=1, source_target_pairs={{0,1},{1,0},{2,3},{3,2},{4,5},{5,4},{6,7},{7,6},{8,9},{9,8},{10,11... | collective-permute-start | bytes 9437192 | tf_op jit(solution)/shard_map/ppermute | solution.py:202
  24.3 8.2 %collective-permute-start.1 = (bf16[128,1024]{1,0:T(8,128)(2,1)S(1)}, bf16[128,1024]{1,0:T(8,128)(2,1)S(1)}, u32[]{:S(2)}, u32[]{:S(2)}) collective-permute-start(bf16[128,1024]{1,0:T(8,128)(2,1)S(1)} %bitcast.4), channel_id=1, source_target_pairs={{0,28},{1,5},{2,30},{3,7},{4,0},{5,9},{6,2},{7,11},{8,4},{9,13},{1... | collective-permute-start | bytes 786440 | tf_op jit(solution)/shard_map/ppermute | solution.py:203
  25.1 8.5 %collective-permute-start.3 = (bf16[128,1024]{1,0:T(8,128)(2,1)S(1)}, bf16[128,1024]{1,0:T(8,128)(2,1)S(1)}, u32[]{:S(2)}, u32[]{:S(2)}) collective-permute-start(bf16[128,1024]{1,0:T(8,128)(2,1)S(1)} %bitcast.5), channel_id=1, source_target_pairs={{0,64},{1,65},{2,66},{3,67},{4,68},{5,69},{6,70},{7,71},{8,72},{9,... | collective-permute-start | bytes 786440 | tf_op jit(solution)/shard_map/ppermute | solution.py:203
  26.0 7.6 %collective-permute-start.2 = (bf16[128,1024]{1,0:T(8,128)(2,1)S(1)}, bf16[128,1024]{1,0:T(8,128)(2,1)S(1)}, u32[]{:S(2)}, u32[]{:S(2)}) collective-permute-start(bf16[128,1024]{1,0:T(8,128)(2,1)S(1)} %bitcast.6), channel_id=1, source_target_pairs={{0,192},{1,193},{2,194},{3,195},{4,196},{5,197},{6,198},{7,199},{8... | collective-permute-start | bytes 786440 | tf_op jit(solution)/shard_map/ppermute | solution.py:203
  27.7 1.9 %copy-start = (bf16[1536,1024]{1,0:T(8,128)(2,1)S(1)}, bf16[1536,1024]{1,0:T(8,128)(2,1)}, u32[]{:S(2)}) copy-start(bf16[1536,1024]{1,0:T(8,128)(2,1)} %docs.3) | copy-start | bytes 9437188
  33.6 5.3 %copy-start.1 = (bf16[1536,1024]{1,0:T(8,128)(2,1)S(1)}, bf16[1536,1024]{1,0:T(8,128)(2,1)}, u32[]{:S(2)}) copy-start(bf16[1536,1024]{1,0:T(8,128)(2,1)} %docs.3) | copy-start | bytes 9437188
  35.6 3.3 %collective-permute-start.4 = (f32[4,1536]{1,0:T(4,128)S(1)}, f32[4,1536]{1,0:T(4,128)S(1)}, u32[]{:S(2)}, u32[]{:S(2)}) collective-permute-start(f32[4,1536]{1,0:T(4,128)S(1)} %get-tuple-element.22.mine), channel_id=1, source_target_pairs={{0,1},{1,0},{2,3},{3,2},{4,5},{5,4},{6,7},{7,6},{8,9},{9,8},{10,11... | collective-permute-start | bytes 73736 | tf_op jit(solution)/shard_map/ppermute | solution.py:225
  41.6 8.9 %collective-permute-start.5 = (bf16[1040,128]{1,0:T(8,128)(2,1)S(1)}, bf16[1040,128]{1,0:T(8,128)(2,1)S(1)}, u32[]{:S(2)}, u32[]{:S(2)}) collective-permute-start(bf16[1040,128]{1,0:T(8,128)(2,1)S(1)} %get-tuple-element.24), channel_id=1, source_target_pairs={{0,64},{1,65},{2,66},{3,67},{4,68},{5,69},{6,70},{7,71},{8,72},{9,... | collective-permute-start | bytes 798728 | tf_op jit(solution)/shard_map/ppermute | solution.py:245
  41.7 8.8 %collective-permute-start.6 = (bf16[1040,128]{1,0:T(8,128)(2,1)S(1)}, bf16[1040,128]{1,0:T(8,128)(2,1)S(1)}, u32[]{:S(2)}, u32[]{:S(2)}) collective-permute-start(bf16[1040,128]{1,0:T(8,128)(2,1)S(1)} %get-tuple-element.25), channel_id=1, source_target_pairs={{0,192},{1,193},{2,194},{3,195},{4,196},{5,197},{6,198},{7,199},{8... | collective-permute-start | bytes 798728 | tf_op jit(solution)/shard_map/ppermute | solution.py:245
  44.3 6.2 %collective-permute-start.7 = (bf16[1040,128]{1,0:T(8,128)(2,1)S(1)}, bf16[1040,128]{1,0:T(8,128)(2,1)S(1)}, u32[]{:S(2)}, u32[]{:S(2)}) collective-permute-start(bf16[1040,128]{1,0:T(8,128)(2,1)S(1)} %get-tuple-element.26), channel_id=1, source_target_pairs={{0,4},{1,29},{2,6},{3,31},{4,8},{5,1},{6,10},{7,3},{8,12},{9,5},{1... | collective-permute-start | bytes 798728 | tf_op jit(solution)/shard_map/ppermute | solution.py:245
  45.9 15.8 %copy-start.3 = (s32[4]{0:T(128)S(1)}, s32[4]{0:T(128)}, u32[]{:S(2)}) copy-start(s32[4]{0:T(128)} %constant.72.clone) | copy-start | bytes 52
  45.9 25.9 %copy-start.2 = (bf16[16,1024]{1,0:T(8,128)(2,1)S(1)}, bf16[16,1024]{1,0:T(8,128)(2,1)}, u32[]{:S(2)}) copy-start(bf16[16,1024]{1,0:T(8,128)(2,1)} %centroids.1) | copy-start | bytes 98308
  51.4 17.4 %all-to-all-start.1 = ((bf16[16,80,128]{2,1,0:T(8,128)(2,1)}), bf16[16,80,128]{2,1,0:T(8,128)(2,1)S(1)}, u32[]{:S(2)}, u32[]{:S(2)}) async-start(bf16[16,80,128]{2,1,0:T(8,128)(2,1)} %shard_map.57), calls=%async_computation.1 | async-start | bytes 655360 | tf_op jit(solution)/shard_map/all_to_all | solution.py:190
  68.9 2.8 %collective-permute-start.8 = (f32[9,8,128]{2,1,0:T(8,128)S(1)}, f32[9,8,128]{2,1,0:T(8,128)S(1)}, u32[]{:S(2)}, u32[]{:S(2)}) collective-permute-start(f32[9,8,128]{2,1,0:T(8,128)S(1)} %shard_map.58.mine), channel_id=1, source_target_pairs={{0,2},{1,3},{2,0},{3,1},{4,6},{5,7},{6,4},{7,5},{8,10},{9,11},{10,... | collective-permute-start | bytes 110600 | tf_op jit(solution)/shard_map/ppermute | solution.py:252
  71.8 4.8 %collective-permute-start.9 = (f32[8,1024]{1,0:T(8,128)S(1)}, f32[8,1024]{1,0:T(8,128)S(1)}, u32[]{:S(2)}, u32[]{:S(2)}) collective-permute-start(f32[8,1024]{1,0:T(8,128)S(1)} %shard_map.59.mine), channel_id=1, source_target_pairs={{0,1},{1,0},{2,3},{3,2},{4,5},{5,4},{6,7},{7,6},{8,9},{9,8},{10,11... | collective-permute-start | bytes 98312 | tf_op jit(solution)/shard_map/ppermute | solution.py:260
